TPU v7x, 128 devices: a whole 4x4x4 slice. The times are simulated.
128 devices in a mesh: seq: 32 (over y, x, core), ch: 4 (over z).
Axes of the slice: x: 4, y: 4, z: 4, core: 2. Of those that a mesh axis runs over, the one named last changes fastest.
Arguments:
- token_ids: int32 [8192], P('seq'), may hold values from 65 to 84, as said below
- embedding: bfloat16 [512, 8192], P(None, 'ch'), may hold values from -1200 to 1200
- norm_gain: float32 [8192], P('ch'), may hold values from 0.5 to 1.5
- conv_weight: float32 [3, 7, 8192], P(None, None, 'ch'), may hold values from -2 to 2
- pole_rates: float32 [16, 8192], P(None, 'ch'), may hold values from 0.001 to 0.105
- residues: float32 [16, 8192], P(None, 'ch'), may hold values from -70 to 70
- skip_gain: float32 [8192], P('ch'), may hold values from -1.5 to 1.5
- cotangent: bfloat16 [8192, 8192], P('seq', 'ch'), may hold values from -6 to 6
Outputs:
- hyena_out: bfloat16 [8192, 8192], P('seq', 'ch')
- grad_normed: bfloat16 [8192, 8192], P('seq', 'ch')
- grad_conv: float32 [3, 7, 8192], P(None, None, 'ch')
- grad_residues: float32 [16, 8192], P(None, 'ch')
- grad_skip: float32 [8192], P('ch')
Inputs may be any that keep to these rules, and one draw needn't show every extreme that they name: `token_ids`: every token is the byte code of A, C, G or T.
All inputs are finite; a program needn't handle non-finite values.
Results may differ from a plain program's by a relative error of at most 0.03.
Values may be sent and summed in bfloat16 or wider, within the bound.
No kernel may reach another device: no remote copies, remote signals or barrier semaphores. Data moves between devices by JAX's collectives and lax.ppermute only.
A program may use at most 128 MiB of HBM per device.

v0:
```python
import jax
import jax.numpy as jnp
from jax import lax
from jax.sharding import PartitionSpec as P

D = 8192
POLES = 16
TAPS = 7


def shifted(block, axis, distance):
    devices = range(lax.axis_size(axis))
    route = [(i - distance, i) for i in devices if i - distance in devices]
    return lax.ppermute(block, axis, route)


def embed_lookup(ids, embedding):
    vocab_ids = lax.broadcasted_iota(jnp.int32, (1, embedding.shape[0]), 1)
    one_hot = (ids[:, None] == vocab_ids).astype(jnp.bfloat16)
    return jnp.dot(one_hot, embedding, preferred_element_type=jnp.float32).astype(jnp.bfloat16)


def per_device(
    token_ids, embedding, norm_gain, conv_weight, pole_rates, residues, skip_gain, cotangent
):
    length = token_ids.shape[0]
    channels = embedding.shape[1]
    margin = TAPS - 1
    highest = lax.Precision.HIGHEST
    embedded = embed_lookup(token_ids, embedding)
    widened = embedded.astype(jnp.float32)
    sum_squares = lax.psum(jnp.sum(widened * widened, axis=1), "ch")
    scale_rows = lax.rsqrt(sum_squares / D + 1e-05)
    normed = (widened * scale_rows[:, None] * norm_gain[None, :]).astype(jnp.bfloat16)
    leading = shifted(normed[length - margin :], "seq", 1)
    padded = lax.optimization_barrier(jnp.concatenate([leading, normed], 0)).astype(jnp.float32)
    features = []
    for feature in range(3):
        summed = jnp.zeros((length, channels), jnp.float32)
        for offset in range(TAPS):
            summed = (
                summed
                + conv_weight[feature, offset][None, :]
                * padded[margin - offset : margin - offset + length]
            )
        features.append(summed)
    features = lax.optimization_barrier(jnp.stack(features).astype(jnp.bfloat16)).astype(
        jnp.float32
    )
    query_feat = features[0]
    key_feat = features[1]
    value_feat = features[2]
    mixed_kv = key_feat * value_feat
    grad_long = cotangent.astype(jnp.float32) * query_feat
    block_len = min(32, length)
    block_count = length // block_len
    steps_in = lax.broadcasted_iota(jnp.float32, (block_len, 1, 1), 0)
    rate_grid = pole_rates[None]
    growing = jnp.exp(rate_grid * steps_in)
    shrinking = jnp.exp(-rate_grid * steps_in)
    entering = jnp.exp(-rate_grid * (steps_in + 1.0))
    leaving = jnp.exp(-rate_grid * (block_len - steps_in))
    to_end = jnp.exp(-rate_grid * (block_len - 1.0 - steps_in))
    row_index = lax.broadcasted_iota(jnp.int32, (block_len, block_len), 0)
    col_index = lax.broadcasted_iota(jnp.int32, (block_len, block_len), 1)
    lower_ones = (row_index >= col_index).astype(jnp.float32)
    upper_ones = (row_index <= col_index).astype(jnp.float32)
    mixed_blocks = mixed_kv.reshape(block_count, block_len, channels)
    grad_blocks = grad_long.reshape(block_count, block_len, channels)
    block_ends = jnp.einsum("bjc,jnc->bnc", mixed_blocks, to_end, precision=highest)
    block_starts = jnp.einsum("bjc,jnc->bnc", grad_blocks, shrinking, precision=highest)
    block_pos = lax.broadcasted_iota(jnp.float32, (block_count, 1, 1), 0)
    end_state = jnp.sum(
        jnp.exp(-rate_grid * block_len * (block_count - 1.0 - block_pos)) * block_ends, 0
    )
    start_adjoint = jnp.sum(jnp.exp(-rate_grid * block_len * block_pos) * block_starts, 0)
    zeros_state = jnp.zeros_like(pole_rates)
    position = lax.axis_index("seq")
    ends_piece = lax.all_gather(end_state[None], "seq", axis=0, tiled=True)
    starts_piece = lax.all_gather(start_adjoint[None], "seq", axis=0, tiled=True)
    shard_ids = lax.broadcasted_iota(jnp.int32, (ends_piece.shape[0], 1, 1), 0)
    gap_before = position - 1 - shard_ids
    gap_after = shard_ids - position - 1
    weight_before = jnp.where(
        gap_before >= 0,
        jnp.exp(-rate_grid * length * jnp.maximum(gap_before, 0).astype(jnp.float32)),
        0.0,
    )
    weight_after = jnp.where(
        gap_after >= 0,
        jnp.exp(-rate_grid * length * jnp.maximum(gap_after, 0).astype(jnp.float32)),
        0.0,
    )
    state_in = jnp.sum(weight_before * ends_piece, 0)
    adjoint_in = jnp.sum(weight_after * starts_piece, 0)

    def forward_step(carried, inputs):
        state_now, residue_acc = carried
        mixed_block, grad_block = inputs
        scaled = (growing * mixed_block[:, None, :]).reshape(block_len, -1)
        running = jnp.dot(lower_ones, scaled, precision=highest).reshape(block_len, POLES, channels)
        states = shrinking * running + entering * state_now[None]
        long_block = jnp.sum(states * residues[None], 1) + skip_gain[None, :] * mixed_block
        return (
            (states[block_len - 1], residue_acc + jnp.sum(states * grad_block[:, None, :], 0)),
            long_block,
        )

    (spent_state, residue_terms), long_blocks = lax.scan(
        forward_step, (state_in, zeros_state), (mixed_blocks, grad_blocks)
    )

    def backward_step(after, grad_block):
        scaled = (shrinking * grad_block[:, None, :]).reshape(block_len, -1)
        running = jnp.dot(upper_ones, scaled, precision=highest).reshape(block_len, POLES, channels)
        adjoints = growing * running + leaving * after[None]
        return (
            adjoints[0],
            skip_gain[None, :] * grad_block + jnp.sum(adjoints * residues[None], 1),
        )

    spent_adjoint, mixed_grads = lax.scan(backward_step, adjoint_in, grad_blocks, reverse=True)
    long_conv = long_blocks.reshape(length, channels)
    grad_mixed = mixed_grads.reshape(length, channels)
    hyena_out = (query_feat * long_conv).astype(jnp.bfloat16)
    skip_terms = jnp.sum(grad_long * mixed_kv, 0)
    feature_grads = jnp.stack(
        [cotangent.astype(jnp.float32) * long_conv, grad_mixed * value_feat, grad_mixed * key_feat]
    ).astype(jnp.bfloat16)
    following = shifted(feature_grads[:, :margin], "seq", -1)
    grads_f32 = lax.optimization_barrier(feature_grads).astype(jnp.float32)
    conv_terms = jnp.stack(
        [
            jnp.stack(
                [
                    jnp.sum(
                        grads_f32[feature] * padded[margin - offset : margin - offset + length], 0
                    )
                    for offset in range(TAPS)
                ]
            )
            for feature in range(3)
        ]
    )
    trailing = jnp.concatenate([grads_f32, following.astype(jnp.float32)], 1)
    grad_input = jnp.zeros((length, channels), jnp.float32)
    for feature in range(3):
        for offset in range(TAPS):
            grad_input = (
                grad_input
                + conv_weight[feature, offset][None, :]
                * trailing[feature, offset : offset + length]
            )
    conv_total, residue_total, skip_total = (
        lax.psum(conv_terms.astype(jnp.bfloat16), "seq").astype(jnp.float32),
        lax.psum(residue_terms.astype(jnp.bfloat16), "seq").astype(jnp.float32),
        lax.psum(skip_terms.astype(jnp.bfloat16), "seq").astype(jnp.float32),
    )
    return (hyena_out, grad_input.astype(jnp.bfloat16), conv_total, residue_total, skip_total)


def solution(mesh):
    in_specs = (
        P("seq"),
        P(None, "ch"),
        P("ch"),
        P(None, None, "ch"),
        P(None, "ch"),
        P(None, "ch"),
        P("ch"),
        P("seq", "ch"),
    )
    out_specs = (P("seq", "ch"), P("seq", "ch"), P(None, None, "ch"), P(None, "ch"), P("ch"))
    return jax.shard_map(
        per_device, mesh=mesh, in_specs=in_specs, out_specs=out_specs, check_vma=False
    )
```

profile of v0, /device:TPU:7, one launch (start us, length us, event | category | flops | bytes accessed | tf_op | source)
XLA Modules:
  0.0 766.4 jit_solution(4196218169158239120)
XLA Ops:
  10.3 9.9 %psum.28 = f32[256]{0:T(256)S(1)} all-reduce(f32[256]{0:T(256)S(1)} %get-tuple-element.553), channel_id=1, replica_groups=mesh['seq'=32,'ch'=4] {'ch'}, use_global_device_ids=true, to_apply=%region_1.0 | all-reduce | flops 256 | bytes 2048 | tf_op jit(solution)/shard_map/psum | solution.py:32
  20.5 5.7 collective-permute-start
  39.9 6.4 copy.32
  46.3 39.7 %fusion.34 = f32[16,2048]{0,1:T(8,128)} fusion(f32[16,2048]{0,1:T(8,128)S(1)} %copy.28, f32[8,32,2048]{1,0,2:T(8,128)} %copy.32, f32[16,2048]{0,1:T(8,128)S(1)} %copy-done.10), kind=kOutput, calls=%fused_computation.64 | convolution fusion | flops 102465536 | bytes 2490368 | tf_op jit(solution)/shard_map/bjc,jnc->bnc/dot_general | solution.py:71
  88.3 6.3 copy.30
  94.6 48.9 %fusion.35 = f32[16,2048]{0,1:T(8,128)} fusion(f32[8]{0:T(128)S(1)} %iota_subtract_fusion.2, f32[16,2048]{0,1:T(8,128)S(1)} %copy.28, f32[8,32,2048]{1,0,2:T(8,128)} %copy.30, f32[32]{0:T(128)S(1)} %iota_subtract_fusion.1, f32[16,2048]{0,1:T(8,128)S(1)} %copy-done.10), kind=kOutput, calls=%fused_computation.66 | convolution fusion | flops 102465536 | bytes 2490528 | tf_op jit(solution)/shard_map/bjc,jnc->bnc/dot_general | solution.py:70
  145.8 52.7 %psum.31 = bf16[2048]{0:T(1024)(128)(2,1)S(1)} all-reduce(bf16[2048]{0:T(1024)(128)(2,1)S(1)} %get-tuple-element.500), channel_id=1, replica_groups=mesh['seq'=32,'ch'=4] {'seq'}, use_global_device_ids=true, to_apply=%region_37.38 | all-reduce | flops 2048 | bytes 8192 | tf_op jit(solution)/shard_map/psum | solution.py:157
  199.2 4.5 multiply_reduce_fusion.2
  205.3 315.6 %while.36 = (s32[]{:T(128)}, f32[16,2048]{1,0:T(8,128)S(1)}, f32[16,2048]{1,0:T(8,128)S(1)}, f32[8,32,2048]{2,1,0:T(8,128)}, f32[8,32,2048]{2,1,0:T(8,128)}, /*i...) while((s32[]{:T(128)}, f32[16,2048]{1,0:T(8,128)S(1)}, ...), condition=%wide.region_7.8_spmd.clone.clone.clone, body=%wide.region_4.7_spmd.clone.clone.clone.sunk | while | flops 417433600 | bytes 113647920 | solution.py:109
  218.1 5.7 multiply_reduce_fusion.28
  225.2 4.4 copy.54
  229.6 4.4 copy.55
  234.0 4.4 copy.56
  238.4 4.9 fusion.156
  257.5 5.7 multiply_reduce_fusion.28
  264.6 4.4 copy.54
  269.0 4.4 copy.55
  273.4 4.4 copy.56
  277.8 4.9 fusion.156
  296.9 5.7 multiply_reduce_fusion.28
  304.0 4.4 copy.54
  308.4 4.4 copy.55
  312.8 4.4 copy.56
  317.2 4.9 fusion.156
  336.3 5.7 multiply_reduce_fusion.28
  343.4 4.4 copy.54
  347.8 4.4 copy.55
  352.2 4.4 copy.56
  356.6 4.9 fusion.156
  375.7 5.7 multiply_reduce_fusion.28
  387.2 4.4 copy.55
  391.6 4.4 copy.56
  396.0 4.9 fusion.156
  415.0 5.7 multiply_reduce_fusion.28
  426.5 4.4 copy.55
  430.9 4.4 copy.56
  435.3 4.9 fusion.156
  454.4 5.7 multiply_reduce_fusion.28
  465.9 4.4 copy.55
  470.3 4.4 copy.56
  474.7 4.9 fusion.156
  493.8 5.7 multiply_reduce_fusion.28
  505.3 4.4 copy.55
  509.7 4.4 copy.56
  514.1 4.9 fusion.156
  526.6 110.8 %while.35 = (s32[]{:T(128)}, f32[16,2048]{1,0:T(8,128)S(1)}, f32[8,32,2048]{2,1,0:T(8,128)}, f32[8,32,2048]{2,1,0:T(8,128)}, f32[2048]{0:T(1024)S(1)}, /*index=5...) while((s32[]{:T(128)}, f32[16,2048]{1,0:T(8,128)S(1)}, ...), condition=%wide.region_12.13_spmd.clone.clone, body=%wide.region_10.12_spmd.clone.clone.sunk | while | flops 412157952 | bytes 40509704 | solution.py:122
  651.4 18.2 %fusion.50 = bf16[256,2048]{1,0:T(8,128)(2,1)} fusion(f32[3,6,2048]{2,1,0:T(8,128)S(1)} %convert_element_type.84, f32[3,256,2048]{2,1,0:T(8,128)} %copy-done.5, f32[2048]{0:T(1024)S(1)} %bitcast.437, f32[2048]{0:T(1024)S(1)} %bitcast.435, f32[2048]{0:T(1024)S(1)} %bitcast.399, f32[2048]{0:T(1024)S(1)} %bitcast.401, f32[2048]{0:T(1024)S(1)} %bitcast.403, ...), kind=kLoop, calls=%fused_computation.88 | loop fusion | flops 31457280 | bytes 13950976 | tf_op jit(solution)/shard_map/convert_element_type | solution.py:159
  669.6 87.0 %all-reduce.3.cloned.1.call-done = (bf16[3,7,2048]{2,1,0:T(8,128)(2,1)}, bf16[16,2048]{1,0:T(8,128)(2,1)}) async-done(((bf16[3,7,2048]{2,1,0:T(8,128)(2,1)}, bf16[16,2048]{1,0:T(8,128)(2,1)}), (bf16[3,7,2048]{2,1,0:T(8,128)(2,1)}, bf16[16,2048]{1,0:T(8,128)(2,1)})) %all-reduce.3.cloned.1.call-update) | async-done | bytes 151568 | tf_op jit(solution)/shard_map/psum | solution.py:155
  (357 shorter events, 297.4 us)
Async XLA Ops:
  7.2 13.0 %copy-start.55 = (f32[2048]{0:T(1024)S(1)}, f32[2048]{0:T(1024)}, u32[]{:S(2)}) copy-start(f32[2048]{0:T(1024)} %param.14) | copy-start | bytes 24580
  7.2 19.0 %copy-start.7 = (f32[16,2048]{1,0:T(8,128)S(1)}, f32[16,2048]{1,0:T(8,128)}, u32[]{:S(2)}) copy-start(f32[16,2048]{1,0:T(8,128)} %param.16) | copy-start | bytes 393220
  7.2 192.0 %all-gather.7.cloned.1.call-start = ((), (), s32[]{:S(2)}) async-start(), calls=%async_computation.1 | async-start | bytes 4325376 | tf_op jit(solution)/shard_map/all_gather | solution.py:80
  10.3 16.0 %copy-start.12 = (f32[3,7,2048]{2,1,0:T(8,128)S(1)}, f32[3,7,2048]{2,1,0:T(8,128)}, u32[]{:S(2)}) copy-start(f32[3,7,2048]{2,1,0:T(8,128)} %param.15) | copy-start | bytes 516100
  20.5 7.8 %collective-permute-start = (bf16[6,2048]{1,0:T(8,128)(2,1)S(1)}, bf16[6,2048]{1,0:T(8,128)(2,1)S(1)}, u32[]{:S(2)}, u32[]{:S(2)}) collective-permute-start(bf16[6,2048]{1,0:T(8,128)(2,1)S(1)} %slice.312), channel_id=1, source_target_pairs={{0,4},{4,8},{8,12},{12,16},{16,20},{20,24},{24,28},{28,32},{32,36}... | collective-permute-start | bytes 73736 | tf_op jit(solution)/shard_map/ppermute | solution.py:14
  26.5 4.2 copy-start.25
  26.5 6.0 copy-start.13
  26.5 6.0 copy-start.39
  26.6 6.0 copy-start.41
  26.6 6.0 copy-start.43
  26.6 6.0 copy-start.45
  26.6 6.0 copy-start.47
  26.6 6.0 copy-start.49
  39.9 6.4 copy-start.10
  88.2 110.9 %all-gather.5.cloned.1.call-start = ((), (), s32[]{:S(2)}) async-start(), calls=%async_computation | async-start | bytes 4325376 | tf_op jit(solution)/shard_map/all_gather | solution.py:79
  145.7 610.9 %all-reduce.3.cloned.1.call-start = ((), (), s32[]{:S(2)}) async-start(), calls=%async_computation.2 | async-start | bytes 327680 | tf_op jit(solution)/shard_map/psum | solution.py:155
  234.0 4.4 copy-start.4
  273.4 4.4 copy-start.4
  312.8 4.4 copy-start.4
  352.2 4.4 copy-start.4
  391.6 4.4 copy-start.4
  430.9 4.4 copy-start.4
  470.3 4.4 copy-start.4
  509.7 4.4 copy-start.4
  641.4 9.7 %collective-permute-start.1 = (bf16[3,6,2048]{2,1,0:T(8,128)(2,1)S(1)}, bf16[3,6,2048]{2,1,0:T(8,128)(2,1)S(1)}, u32[]{:S(2)}, u32[]{:S(2)}) collective-permute-start(bf16[3,6,2048]{2,1,0:T(8,128)(2,1)S(1)} %slice.324), channel_id=1, source_target_pairs={{4,0},{8,4},{12,8},{16,12},{20,16},{24,20},{28,24},{32,28},{36,32}... | collective-permute-start | bytes 221192 | tf_op jit(solution)/shard_map/ppermute | solution.py:14
  644.9 4.2 copy-start.5
  644.9 6.2 copy-start.14
  644.9 6.2 copy-start.16
  645.0 6.2 copy-start.18
  645.0 6.2 copy-start.20
  645.0 6.2 copy-start.22
  645.0 6.2 copy-start.24
  645.0 6.2 copy-start.26
  645.0 6.2 copy-start.28
  645.0 6.2 copy-start.30
  645.0 6.2 copy-start.32
  645.0 6.2 copy-start.34
  645.0 6.2 copy-start.36
  645.0 6.2 copy-start.38
  645.1 6.2 copy-start.40
  645.1 6.2 copy-start.42
  645.1 6.2 copy-start.44
  645.1 6.2 copy-start.46
  645.1 6.2 copy-start.48
  645.1 6.2 copy-start.50
  645.1 6.2 copy-start.52
  645.1 6.2 copy-start.54
  651.4 108.3 %copy-start.1 = (bf16[512,2048]{1,0:T(8,128)(2,1)S(1)}, bf16[512,2048]{1,0:T(8,128)(2,1)}, u32[]{:S(2)}) copy-start(bf16[512,2048]{1,0:T(8,128)(2,1)} %param.13) | copy-start | bytes 6291460
  (20 other events, 57.3 us)
Sparse Core Ops, SparseCore 0:
  88.4 44.6 all-gather.6
  145.8 44.6 all-gather.4
  651.2 105.2 all-reduce.2
where the time goes:
time: 775 us; the launch traced here: 766 us
  local copies, waits for them, and re-layouts  252 us (33%)
  other arithmetic  189 us (24%)
  matrix products  151 us (19%)
  waiting for transfers between devices  87.1 us (11%)
  blocking collectives  62.6 us (8%)
  between operations  15.2 us (2%)
    while x80, local copies, waits for them, and re-layouts  199 us
    psum x1, waiting for transfers between devices, per_device(): lax.psum(conv_terms.astype(jnp.bfloat16), 'seq').astype(jnp.float32)  87 us
    psum x1, blocking collectives, per_device(): lax.psum(skip_terms.astype(jnp.bfloat16), 'seq').astype(jnp.float32)  52.7 us
    dot_general x1, matrix products, per_device(): jnp.einsum('bjc,jnc->bnc', mixed_blocks, to_end, precision=highest)  48.9 us
    reduce_sum x8, other arithmetic, forward_step(): jnp.sum(states * residues[None], 1) + skip_gain[None, :] * mixed_block  45.8 us
    dot_general x1, matrix products, per_device(): jnp.einsum('bjc,jnc->bnc', grad_blocks, shrinking, precision=highest)  39.7 us
    reduce_sum x8, other arithmetic, forward_step(): jnp.sum(states * grad_block[:, None, :], 0)  39.2 us
    dot_general x8, matrix products, forward_step(): jnp.dot(lower_ones, scaled, precision=highest)  31.3 us
  transfers between devices with their start and end apart: 5, of which 1 were waited for; matrix products, arithmetic and copies ran while one was open for 11% of the time, Pallas kernels for 0%

commit v1 on v0

v1 whole, which is shorter than its diff:
```python
import jax
import jax.numpy as jnp
from jax import lax
from jax.experimental import pallas as pl
from jax.experimental.pallas import tpu as pltpu
from jax.sharding import PartitionSpec as P

D = 8192
POLES = 16
TAPS = 7
LETTERS = (65, 67, 71, 84)
SEGS = 8
LANES = 128
f32 = jnp.float32
bf16 = jnp.bfloat16


def shifted(block, axis, distance):
    devices = range(lax.axis_size(axis))
    route = [(i - distance, i) for i in devices if i - distance in devices]
    return lax.ppermute(block, axis, route)


def rows(ref, n):
    return jnp.broadcast_to(ref[n : n + 1, :], (SEGS, LANES))


def states_kernel(
    hot_ref, order_ref, embed_ref, scale_ref, gain_ref, weight_ref, rate_ref, cot_ref,
    feat_ref, cotp_ref, normed_ref, inner_ref, ends_ref, x_ref, g_ref,
):
    steps = x_ref.shape[0]
    length = steps * SEGS
    normed = (embed_ref[...] * scale_ref[...] * gain_ref[...]).astype(bf16).astype(f32)
    normed_ref[...] = normed
    cot = jnp.dot(order_ref[...], cot_ref[...], preferred_element_type=f32)
    cotp_ref[...] = cot.astype(bf16)
    feats = []
    for f in range(3):
        table = jnp.concatenate(
            [weight_ref[f, i : i + 1, :] * normed for i in range(TAPS)]
            + [jnp.zeros((SEGS, LANES), f32)],
            0,
        )
        high = table.astype(bf16)
        low = (table - high.astype(f32)).astype(bf16)
        summed = jnp.dot(
            hot_ref[...], jnp.concatenate([high, low], 0), preferred_element_type=f32
        ).astype(bf16)
        feat_ref[f] = summed
        feats.append(summed.astype(f32))
    x_ref[...] = (feats[1] * feats[2]).reshape(steps, SEGS, LANES)
    g_ref[...] = (cot * feats[0]).reshape(steps, SEGS, LANES)
    seg = lax.broadcasted_iota(jnp.int32, (SEGS, LANES), 0)
    for part in range(2):
        base = part * 8
        rates = [rows(rate_ref, base + n) for n in range(8)]
        decay = [jnp.exp(-p) for p in rates]
        for way in range(2):
            src = g_ref if way else x_ref
            state = [jnp.zeros((SEGS, LANES), f32)] * 8
            for i in range(steps):
                now = src[steps - 1 - i if way else i]
                state = [d * s + now for d, s in zip(decay, state)]
            for n in range(8):
                inc = state[n]
                for hop in (1, 2, 4):
                    factor = jnp.exp(rates[n] * (-float(steps * hop)))
                    if way:
                        factor = jnp.where(seg < SEGS - hop, factor, 0.0)
                        inc = inc + factor * pltpu.roll(inc, SEGS - hop, 0)
                    else:
                        factor = jnp.where(seg >= hop, factor, 0.0)
                        inc = inc + factor * pltpu.roll(inc, hop, 0)
                if way:
                    ends_ref[part, 8 + n : 9 + n, :] = inc[0:1]
                    inner = jnp.where(seg < SEGS - 1, pltpu.roll(inc, SEGS - 1, 0), 0.0)
                else:
                    ends_ref[part, n : n + 1, :] = inc[SEGS - 1 :]
                    inner = jnp.where(seg >= 1, pltpu.roll(inc, 1, 0), 0.0)
                inner_ref[way, base + n] = inner


def carry_kernel(length, got_ref, rate_ref, out_ref):
    devices = got_ref.shape[0]
    decay = jnp.exp(rate_ref[...] * (-float(length)))
    state = jnp.zeros((8, LANES), f32)
    for j in range(devices):
        out_ref[j, 0:8, :] = state
        state = decay * state + got_ref[j, 0:8, :]
    state = jnp.zeros((8, LANES), f32)
    for j in reversed(range(devices)):
        out_ref[j, 8:16, :] = state
        state = decay * state + got_ref[j, 8:16, :]


def main_kernel(
    feat_ref, cotp_ref, inner_ref, enter_ref, rate_ref, residue_ref, skip_ref, hot_t_ref,
    order_t_ref, normed_ref,
    out_ref, grads_ref, first_ref, params_ref, x_ref, g_ref, y_ref, m_ref,
):
    steps = x_ref.shape[0]
    length = steps * SEGS
    key = feat_ref[1].astype(f32)
    value = feat_ref[2].astype(f32)
    mixed = key * value
    glong = cotp_ref[...].astype(f32) * feat_ref[0].astype(f32)
    x_ref[...] = mixed.reshape(steps, SEGS, LANES)
    g_ref[...] = glong.reshape(steps, SEGS, LANES)
    skip = jnp.broadcast_to(skip_ref[...], (SEGS, LANES))
    seg = lax.broadcasted_iota(jnp.int32, (SEGS, LANES), 0).astype(f32)
    total = jnp.zeros((SEGS, LANES), f32)
    residue_grads = []
    for part in range(2):
        base = part * 8
        rates = [rows(rate_ref, base + n) for n in range(8)]
        decay = [jnp.exp(-p) for p in rates]
        residue = [rows(residue_ref, base + n) for n in range(8)]
        for way in range(2):
            state = []
            for n in range(8):
                gap = (SEGS - 1.0 - seg) if way else seg
                spread = jnp.exp(rates[n] * (gap * (-float(steps))))
                entering = jnp.broadcast_to(
                    enter_ref[part, 8 * way + n : 8 * way + n + 1, :], (SEGS, LANES)
                )
                state.append(inner_ref[way, base + n] + spread * entering)
            acc = [jnp.zeros((SEGS, LANES), f32)] * 8
            for k in range(steps):
                i = steps - 1 - k if way else k
                src, dst = (g_ref, m_ref) if way else (x_ref, y_ref)
                now = src[i]
                state = [d * s + now for d, s in zip(decay, state)]
                terms = [r * s for r, s in zip(residue, state)]
                while len(terms) > 1:
                    terms = [a + b for a, b in zip(terms[::2], terms[1::2])]
                dst[i] = terms[0] + (dst[i] if part else skip * now)
                if not way:
                    other = g_ref[i]
                    acc = [a + other * s for a, s in zip(acc, state)]
                    if not part:
                        total = total + other * now
            if not way:
                residue_grads += [jnp.sum(a, 0, keepdims=True) for a in acc]
    long_conv = y_ref[...].reshape(length, LANES)
    grad_mixed = m_ref[...].reshape(length, LANES)
    hyena = (feat_ref[0].astype(f32) * long_conv).astype(bf16)
    out_ref[...] = jnp.dot(order_t_ref[...], hyena, preferred_element_type=f32).astype(bf16)
    grads = [
        (cotp_ref[...].astype(f32) * long_conv).astype(bf16),
        (grad_mixed * feat_ref[2].astype(f32)).astype(bf16),
        (grad_mixed * feat_ref[1].astype(f32)).astype(bf16),
    ]
    pieces = residue_grads
    normed = normed_ref[...]
    for f in range(3):
        grads_ref[f] = grads[f]
        wide = grads[f].astype(f32)
        first_ref[f] = jnp.concatenate(
            [wide[8 * i : 8 * i + 1] for i in range(TAPS - 1)] + [jnp.zeros((2, LANES), f32)], 0
        )
        by_token = jnp.dot(hot_t_ref[...], grads[f], preferred_element_type=f32)
        for i in range(TAPS + 1):
            pieces.append(
                jnp.sum(by_token[8 * i : 8 * i + 8] * normed, 0, keepdims=True)
            )
    pieces.append(jnp.sum(total, 0, keepdims=True))
    pieces.append(jnp.zeros((64 - len(pieces), LANES), f32))
    params_ref[...] = jnp.concatenate(pieces, 0).astype(bf16).reshape(2, 32, LANES)


def sum_kernel(got_ref, out_ref):
    total = got_ref[0].astype(f32)
    for j in range(1, got_ref.shape[0]):
        total = total + got_ref[j].astype(f32)
    total = total.astype(bf16)
    for j in range(got_ref.shape[0]):
        out_ref[j] = total


def spread_kernel(got_ref, conv_ref, residue_ref, skip_ref):
    whole = got_ref[...].reshape(64, LANES).astype(f32)
    residue_ref[...] = whole[0:POLES]
    for f in range(3):
        conv_ref[f] = whole[POLES + 8 * f : POLES + 8 * f + TAPS]
    skip_ref[...] = whole[POLES + 24 : POLES + 25]


def input_kernel(grads_ref, after_ref, weight_ref, order_t_ref, out_ref, wide_ref):
    steps = grads_ref.shape[1] // SEGS
    seg = lax.broadcasted_iota(jnp.int32, (SEGS, LANES), 0)
    for f in range(3):
        wide_ref[f, 0:steps] = grads_ref[f].astype(f32).reshape(steps, SEGS, LANES)
        for i in range(TAPS - 1):
            ahead = pltpu.roll(wide_ref[f, i], SEGS - 1, 0)
            last = jnp.broadcast_to(after_ref[f, i : i + 1, :], (SEGS, LANES))
            wide_ref[f, steps + i] = jnp.where(seg < SEGS - 1, ahead, last)
    summed = jnp.zeros((steps, SEGS, LANES), f32)
    for f in range(3):
        for i in range(TAPS):
            summed = summed + weight_ref[f, i : i + 1, :][None] * wide_ref[f, i : i + steps]
    natural = jnp.dot(
        order_t_ref[...], summed.reshape(steps * SEGS, LANES).astype(bf16),
        preferred_element_type=f32,
    )
    out_ref[...] = natural.astype(bf16)


def whole(*shape):
    return pl.BlockSpec(shape, lambda b: (0,) * len(shape))


def lanes(*shape):
    return pl.BlockSpec(shape + (LANES,), lambda b: (0,) * len(shape) + (b,))


def firsts(*shape):
    return pl.BlockSpec(shape, lambda b: (b,) + (0,) * (len(shape) - 1))


def struct(shape, dtype):
    return jax.ShapeDtypeStruct(shape, dtype)


def params_of():
    return pltpu.CompilerParams(vmem_limit_bytes=48 * 1024 * 1024)


def exchange(block):
    return lax.all_to_all(block, "seq", 0, 0, tiled=True)


def per_device(
    token_ids, embedding, norm_gain, conv_weight, pole_rates, residues, skip_gain, cotangent
):
    length = token_ids.shape[0]
    channels = embedding.shape[1]
    margin = TAPS - 1
    steps = length // SEGS
    blocks = channels // LANES
    devices = lax.axis_size("seq")

    embed = jnp.concatenate(
        [embedding[v : v + 1] for v in LETTERS] + [jnp.zeros((4, channels), bf16)], 0
    ).astype(f32)
    sum_squares = lax.psum(jnp.sum(embed * embed, axis=1), "ch")
    scale = jnp.broadcast_to(lax.rsqrt(sum_squares / D + 1e-05)[:, None], (8, LANES))

    leading = shifted(token_ids[length - margin :], "seq", 1)
    padded = jnp.concatenate([leading, token_ids])
    taps = jnp.stack(
        [
            padded[margin - i : margin - i + length].reshape(SEGS, steps).T.reshape(length)
            for i in range(TAPS)
        ]
        + [jnp.zeros((length,), jnp.int32)]
    )
    letters = jnp.array(LETTERS + (-1, -1, -1, -1), jnp.int32)
    hot_t = (taps[:, None, :] == letters[None, :, None]).astype(bf16).reshape(64, length)
    hot = jnp.concatenate([hot_t, hot_t], 0).T
    place = jnp.arange(length, dtype=jnp.int32)
    source = (place % SEGS) * steps + place // SEGS
    order = (source[:, None] == place[None, :]).astype(bf16)
    order_t = (source[None, :] == place[:, None]).astype(bf16)

    feats, cotp, normed, inner, ends = pl.pallas_call(
        states_kernel,
        grid=(blocks,),
        in_specs=[
            whole(length, 128), whole(length, length), lanes(8), whole(8, LANES), lanes(1),
            lanes(3, TAPS), lanes(POLES), lanes(length),
        ],
        out_specs=[
            lanes(3, length), lanes(length), lanes(8), lanes(2, POLES, SEGS),
            firsts(2, 16, LANES),
        ],
        out_shape=[
            struct((3, length, channels), bf16), struct((length, channels), bf16),
            struct((8, channels), f32), struct((2, POLES, SEGS, channels), f32),
            struct((2 * blocks, 16, LANES), f32),
        ],
        scratch_shapes=[pltpu.VMEM((steps, SEGS, LANES), f32)] * 2,
        compiler_params=params_of(),
        name="states",
    )(hot, order, embed, scale, norm_gain[None], conv_weight, pole_rates, cotangent)

    position = lax.axis_index("seq")
    own_rates = lax.dynamic_slice(
        pole_rates, ((position % 2) * 8, (position // 2) * LANES), (8, LANES)
    )
    carried = pl.pallas_call(
        lambda *refs: carry_kernel(length, *refs),
        out_shape=struct((devices, 16, LANES), f32),
        name="carry",
    )(exchange(ends), own_rates)
    entering = exchange(carried)

    hyena, grads, first, params = pl.pallas_call(
        main_kernel,
        grid=(blocks,),
        in_specs=[
            lanes(3, length), lanes(length), lanes(2, POLES, SEGS), firsts(2, 16, LANES),
            lanes(POLES), lanes(POLES), lanes(1), whole(64, length), whole(length, length),
            lanes(8),
        ],
        out_specs=[
            lanes(length), lanes(3, length), lanes(3, 8), firsts(2, 32, LANES),
        ],
        out_shape=[
            struct((length, channels), bf16), struct((3, length, channels), bf16),
            struct((3, 8, channels), f32), struct((2 * blocks, 32, LANES), bf16),
        ],
        scratch_shapes=[pltpu.VMEM((steps, SEGS, LANES), f32)] * 4,
        compiler_params=params_of(),
        name="main",
    )(feats, cotp, inner, entering, pole_rates, residues, skip_gain[None], hot_t, order_t, normed)

    after = shifted(first.astype(bf16), "seq", -1).astype(f32)
    grad_input = pl.pallas_call(
        input_kernel,
        grid=(blocks,),
        in_specs=[lanes(3, length), lanes(3, 8), lanes(3, TAPS), whole(length, length)],
        out_specs=lanes(length),
        out_shape=struct((length, channels), bf16),
        scratch_shapes=[pltpu.VMEM((3, steps + 8, SEGS, LANES), f32)],
        compiler_params=params_of(),
        name="input_grad",
    )(grads, after, conv_weight, order_t)

    summed = pl.pallas_call(
        sum_kernel,
        out_shape=struct((devices, 32, LANES), bf16),
        name="sum",
    )(exchange(params))
    conv_total, residue_total, skip_total = pl.pallas_call(
        spread_kernel,
        grid=(blocks,),
        in_specs=[firsts(2, 32, LANES)],
        out_specs=[lanes(3, TAPS), lanes(POLES), lanes(1)],
        out_shape=[
            struct((3, TAPS, channels), f32), struct((POLES, channels), f32),
            struct((1, channels), f32),
        ],
        name="spread",
    )(exchange(summed))
    return hyena, grad_input, conv_total, residue_total, skip_total[0]


def solution(mesh):
    in_specs = (
        P("seq"),
        P(None, "ch"),
        P("ch"),
        P(None, None, "ch"),
        P(None, "ch"),
        P(None, "ch"),
        P("ch"),
        P("seq", "ch"),
    )
    out_specs = (P("seq", "ch"), P("seq", "ch"), P(None, None, "ch"), P(None, "ch"), P("ch"))
    return jax.shard_map(
        per_device, mesh=mesh, in_specs=in_specs, out_specs=out_specs, check_vma=False
    )
```

time: 775 us -> 141 us (0.18)
  local copies, waits for them, and re-layouts: 252 us -> 19 us
  other arithmetic: 189 us -> 2.68 us
  matrix products: 151 us -> 0 us
  waiting for transfers between devices: 87.1 us -> 12.6 us
  Pallas kernels: 0 us -> 49.7 us
  blocking collectives: 62.6 us -> 35.2 us
  between operations: 15.2 us -> 0.85 us
  starting transfers between devices: 7.74 us -> 19.4 us
    while x80 -> x0, local copies, waits for them, and re-layouts: 199 us -> none
    dot_general x19 -> x0, matrix products: 151 us -> none  [the longest x1 48.9 us: per_device(): jnp.einsum('bjc,jnc->bnc', mixed_blocks, to_end, precision=highest)]
    reduce_sum x27 -> x1, other arithmetic: 113 us -> 0.13 us  [per_device(): sum_squares = lax.psum(jnp.sum(embed * embed, axis=1), 'ch')]
    psum x1 -> x0, waiting for transfers between devices: 87 us -> none  [per_device(): lax.psum(conv_terms.astype(jnp.bfloat16), 'seq').astype(jnp.float32)]
    psum x2 -> x1, blocking collectives: 62.6 us -> 9.75 us  [per_device(): sum_squares = lax.psum(jnp.sum(embed * embed, axis=1), 'ch')]
    pallas_call x0 -> x6, Pallas kernels: none -> 49.7 us  [the longest x1 18.8 us: per_device(): pl.pallas_call(main_kernel, grid=(blocks,), in_specs=[lanes(3, length), l...]
    dynamic_update_slice x16 -> x0, other arithmetic: 27.2 us -> none  [per_device(): lax.scan(forward_step, (state_in, zeros_state), (mixed_blocks, grad_blocks))]
    mul x26 -> x0, local copies, waits for them, and re-layouts: 26.9 us -> none  [the longest x16 12.5 us: forward_step(): states * grad_block[:, None, :]]
  transfers between devices with their start and end apart: 5 -> 4, of which waited for: 1 -> 2; matrix products, arithmetic and copies ran while one was open for 11% -> 4% of each run, Pallas kernels for 0% -> 6%
where the time goes in v1:
time: 141 us; the launch traced here: 139 us
  Pallas kernels  49.7 us (35%)
  blocking collectives  35.2 us (25%)
  starting transfers between devices  19.4 us (14%)
  local copies, waits for them, and re-layouts  19 us (13%)
  waiting for transfers between devices  12.6 us (9%)
  other arithmetic  2.68 us (2%)
    all_to_all x2, blocking collectives, exchange(): return lax.all_to_all(block, 'seq', 0, 0, tiled=True)  25.4 us
    pallas_call x1, Pallas kernels, per_device(): pl.pallas_call(main_kernel, grid=(blocks,), in_specs=[lanes(3, length), l...  18.8 us
    all_to_all x2, starting transfers between devices, exchange(): return lax.all_to_all(block, 'seq', 0, 0, tiled=True)  13.4 us
    unnamed x36, local copies, waits for them, and re-layouts  12.6 us
    pallas_call x1, Pallas kernels, per_device(): pl.pallas_call(states_kernel, grid=(blocks,), in_specs=[whole(length, 128...  10.7 us
    psum x1, blocking collectives, per_device(): sum_squares = lax.psum(jnp.sum(embed * embed, axis=1), 'ch')  9.75 us
    pallas_call x1, Pallas kernels, per_device(): pl.pallas_call(input_kernel, grid=(blocks,), in_specs=[lanes(3, length),...  8.84 us
    pallas_call x1, Pallas kernels, per_device(): pl.pallas_call(spread_kernel, grid=(blocks,), in_specs=[firsts(2, 32, LAN...  7.95 us
  transfers between devices with their start and end apart: 4, of which 2 were waited for; matrix products, arithmetic and copies ran while one was open for 4% of the time, Pallas kernels for 6%

profile of v1, /device:TPU:7, one launch (start us, length us, event | category | flops | bytes accessed | tf_op | source)
XLA Modules:
  0.0 139.4 jit_solution(14525128347021507443)
XLA Ops:
  0.6 0.8 slice.33
  1.4 3.7 %collective-permute-start = (s32[6]{0:T(128)S(1)}, s32[6]{0:T(128)S(1)}, u32[]{:S(2)}, u32[]{:S(2)}) collective-permute-start(s32[6]{0:T(128)S(1)} %slice.33), channel_id=1, source_target_pairs={{0,4},{4,8},{8,12},{12,16},{16,20},{20,24},{24,28},{28,32},{32,36}... | collective-permute-start | bytes 80 | tf_op jit(solution)/shard_map/ppermute | solution.py:21
  5.1 0.8 reshape.81
  5.9 0.9 fusion.7
  6.9 0.1 multiply_reduce_fusion
  7.0 0.6 convert_element_type.23.embed_ref
  7.6 0.7 eq.58
  8.3 0.1 eq.59
  8.5 0.1 stack_reshape.21
  8.5 9.8 %psum.7 = f32[8]{0:T(128)S(1)} all-reduce(f32[8]{0:T(128)S(1)} %multiply_reduce_fusion), channel_id=1, replica_groups=mesh['seq'=32,'ch'=4] {'ch'}, use_global_device_ids=true, to_apply=%region_1.0 | all-reduce | flops 8 | bytes 64 | tf_op jit(solution)/shard_map/psum | solution.py:246
  18.3 0.1 fusion.1
  18.4 0.8 pad_add_fusion
  19.8 0.1 stack_reshape.22
  20.0 0.1 stack_reshape.23
  20.1 0.1 stack_reshape.24
  20.3 0.1 stack_reshape.25
  20.5 0.1 stack_reshape.26
  20.7 0.1 stack_reshape.27
  20.9 0.7 copy.22.hot_ref
  21.7 1.2 copy-done.1
  22.9 0.9 copy-done.2
  23.9 0.9 copy-done.4
  24.8 0.8 copy-done.8
  25.6 0.8 copy-done.9
  26.4 0.7 copy-done.15
  27.1 10.7 %states.1 = (bf16[3,256,2048]{2,1,0:T(8,128)(2,1)}, bf16[256,2048]{1,0:T(8,128)(2,1)S(1)}, f32[8,2048]{1,0:T(8,128)S(1)}, f32[2,16,8,2048]{3,2,1,0:T(8,128)S(1)}, f32[32,16,128]{2,1,0:T(8,128)S(1)}) custom-call(bf16[256,128]{1,0:T(8,128)(2,1)S(1)} %copy-done.9, bf16[256,256]{1,0:T(8,128)(2,1)S(1)} %get-tuple-element.40.order_ref, f32[8,2048]{1,0:T(8,128)S(1)} %copy-done.8, ...), custom_call_target="tpu_custom_call" | custom-call | tf_op jit(solution)/shard_map/states/pallas_call | solution.py:266
  37.8 0.7 copy-done.10
  38.5 0.6 copy-done.13
  39.2 8.2 %all-to-all-start = ((f32[32,16,128]{2,1,0:T(8,128)}), f32[32,16,128]{2,1,0:T(8,128)}, u32[]{:S(2)}, u32[]{:S(2)}) async-start(f32[32,16,128]{2,1,0:T(8,128)} %copy-done.10), calls=%async_computation | async-start | bytes 524288 | tf_op jit(solution)/shard_map/all_to_all | solution.py:230
  47.4 0.6 dynamic_slice.3.refs_1_
  48.0 6.9 %all-to-all-done.refs_0_ = f32[32,16,128]{2,1,0:T(8,128)} async-done(((f32[32,16,128]{2,1,0:T(8,128)}), f32[32,16,128]{2,1,0:T(8,128)}, u32[]{:S(2)}, u32[]{:S(2)}) %all-to-all-start) | async-done | bytes 262176 | tf_op jit(solution)/shard_map/all_to_all | solution.py:230
  54.9 1.7 %carry.1 = f32[32,16,128]{2,1,0:T(8,128)} custom-call(f32[32,16,128]{2,1,0:T(8,128)} %all-to-all-done.refs_0_, f32[8,128]{1,0:T(8,128)} %dynamic_slice.3.refs_1_), custom_call_target="tpu_custom_call" | custom-call | tf_op jit(solution)/shard_map/carry/pallas_call | solution.py:291
  56.6 12.8 %all_to_all.20.enter_ref = f32[32,16,128]{2,1,0:T(8,128)S(1)} all-to-all(f32[32,16,128]{2,1,0:T(8,128)} %carry.1), channel_id=1, replica_groups=mesh['seq'=32,'ch'=4] {'seq'}, dimensions={0} | all-to-all | bytes 524288 | tf_op jit(solution)/shard_map/all_to_all | solution.py:230
  69.4 0.8 copy-done.7
  70.1 0.9 copy-done.12
  71.0 0.8 copy-done.14
  71.9 18.8 %main.1 = (bf16[256,2048]{1,0:T(8,128)(2,1)}, bf16[3,256,2048]{2,1,0:T(8,128)(2,1)}, f32[3,8,2048]{2,1,0:T(8,128)S(1)}, bf16[32,32,128]{2,1,0:T(8,128)(2,1)S(1)}) custom-call(bf16[3,256,2048]{2,1,0:T(8,128)(2,1)} %get-tuple-element.17.feat_ref, bf16[256,2048]{1,0:T(8,128)(2,1)S(1)} %get-tuple-element.18.cotp_ref, ...), custom_call_target="tpu_custom_call" | custom-call | tf_op jit(solution)/shard_map/main/pallas_call | solution.py:298
  90.6 0.7 copy-done.11
  91.3 12.7 %all_to_all.21.got_ref = bf16[32,32,128]{2,1,0:T(8,128)(2,1)} all-to-all(bf16[32,32,128]{2,1,0:T(8,128)(2,1)S(1)} %get-tuple-element.25), channel_id=1, replica_groups=mesh['seq'=32,'ch'=4] {'seq'}, dimensions={0} | all-to-all | bytes 524288 | tf_op jit(solution)/shard_map/all_to_all | solution.py:230
  104.0 1.7 %sum.1 = bf16[32,32,128]{2,1,0:T(8,128)(2,1)} custom-call(bf16[32,32,128]{2,1,0:T(8,128)(2,1)} %all_to_all.21.got_ref), custom_call_target="tpu_custom_call" | custom-call | tf_op jit(solution)/shard_map/sum/pallas_call | solution.py:330
  105.7 5.2 %all-to-all-start.3 = ((bf16[32,32,128]{2,1,0:T(8,128)(2,1)}), bf16[32,32,128]{2,1,0:T(8,128)(2,1)S(1)}, u32[]{:S(2)}, u32[]{:S(2)}) async-start(bf16[32,32,128]{2,1,0:T(8,128)(2,1)} %sum.1), calls=%async_computation.3 | async-start | bytes 524288 | tf_op jit(solution)/shard_map/all_to_all | solution.py:230
  111.0 0.9 convert_element_type.25
  111.9 2.3 %collective-permute-start.1 = (bf16[3,8,2048]{2,1,0:T(8,128)(2,1)S(1)}, bf16[3,8,2048]{2,1,0:T(8,128)(2,1)S(1)}, u32[]{:S(2)}, u32[]{:S(2)}) collective-permute-start(bf16[3,8,2048]{2,1,0:T(8,128)(2,1)S(1)} %convert_element_type.25), channel_id=1, source_target_pairs={{4,0},{8,4},{12,8},{16,12},{20,16},{24,20},{28,24},{32,28},{36,32}... | collective-permute-start | bytes 294920 | tf_op jit(solution)/shard_map/ppermute | solution.py:21
  114.2 5.8 %collective-permute-done.1 = bf16[3,8,2048]{2,1,0:T(8,128)(2,1)S(1)} collective-permute-done((bf16[3,8,2048]{2,1,0:T(8,128)(2,1)S(1)}, bf16[3,8,2048]{2,1,0:T(8,128)(2,1)S(1)}, u32[]{:S(2)}, u32[]{:S(2)}) %collective-permute-start.1) | collective-permute-done | bytes 98336 | tf_op jit(solution)/shard_map/ppermute | solution.py:21
  120.0 1.9 %copy-done = bf16[3,256,2048]{2,1,0:T(8,128)(2,1)S(1)} copy-done((bf16[3,256,2048]{2,1,0:T(8,128)(2,1)S(1)}, bf16[3,256,2048]{2,1,0:T(8,128)(2,1)}, u32[]{:S(2)}) %copy-start) | copy-done | bytes 3145752
  121.9 8.8 %input_grad.1 = bf16[256,2048]{1,0:T(8,128)(2,1)} custom-call(bf16[3,256,2048]{2,1,0:T(8,128)(2,1)S(1)} %copy-done, f32[3,8,2048]{2,1,0:T(8,128)S(1)} %convert_element_type.26.after_ref, f32[3,7,2048]{2,1,0:T(8,128)S(1)} %copy-done.3, bf16[256,256]{1,0:T(8,128)(2,1)S(1)} %get-tuple-element.39.order_t_ref), custom_call_target="tpu_custom_call" | custom-call | tf_op jit(solution)/shard_map/input_grad/pallas_call | solution.py:319
  130.7 0.7 copy-done.17
  131.4 7.9 %spread.1 = (f32[3,7,2048]{2,1,0:T(8,128)}, f32[16,2048]{1,0:T(8,128)}, f32[1,2048]{1,0:T(1,128)}) custom-call(bf16[32,32,128]{2,1,0:T(8,128)(2,1)} %copy-done.17), custom_call_target="tpu_custom_call" | custom-call | tf_op jit(solution)/shard_map/spread/pallas_call | solution.py:335
  (48 shorter events, 1.4 us)
Async XLA Ops:
  0.6 46.8 %copy-start.5 = (f32[16,2048]{1,0:T(8,128)S(1)}, f32[16,2048]{1,0:T(8,128)}, u32[]{:S(2)}) copy-start(f32[16,2048]{1,0:T(8,128)} %rate_ref.3) | copy-start | bytes 393220
  1.4 17.0 %collective-permute-start = (s32[6]{0:T(128)S(1)}, s32[6]{0:T(128)S(1)}, u32[]{:S(2)}, u32[]{:S(2)}) collective-permute-start(s32[6]{0:T(128)S(1)} %slice.33), channel_id=1, source_target_pairs={{0,4},{4,8},{8,12},{12,16},{16,20},{20,24},{24,28},{28,32},{32,36}... | collective-permute-start | bytes 80 | tf_op jit(solution)/shard_map/ppermute | solution.py:21
  8.5 60.9 %copy-start.16 = (f32[2048]{0:T(1024)S(1)}, f32[2048]{0:T(1024)}, u32[]{:S(2)}) copy-start(f32[2048]{0:T(1024)} %param.15) | copy-start | bytes 24580
  20.9 0.8 copy-start.6
  21.7 1.2 copy-start.1
  22.9 0.9 copy-start.2
  23.9 0.9 copy-start.4
  24.8 0.8 copy-start.8
  25.6 0.8 copy-start.9
  26.4 0.7 copy-start.15
  37.8 0.7 copy-start.10
  38.5 0.6 copy-start.13
  39.2 15.7 %all-to-all-start = ((f32[32,16,128]{2,1,0:T(8,128)}), f32[32,16,128]{2,1,0:T(8,128)}, u32[]{:S(2)}, u32[]{:S(2)}) async-start(f32[32,16,128]{2,1,0:T(8,128)} %copy-done.10), calls=%async_computation | async-start | bytes 524288 | tf_op jit(solution)/shard_map/all_to_all | solution.py:230
  69.3 0.8 copy-start.7
  70.1 0.9 copy-start.12
  71.0 0.8 copy-start.14
  90.6 0.7 copy-start.11
  91.3 28.7 %copy-start.3 = (f32[3,7,2048]{2,1,0:T(8,128)S(1)}, f32[3,7,2048]{2,1,0:T(8,128)}, u32[]{:S(2)}) copy-start(f32[3,7,2048]{2,1,0:T(8,128)} %weight_ref.3) | copy-start | bytes 516100
  105.7 25.0 %all-to-all-start.3 = ((bf16[32,32,128]{2,1,0:T(8,128)(2,1)}), bf16[32,32,128]{2,1,0:T(8,128)(2,1)S(1)}, u32[]{:S(2)}, u32[]{:S(2)}) async-start(bf16[32,32,128]{2,1,0:T(8,128)(2,1)} %sum.1), calls=%async_computation.3 | async-start | bytes 524288 | tf_op jit(solution)/shard_map/all_to_all | solution.py:230
  111.9 8.0 %collective-permute-start.1 = (bf16[3,8,2048]{2,1,0:T(8,128)(2,1)S(1)}, bf16[3,8,2048]{2,1,0:T(8,128)(2,1)S(1)}, u32[]{:S(2)}, u32[]{:S(2)}) collective-permute-start(bf16[3,8,2048]{2,1,0:T(8,128)(2,1)S(1)} %convert_element_type.25), channel_id=1, source_target_pairs={{4,0},{8,4},{12,8},{16,12},{20,16},{24,20},{28,24},{32,28},{36,32}... | collective-permute-start | bytes 294920 | tf_op jit(solution)/shard_map/ppermute | solution.py:21
  120.0 1.9 %copy-start = (bf16[3,256,2048]{2,1,0:T(8,128)(2,1)S(1)}, bf16[3,256,2048]{2,1,0:T(8,128)(2,1)}, u32[]{:S(2)}) copy-start(bf16[3,256,2048]{2,1,0:T(8,128)(2,1)} %get-tuple-element.23.grads_ref) | copy-start | bytes 9437188
  130.7 0.7 copy-start.17

commit v2 on v1

v2 whole, which is shorter than its diff:
```python
import jax
import jax.numpy as jnp
from jax import lax
from jax.experimental import pallas as pl
from jax.experimental.pallas import tpu as pltpu
from jax.sharding import PartitionSpec as P

D = 8192
POLES = 16
TAPS = 7
LETTERS = (65, 67, 71, 84)
FIRST_ROW = 64
SEGS = 8
LANES = 128
HALVES = 4
WIDTH = HALVES * LANES
PARAM_ROWS = 48
f32 = jnp.float32
bf16 = jnp.bfloat16


def rows(ref, n, h):
    return jnp.broadcast_to(ref[n : n + 1, part_of(h)], (SEGS, LANES))


def part_of(h):
    return slice(h * LANES, (h + 1) * LANES)


def tree(terms):
    while len(terms) > 1:
        odd = terms[len(terms) // 2 * 2 :]
        terms = [a + b for a, b in zip(terms[::2], terms[1::2])] + odd
    return terms[0]


def embed_kernel(table_ref, embed_ref, squares_ref):
    wide = table_ref[...].astype(f32)
    picked = [wide[v - FIRST_ROW : v - FIRST_ROW + 1] for v in LETTERS]
    embed = jnp.concatenate(picked + [jnp.zeros((4, wide.shape[1]), f32)], 0)
    embed_ref[...] = embed
    summed = jnp.sum(embed * embed, axis=1, keepdims=True)
    squares_ref[...] = jnp.broadcast_to(summed, squares_ref.shape)


def hot_kernel(tokens_ref, hot_ref, hot_t_ref, order_ref, order_t_ref):
    length = order_ref.shape[0]
    steps = length // SEGS
    margin = TAPS - 1
    letter = lax.broadcasted_iota(jnp.int32, (8, length), 0)
    value = jnp.full((8, length), -1, jnp.int32)
    for n, v in enumerate(LETTERS):
        value = jnp.where(letter == n, v, value)
    tokens = tokens_ref[...]
    pieces = []
    for i in range(TAPS):
        seen = jnp.broadcast_to(tokens[:, margin - i : margin - i + length], (8, length))
        pieces.append(jnp.where(seen == value, 1.0, 0.0))
    pieces.append(jnp.zeros((8, length), f32))
    natural = jnp.concatenate(pieces, 0).astype(bf16)
    row = lax.broadcasted_iota(jnp.int32, (length, length), 0)
    col = lax.broadcasted_iota(jnp.int32, (length, length), 1)
    order = jnp.where((row % SEGS) * steps + row // SEGS == col, 1.0, 0.0).astype(bf16)
    order_t = jnp.where((col % SEGS) * steps + col // SEGS == row, 1.0, 0.0).astype(bf16)
    order_ref[...] = order
    order_t_ref[...] = order_t
    hot_t_ref[...] = jnp.dot(natural, order_t, preferred_element_type=f32).astype(bf16)
    double = jnp.concatenate([natural, natural], 0)
    hot_ref[...] = lax.dot_general(
        order, double, (((1,), (1,)), ((), ())), preferred_element_type=f32
    ).astype(bf16)


def states_kernel(
    hot_ref, order_ref, embed_ref, sum0_ref, sum1_ref, sum2_ref, sum3_ref, gain_ref,
    weight_ref, rate_ref, cot_ref,
    feat_ref, cotp_ref, normed_ref, inner_ref, ends_ref, x_ref, g_ref,
):
    steps = x_ref.shape[1]
    squares = (sum0_ref[...] + sum1_ref[...]) + (sum2_ref[...] + sum3_ref[...])
    scale = lax.rsqrt(squares / D + 1e-05)
    scale = jnp.concatenate([scale] * HALVES, 1)
    normed = (embed_ref[...] * scale * gain_ref[...]).astype(bf16).astype(f32)
    normed_ref[...] = normed
    cot = jnp.dot(order_ref[...], cot_ref[...], preferred_element_type=f32)
    cotp_ref[...] = cot.astype(bf16)
    feats = []
    for f in range(3):
        table = jnp.concatenate(
            [weight_ref[f, i : i + 1, :] * normed for i in range(TAPS)]
            + [jnp.zeros((SEGS, WIDTH), f32)],
            0,
        )
        high = table.astype(bf16)
        low = (table - high.astype(f32)).astype(bf16)
        summed = jnp.dot(
            hot_ref[...], jnp.concatenate([high, low], 0), preferred_element_type=f32
        ).astype(bf16)
        feat_ref[f] = summed
        feats.append(summed.astype(f32))
    mixed = feats[1] * feats[2]
    glong = cot * feats[0]
    for h in range(HALVES):
        x_ref[h] = mixed[:, part_of(h)].reshape(steps, SEGS, LANES)
        g_ref[h] = glong[:, part_of(h)].reshape(steps, SEGS, LANES)
    seg = lax.broadcasted_iota(jnp.int32, (SEGS, LANES), 0)
    for h in range(HALVES):
        for part in range(2):
            base = part * 8
            rates = [rows(rate_ref, base + n, h) for n in range(8)]
            decay = [jnp.exp(-p) for p in rates]
            fwd = [jnp.zeros((SEGS, LANES), f32)] * 8
            bwd = fwd
            for i in range(steps):
                now = x_ref[h, i]
                fwd = [d * s + now for d, s in zip(decay, fwd)]
                now = g_ref[h, steps - 1 - i]
                bwd = [d * s + now for d, s in zip(decay, bwd)]
            for n in range(8):
                inc, dec = fwd[n], bwd[n]
                for hop in (1, 2, 4):
                    factor = jnp.exp(rates[n] * (-float(steps * hop)))
                    inc = inc + jnp.where(seg >= hop, factor, 0.0) * pltpu.roll(inc, hop, 0)
                    dec = dec + jnp.where(seg < SEGS - hop, factor, 0.0) * pltpu.roll(
                        dec, SEGS - hop, 0
                    )
                ends_ref[2 * h + part, n : n + 1, :] = inc[SEGS - 1 :]
                ends_ref[2 * h + part, 8 + n : 9 + n, :] = dec[0:1]
                inner_ref[0, base + n, :, part_of(h)] = jnp.where(
                    seg >= 1, pltpu.roll(inc, 1, 0), 0.0
                )
                inner_ref[1, base + n, :, part_of(h)] = jnp.where(
                    seg < SEGS - 1, pltpu.roll(dec, SEGS - 1, 0), 0.0
                )


def carry_kernel(length, got_ref, rate_ref, out_ref):
    devices = got_ref.shape[0]
    decay = jnp.exp(rate_ref[...] * (-float(length)))
    state = jnp.zeros((8, LANES), f32)
    adjoint = jnp.zeros((8, LANES), f32)
    for j in range(devices):
        out_ref[j, 0:8, :] = state
        state = decay * state + got_ref[j, 0:8, :]
        k = devices - 1 - j
        out_ref[k, 8:16, :] = adjoint
        adjoint = decay * adjoint + got_ref[k, 8:16, :]


def forward_kernel(
    feat_ref, cotp_ref, inner_ref, rate_ref, residue_ref, skip_ref,
    conv_ref, param_ref, x_ref, g_ref,
):
    steps = x_ref.shape[0]
    for h in range(HALVES):
        at = part_of(h)
        mixed = feat_ref[1, :, at].astype(f32) * feat_ref[2, :, at].astype(f32)
        glong = cotp_ref[:, at].astype(f32) * feat_ref[0, :, at].astype(f32)
        x_ref[...] = mixed.reshape(steps, SEGS, LANES)
        g_ref[...] = glong.reshape(steps, SEGS, LANES)
        skip = jnp.broadcast_to(skip_ref[:, at], (SEGS, LANES))
        total = jnp.zeros((SEGS, LANES), f32)
        pieces = []
        for part in range(2):
            base = part * 8
            decay = [jnp.exp(-rows(rate_ref, base + n, h)) for n in range(8)]
            residue = [rows(residue_ref, base + n, h) for n in range(8)]
            state = [inner_ref[0, base + n, :, at] for n in range(8)]
            acc = [jnp.zeros((SEGS, LANES), f32)] * 8
            for i in range(steps):
                now, other = x_ref[i], g_ref[i]
                state = [d * s + now for d, s in zip(decay, state)]
                summed = tree([r * s for r, s in zip(residue, state)])
                spot = slice(SEGS * i, SEGS * i + SEGS)
                conv_ref[spot, at] = summed + (conv_ref[spot, at] if part else skip * now)
                acc = [a + other * s for a, s in zip(acc, state)]
                if not part:
                    total = total + other * now
            pieces += [jnp.sum(a, 0, keepdims=True) for a in acc]
        pieces.append(jnp.sum(total, 0, keepdims=True))
        pieces.append(jnp.zeros((24 - len(pieces), LANES), f32))
        param_ref[:, at] = jnp.concatenate(pieces, 0)


def backward_kernel(
    feat_ref, cotp_ref, inner_ref, rate_ref, residue_ref, skip_ref, grad_ref, g_ref
):
    steps = g_ref.shape[0]
    for h in range(HALVES):
        at = part_of(h)
        glong = cotp_ref[:, at].astype(f32) * feat_ref[0, :, at].astype(f32)
        g_ref[...] = glong.reshape(steps, SEGS, LANES)
        skip = jnp.broadcast_to(skip_ref[:, at], (SEGS, LANES))
        for part in range(2):
            base = part * 8
            decay = [jnp.exp(-rows(rate_ref, base + n, h)) for n in range(8)]
            residue = [rows(residue_ref, base + n, h) for n in range(8)]
            state = [inner_ref[1, base + n, :, at] for n in range(8)]
            for i in reversed(range(steps)):
                now = g_ref[i]
                state = [d * s + now for d, s in zip(decay, state)]
                summed = tree([r * s for r, s in zip(residue, state)])
                spot = slice(SEGS * i, SEGS * i + SEGS)
                grad_ref[spot, at] = summed + (grad_ref[spot, at] if part else skip * now)


def finish_kernel(
    feat_ref, cotp_ref, conv_ref, mixgrad_ref, local_ref, ends_ref, enter_ref, rate_ref,
    residue_ref, hot_t_ref, normed_ref,
    y_ref, grads_ref, first_ref, params_ref, m_ref,
):
    length = y_ref.shape[0]
    steps = length // SEGS
    seg = lax.broadcasted_iota(jnp.int32, (SEGS, LANES), 0).astype(f32)
    for h in range(HALVES):
        at = part_of(h)
        rates = [rows(rate_ref, n, h) for n in range(POLES)]
        decay = [jnp.exp(-p) for p in rates]
        for way in range(2):
            gap = (SEGS - 1.0 - seg) if way else seg
            wave = []
            for n in range(POLES):
                line = 8 * way + n % 8
                entering = enter_ref[2 * h + n // 8, line : line + 1, :]
                start = entering * residue_ref[n : n + 1, at]
                wave.append(jnp.exp(rates[n] * (gap * (-float(steps)))) * start)
            src, dst = (mixgrad_ref, m_ref) if way else (conv_ref, y_ref)
            for k in range(steps):
                i = steps - 1 - k if way else k
                wave = [d * u for d, u in zip(decay, wave)]
                spot = slice(SEGS * i, SEGS * i + SEGS)
                dst[spot, at] = tree([src[spot, at]] + wave)
        for part in range(2):
            span = slice(8 * part, 8 * part + 8)
            cross = (
                enter_ref[2 * h + part, 0:8, :]
                * ends_ref[2 * h + part, 8:16, :]
                * jnp.exp(-rate_ref[span, at])
            )
            params_ref[span, at] = local_ref[span, at] + cross
    long_conv = y_ref[...]
    grad_mixed = m_ref[...]
    grads = [
        (cotp_ref[...].astype(f32) * long_conv).astype(bf16),
        (grad_mixed * feat_ref[2].astype(f32)).astype(bf16),
        (grad_mixed * feat_ref[1].astype(f32)).astype(bf16),
    ]
    normed = normed_ref[...]
    params_ref[40:48, :] = local_ref[16:24, :]
    heads = []
    for f in range(3):
        grads_ref[f] = grads[f]
        wide = grads[f].astype(f32)
        heads += [wide[8 * i : 8 * i + 1] for i in range(TAPS - 1)] + [jnp.zeros((2, WIDTH), f32)]
        by_token = jnp.dot(hot_t_ref[...], grads[f], preferred_element_type=f32)
        params_ref[16 + 8 * f : 24 + 8 * f, :] = jnp.concatenate(
            [
                jnp.sum(by_token[8 * i : 8 * i + 8] * normed, 0, keepdims=True)
                for i in range(TAPS + 1)
            ],
            0,
        )
    heads.append(jnp.zeros((8, WIDTH), f32))
    first_ref[...] = jnp.concatenate(heads, 0).astype(bf16)


def output_kernel(
    feat_ref, y_ref, grads_ref, after_ref, weight_ref, order_t_ref, *rest
):
    hyena_ref, out_ref, wide_ref, sum_ref = rest[-4:]
    hyena = (feat_ref[0].astype(f32) * y_ref[...]).astype(bf16)
    hyena_ref[...] = jnp.dot(order_t_ref[...], hyena, preferred_element_type=f32).astype(bf16)
    after = after_ref[...].astype(f32)
    steps = grads_ref.shape[1] // SEGS
    seg = lax.broadcasted_iota(jnp.int32, (SEGS, LANES), 0)
    for h in range(HALVES):
        at = part_of(h)
        for f in range(3):
            wide_ref[f, 0:steps] = (
                grads_ref[f, :, at].astype(f32).reshape(steps, SEGS, LANES)
            )
        weight = [
            [jnp.broadcast_to(weight_ref[f, i : i + 1, at], (SEGS, LANES)) for i in range(TAPS)]
            for f in range(3)
        ]
        ahead = [[wide_ref[f, i] for i in range(TAPS - 1)] for f in range(3)]
        for i in range(steps):
            terms = []
            for f in range(3):
                j = i + TAPS - 1
                if j < steps:
                    ahead[f].append(wide_ref[f, j])
                else:
                    j -= steps
                    last = jnp.broadcast_to(after[8 * f + j : 8 * f + j + 1, at], (SEGS, LANES))
                    turned = pltpu.roll(wide_ref[f, j], SEGS - 1, 0)
                    ahead[f].append(jnp.where(seg < SEGS - 1, turned, last))
                terms += [w * a for w, a in zip(weight[f], ahead[f])]
                ahead[f] = ahead[f][1:]
            sum_ref[SEGS * i : SEGS * i + SEGS, at] = tree(terms)
    out_ref[...] = jnp.dot(
        order_t_ref[...], sum_ref[...].astype(bf16), preferred_element_type=f32
    ).astype(bf16)


def spread_kernel(core_ref, mine_ref, other_ref, conv_ref, residue_ref, skip_ref):
    mine = mine_ref[...].astype(f32)
    other = other_ref[...].astype(f32)
    upper = core_ref[0] == 1
    both = jnp.concatenate(
        [jnp.where(upper, other, mine), jnp.where(upper, mine, other)], 1
    )
    residue_ref[...] = both[0:POLES]
    for f in range(3):
        conv_ref[f] = both[POLES + 8 * f : POLES + 8 * f + TAPS]
    skip_ref[...] = both[POLES + 24 : POLES + 25]


def whole(*shape):
    return pl.BlockSpec(shape, lambda b: (0,) * len(shape))


def lanes(*shape):
    return pl.BlockSpec(shape + (WIDTH,), lambda b: (0,) * len(shape) + (b,))


def firsts():
    return pl.BlockSpec((2 * HALVES, 16, LANES), lambda b: (b, 0, 0))


def struct(shape, dtype):
    return jax.ShapeDtypeStruct(shape, dtype)


def roomy():
    return pltpu.CompilerParams(vmem_limit_bytes=60 * 1024 * 1024)


def place(y, x, core):
    return y * 8 + x * 2 + core


def turn(block, dy, dx, dcore):
    route = [
        (place(y, x, c), place((y + dy) % 4, (x + dx) % 4, (c + dcore) % 2))
        for y in range(4)
        for x in range(4)
        for c in range(2)
    ]
    return lax.ppermute(block, "seq", route)


def shifted(block, distance):
    devices = range(lax.axis_size("seq"))
    route = [(i - distance, i) for i in devices if i - distance in devices]
    return lax.ppermute(block, "seq", route)


def added(own, *others):
    total = own.astype(f32)
    for other in others:
        total = total + other.astype(f32)
    return total.astype(bf16)


def exchange(block):
    return lax.all_to_all(block, "seq", 0, 0, tiled=True)


def per_device(
    token_ids, embedding, norm_gain, conv_weight, pole_rates, residues, skip_gain, cotangent
):
    length = token_ids.shape[0]
    channels = embedding.shape[1]
    margin = TAPS - 1
    steps = length // SEGS
    count = channels // WIDTH
    grid = (count,)
    owners = 2 * channels // LANES
    position = lax.axis_index("seq")
    core = position % 2

    embed, squares = pl.pallas_call(
        embed_kernel,
        grid=(1,),
        in_specs=[pl.BlockSpec((32, channels), lambda b: (FIRST_ROW // 32, 0))],
        out_specs=[whole(8, channels), whole(8, LANES)],
        out_shape=[struct((8, channels), f32), struct((8, LANES), f32)],
        compiler_params=roomy(),
        name="embed",
    )(embedding)
    leading = shifted(token_ids[length - margin :], 1)
    sums = [squares] + [
        lax.ppermute(squares, "ch", [(i, (i + k) % 4) for i in range(4)]) for k in (1, 2, 3)
    ]
    tail = jnp.zeros((LANES - margin,), jnp.int32)
    tokens = jnp.concatenate([leading, token_ids, tail])[None]
    hot, hot_t, order, order_t = pl.pallas_call(
        hot_kernel,
        out_shape=[
            struct((length, 128), bf16), struct((64, length), bf16),
            struct((length, length), bf16), struct((length, length), bf16),
        ],
        compiler_params=roomy(),
        name="hot",
    )(tokens)

    feats, cotp, normed, inner, ends = pl.pallas_call(
        states_kernel,
        grid=grid,
        in_specs=[whole(length, 128), whole(length, length), lanes(8)]
        + [whole(8, LANES)] * 4
        + [lanes(1), lanes(3, TAPS), lanes(POLES), lanes(length)],
        out_specs=[
            lanes(3, length), lanes(length), lanes(8), lanes(2, POLES, SEGS), firsts(),
        ],
        out_shape=[
            struct((3, length, channels), bf16), struct((length, channels), bf16),
            struct((8, channels), f32), struct((2, POLES, SEGS, channels), f32),
            struct((owners, 16, LANES), f32),
        ],
        scratch_shapes=[pltpu.VMEM((HALVES, steps, SEGS, LANES), f32)] * 2,
        compiler_params=roomy(),
        name="states",
    )(hot, order, embed, *sums, norm_gain[None], conv_weight, pole_rates, cotangent)

    own_rates = lax.dynamic_slice(pole_rates, (core * 8, (position // 2) * LANES), (8, LANES))
    gathered = exchange(ends)
    local = [lanes(3, length), lanes(length), lanes(2, POLES, SEGS), lanes(POLES), lanes(POLES),
             lanes(1)]
    conv_local, param_local = pl.pallas_call(
        forward_kernel,
        grid=grid,
        in_specs=local,
        out_specs=[lanes(length), lanes(24)],
        out_shape=[struct((length, channels), f32), struct((24, channels), f32)],
        scratch_shapes=[pltpu.VMEM((steps, SEGS, LANES), f32)] * 2,
        compiler_params=roomy(),
        name="forward",
    )(feats, cotp, inner, pole_rates, residues, skip_gain[None])
    gathered, conv_local = lax.optimization_barrier((gathered, conv_local))
    carried = pl.pallas_call(
        lambda *refs: carry_kernel(length, *refs),
        out_shape=struct((owners, 16, LANES), f32),
        compiler_params=roomy(),
        name="carry",
    )(gathered, own_rates)
    carried, cotp_late = lax.optimization_barrier((carried, cotp))
    entering = exchange(carried)
    mix_local = pl.pallas_call(
        backward_kernel,
        grid=grid,
        in_specs=local,
        out_specs=lanes(length),
        out_shape=struct((length, channels), f32),
        scratch_shapes=[pltpu.VMEM((steps, SEGS, LANES), f32)],
        compiler_params=roomy(),
        name="backward",
    )(feats, cotp_late, inner, pole_rates, residues, skip_gain[None])

    long_conv, grads, first, params = pl.pallas_call(
        finish_kernel,
        grid=grid,
        in_specs=[
            lanes(3, length), lanes(length), lanes(length), lanes(length), lanes(24), firsts(),
            firsts(), lanes(POLES), lanes(POLES), whole(64, length), lanes(8),
        ],
        out_specs=[lanes(length), lanes(3, length), lanes(32), lanes(PARAM_ROWS)],
        out_shape=[
            struct((length, channels), f32), struct((3, length, channels), bf16),
            struct((32, channels), bf16), struct((PARAM_ROWS, channels), f32),
        ],
        scratch_shapes=[pltpu.VMEM((length, WIDTH), f32)],
        compiler_params=roomy(),
        name="finish",
    )(
        feats, cotp, conv_local, mix_local, param_local, ends, entering, pole_rates, residues,
        hot_t, normed,
    )

    after = shifted(first, -1)
    half = channels // 2
    kept = lax.dynamic_slice(params, (0, core * half), (PARAM_ROWS, half))
    given = lax.dynamic_slice(params, (0, (1 - core) * half), (PARAM_ROWS, half))
    chip = added(kept, turn(given.astype(bf16), 0, 0, 1))
    near = [turn(chip, 0, k, 0) for k in (1, 2, 3)]
    half_grid = count // 2

    def outputs(start, *previous):
        def spot(*shape):
            return pl.BlockSpec(
                shape + (WIDTH,), lambda b: (0,) * len(shape) + (b + start,)
            )

        anywhere = [pl.BlockSpec(memory_space=pl.ANY)] * len(previous)
        return pl.pallas_call(
            output_kernel,
            grid=(half_grid,),
            in_specs=[
                spot(1, length), spot(length), spot(3, length), spot(32), spot(3, TAPS),
                whole(length, length), *anywhere,
            ],
            out_specs=[spot(length), spot(length)],
            out_shape=[struct((length, channels), bf16)] * 2,
            scratch_shapes=[
                pltpu.VMEM((3, steps, SEGS, LANES), f32), pltpu.VMEM((length, WIDTH), f32),
            ],
            input_output_aliases={6: 0, 7: 1} if previous else {},
            compiler_params=roomy(),
            name="outputs",
        )(feats, long_conv, grads, after, conv_weight, order_t, *previous)

    hyena, grad_input = outputs(0)
    *near, hyena, grad_input = lax.optimization_barrier((*near, hyena, grad_input))
    row = added(chip, *near)
    far = [turn(row, k, 0, 0) for k in (1, 2, 3)]
    row, hyena, grad_input = lax.optimization_barrier((row, hyena, grad_input))
    hyena, grad_input = outputs(half_grid, hyena, grad_input)
    *far, hyena, grad_input = lax.optimization_barrier((*far, hyena, grad_input))
    mine = added(row, *far)
    other = turn(mine, 0, 0, 1)
    vmem = pl.BlockSpec(memory_space=pltpu.VMEM)
    conv_total, residue_total, skip_total = pl.pallas_call(
        spread_kernel,
        in_specs=[pl.BlockSpec(memory_space=pltpu.SMEM), vmem, vmem],
        out_shape=[
            struct((3, TAPS, channels), f32), struct((POLES, channels), f32),
            struct((1, channels), f32),
        ],
        compiler_params=roomy(),
        name="spread",
    )(core[None].astype(jnp.int32), mine, other)
    return hyena, grad_input, conv_total, residue_total, skip_total[0]


def solution(mesh):
    in_specs = (
        P("seq"),
        P(None, "ch"),
        P("ch"),
        P(None, None, "ch"),
        P(None, "ch"),
        P(None, "ch"),
        P("ch"),
        P("seq", "ch"),
    )
    out_specs = (P("seq", "ch"), P("seq", "ch"), P(None, None, "ch"), P(None, "ch"), P("ch"))
    return jax.shard_map(
        per_device, mesh=mesh, in_specs=in_specs, out_specs=out_specs, check_vma=False
    )
```

time: 141 us -> 106 us (0.75)
  blocking collectives: 35.2 us -> 0 us
  starting transfers between devices: 19.4 us -> 34.9 us
  local copies, waits for them, and re-layouts: 19 us -> 6.16 us
  waiting for transfers between devices: 12.6 us -> 6.47 us
  Pallas kernels: 49.7 us -> 54.6 us
  other arithmetic: 2.68 us -> 1.14 us
    all_to_all x2 -> x0, blocking collectives: 25.4 us -> none  [exchange(): return lax.all_to_all(block, 'seq', 0, 0, tiled=True)]
    ppermute x2 -> x13, starting transfers between devices: 5.94 us -> 19.2 us  [the longest x8 6.97 us: turn(): return lax.ppermute(block, 'seq', route)]
    psum x1 -> x0, blocking collectives: 9.75 us -> none  [per_device(): sum_squares = lax.psum(jnp.sum(embed * embed, axis=1), 'ch')]
    unnamed x36 -> x18, local copies, waits for them, and re-layouts: 12.6 us -> 3.29 us
    all_to_all x2, waiting for transfers between devices: 6.86 us -> 0.01 us  [exchange(): return lax.all_to_all(block, 'seq', 0, 0, tiled=True)]
    pallas_call x5 -> x9, Pallas kernels: 48 us -> 52.8 us  [the longest x1 10.8 us: per_device(): pl.pallas_call(finish_kernel, grid=grid, in_specs=[lanes(3, length), lane...]
    all_to_all x2, starting transfers between devices: 13.4 us -> 15.7 us  [exchange(): return lax.all_to_all(block, 'seq', 0, 0, tiled=True)]
    slice x3 -> x1, local copies, waits for them, and re-layouts: 1.77 us -> 0.07 us  [per_device(): leading = shifted(token_ids[length - margin:], 1)]
  transfers between devices with their start and end apart: 4 -> 15, of which waited for: 2 -> 3; matrix products, arithmetic and copies ran while one was open for 4% -> 3% of each run, Pallas kernels for 6% -> 28%
where the time goes in v2:
time: 106 us; the launch traced here: 104 us
  Pallas kernels  54.6 us (52%)
  starting transfers between devices  34.9 us (33%)
  waiting for transfers between devices  6.47 us (6%)
  local copies, waits for them, and re-layouts  6.16 us (6%)
  other arithmetic  1.14 us (1%)
    all_to_all x2, starting transfers between devices, exchange(): return lax.all_to_all(block, 'seq', 0, 0, tiled=True)  15.7 us
    pallas_call x1, Pallas kernels, per_device(): pl.pallas_call(finish_kernel, grid=grid, in_specs=[lanes(3, length), lane...  10.8 us
    pallas_call x1, Pallas kernels, per_device(): pl.pallas_call(states_kernel, grid=grid, in_specs=[whole(length, 128), wh...  10.1 us
    pallas_call x1, Pallas kernels, per_device(): pl.pallas_call(forward_kernel, grid=grid, in_specs=local, out_specs=[lane...  9.96 us
    pallas_call x2, Pallas kernels, outputs(): pl.pallas_call(output_kernel, grid=(half_grid,), in_specs=[spot(1, length...  9.42 us
    pallas_call x1, Pallas kernels, per_device(): pl.pallas_call(backward_kernel, grid=grid, in_specs=local, out_specs=lane...  7.61 us
    ppermute x8, starting transfers between devices, turn(): return lax.ppermute(block, 'seq', route)  6.97 us
    ppermute x2, starting transfers between devices, shifted(): return lax.ppermute(block, 'seq', route)  6.55 us
  transfers between devices with their start and end apart: 15, of which 3 were waited for; matrix products, arithmetic and copies ran while one was open for 3% of the time, Pallas kernels for 28%

profile of v2, /device:TPU:7, one launch (start us, length us, event | category | flops | bytes accessed | tf_op | source)
XLA Modules:
  0.0 104.1 jit_solution(6304564214530499178)
XLA Ops:
  0.6 1.6 %embed.1 = (f32[8,2048]{1,0:T(8,128)}, f32[8,128]{1,0:T(8,128)}) custom-call(bf16[512,2048]{1,0:T(8,128)(2,1)} %table_ref.1), custom_call_target="tpu_custom_call" | custom-call | tf_op jit(solution)/shard_map/embed/pallas_call | solution.py:383
  2.3 1.6 %collective-permute-start.1 = (f32[8,128]{1,0:T(8,128)}, f32[8,128]{1,0:T(8,128)S(1)}, u32[]{:S(2)}, u32[]{:S(2)}) collective-permute-start(f32[8,128]{1,0:T(8,128)} %get-tuple-element.49.sum0_ref), channel_id=1, source_target_pairs={{0,1},{1,2},{2,3},{3,0},{4,5},{5,6},{6,7},{7,4},{8,9},{9,10},{10,1... | collective-permute-start | bytes 12296 | tf_op jit(solution)/shard_map/ppermute | solution.py:394
  3.9 3.3 %collective-permute-start.2 = (f32[8,128]{1,0:T(8,128)}, f32[8,128]{1,0:T(8,128)S(1)}, u32[]{:S(2)}, u32[]{:S(2)}) collective-permute-start(f32[8,128]{1,0:T(8,128)} %get-tuple-element.49.sum0_ref), channel_id=1, source_target_pairs={{0,2},{1,3},{2,0},{3,1},{4,6},{5,7},{6,4},{7,5},{8,10},{9,11},{10,... | collective-permute-start | bytes 12296 | tf_op jit(solution)/shard_map/ppermute | solution.py:394
  7.2 0.7 collective-permute-start.3
  7.9 0.1 slice.3
  8.0 4.5 %collective-permute-start = (s32[6]{0:T(128)S(1)}, s32[6]{0:T(128)S(1)}, u32[]{:S(2)}, u32[]{:S(2)}) collective-permute-start(s32[6]{0:T(128)S(1)} %slice.3), channel_id=1, source_target_pairs={{0,4},{4,8},{8,12},{12,16},{16,20},{20,24},{24,28},{28,32},{32,36}... | collective-permute-start | bytes 80 | tf_op jit(solution)/shard_map/ppermute | solution.py:356
  12.5 0.7 collective-permute-done
  13.2 0.1 pad_add_fusion
  13.3 0.6 broadcast_in_dim.17.tokens_ref
  13.9 1.7 %hot.1 = (bf16[256,128]{1,0:T(8,128)(2,1)}, bf16[64,256]{1,0:T(8,128)(2,1)}, bf16[256,256]{1,0:T(8,128)(2,1)}, bf16[256,256]{1,0:T(8,128)(2,1)}) custom-call(s32[1,384]{1,0:T(1,128)} %broadcast_in_dim.17.tokens_ref), custom_call_target="tpu_custom_call" | custom-call | tf_op jit(solution)/shard_map/hot/pallas_call | solution.py:398
  15.5 0.0 collective-permute-done.1.sum1_ref
  15.6 0.0 collective-permute-done.3.sum3_ref
  15.6 0.5 copy-done.5
  16.1 0.0 copy-done.6
  16.1 0.0 copy-done.7
  16.2 10.1 %states.1 = (bf16[3,256,2048]{2,1,0:T(8,128)(2,1)}, bf16[256,2048]{1,0:T(8,128)(2,1)}, f32[8,2048]{1,0:T(8,128)}, f32[2,16,8,2048]{3,2,1,0:T(8,128)}, f32[32,16,128]{2,1,0:T(8,128)}) custom-call(bf16[256,128]{1,0:T(8,128)(2,1)} %get-tuple-element.46.hot_ref, bf16[256,256]{1,0:T(8,128)(2,1)} %get-tuple-element.47.order_ref, ...), custom_call_target="tpu_custom_call" | custom-call | tf_op jit(solution)/shard_map/states/pallas_call | solution.py:408
  26.2 8.4 %all-to-all-start = ((f32[32,16,128]{2,1,0:T(8,128)}), f32[32,16,128]{2,1,0:T(8,128)S(1)}, u32[]{:S(2)}, u32[]{:S(2)}) async-start(f32[32,16,128]{2,1,0:T(8,128)} %get-tuple-element.52.ends_ref), calls=%async_computation | async-start | bytes 524288 | tf_op jit(solution)/shard_map/all_to_all | solution.py:367
  34.6 1.3 %dynamic_slice.9.refs_1_ = f32[8,128]{1,0:T(8,128)} dynamic-slice(f32[16,2048]{1,0:T(8,128)} %rate_ref.7, s32[]{:T(128)S(6)} %select_n.24, s32[]{:T(128)S(6)} %select_n.26), dynamic_slice_sizes={8,128} | dynamic-slice | bytes 8196 | tf_op jit(solution)/shard_map/dynamic_slice | solution.py:427
  35.9 10.0 %forward.1 = (f32[256,2048]{1,0:T(8,128)}, f32[24,2048]{1,0:T(8,128)}) custom-call(bf16[3,256,2048]{2,1,0:T(8,128)(2,1)} %get-tuple-element.50.feat_ref, bf16[256,2048]{1,0:T(8,128)(2,1)} %get-tuple-element.57.cotp_ref, f32[2,16,8,2048]{3,2,1,0:T(8,128)} %get-tuple-element.53.inner_ref, f32[16,2048]{1,0:T(8,128)} %rate_ref.7, f32[16,2048]{1,0:T(8,128)} %residue_ref.5, ...), custom_call_target="tpu_custom_call" | custom-call | tf_op jit(solution)/shard_map/forward/pallas_call | solution.py:431
  45.9 0.0 all-to-all-done.refs_0_
  45.9 0.0 copy-start.1
  45.9 0.7 copy-done.1
  46.6 1.7 %carry.1 = f32[32,16,128]{2,1,0:T(8,128)} custom-call(f32[32,16,128]{2,1,0:T(8,128)} %copy-done.1, f32[8,128]{1,0:T(8,128)} %dynamic_slice.9.refs_1_), custom_call_target="tpu_custom_call" | custom-call | tf_op jit(solution)/shard_map/carry/pallas_call | solution.py:442
  48.3 7.4 %all-to-all-start.1 = ((f32[32,16,128]{2,1,0:T(8,128)}), f32[32,16,128]{2,1,0:T(8,128)S(1)}, u32[]{:S(2)}, u32[]{:S(2)}) async-start(f32[32,16,128]{2,1,0:T(8,128)} %carry.1), calls=%async_computation.1 | async-start | bytes 524288 | tf_op jit(solution)/shard_map/all_to_all | solution.py:367
  55.7 7.6 %backward.1.mixgrad_ref = f32[256,2048]{1,0:T(8,128)} custom-call(bf16[3,256,2048]{2,1,0:T(8,128)(2,1)} %get-tuple-element.50.feat_ref, bf16[256,2048]{1,0:T(8,128)(2,1)} %get-tuple-element.57.cotp_ref, f32[2,16,8,2048]{3,2,1,0:T(8,128)} %get-tuple-element.53.inner_ref, f32[16,2048]{1,0:T(8,128)} %rate_ref.7, f32[16,2048]{1,0:T(8,128)} %residue_ref.5, ...), custom_call_target="tpu_custom_call" | custom-call | tf_op jit(solution)/shard_map/backward/pallas_call | solution.py:450
  63.3 0.7 copy-done
  64.0 10.8 %finish.1 = (f32[256,2048]{1,0:T(8,128)}, bf16[3,256,2048]{2,1,0:T(8,128)(2,1)}, bf16[32,2048]{1,0:T(8,128)(2,1)}, f32[48,2048]{1,0:T(8,128)}) custom-call(bf16[3,256,2048]{2,1,0:T(8,128)(2,1)} %get-tuple-element.50.feat_ref, bf16[256,2048]{1,0:T(8,128)(2,1)} %get-tuple-element.57.cotp_ref, f32[256,2048]{1,0:T(8,128)} %get-tuple-element.55.conv_ref, ...), custom_call_target="tpu_custom_call" | custom-call | tf_op jit(solution)/shard_map/finish/pallas_call | solution.py:461
  74.9 0.9 dynamic-slice_convert_fusion
  75.8 0.4 collective-permute-start.4
  76.3 2.0 %collective-permute-start.8 = (bf16[32,2048]{1,0:T(8,128)(2,1)}, bf16[32,2048]{1,0:T(8,128)(2,1)S(1)}, u32[]{:S(2)}, u32[]{:S(2)}) collective-permute-start(bf16[32,2048]{1,0:T(8,128)(2,1)} %get-tuple-element.65), channel_id=1, source_target_pairs={{4,0},{8,4},{12,8},{16,12},{20,16},{24,20},{28,24},{32,28},{36,32}... | collective-permute-start | bytes 393224 | tf_op jit(solution)/shard_map/ppermute | solution.py:356
  78.3 1.0 add_convert_fusion.2
  79.3 1.4 %collective-permute-start.5 = (bf16[48,1024]{1,0:T(8,128)(2,1)S(1)}, bf16[48,1024]{1,0:T(8,128)(2,1)S(1)}, u32[]{:S(2)}, u32[]{:S(2)}) collective-permute-start(bf16[48,1024]{1,0:T(8,128)(2,1)S(1)} %add_convert_fusion.2), channel_id=1, source_target_pairs={{0,8},{4,12},{8,16},{12,20},{16,24},{20,28},{24,0},{28,4},{32,40},... | collective-permute-start | bytes 294920 | tf_op jit(solution)/shard_map/ppermute | solution.py:350
  80.7 1.0 collective-permute-start.6
  81.7 0.0 collective-permute-start.7
  81.7 4.5 %collective-permute-done.8.after_ref = bf16[32,2048]{1,0:T(8,128)(2,1)S(1)} collective-permute-done((bf16[32,2048]{1,0:T(8,128)(2,1)}, bf16[32,2048]{1,0:T(8,128)(2,1)S(1)}, u32[]{:S(2)}, u32[]{:S(2)}) %collective-permute-start.8) | collective-permute-done | bytes 131104 | tf_op jit(solution)/shard_map/ppermute | solution.py:356
  86.2 0.7 copy-done.2
  86.8 4.7 %outputs.2 = (bf16[256,2048]{1,0:T(8,128)(2,1)}, bf16[256,2048]{1,0:T(8,128)(2,1)}) custom-call(bf16[3,256,2048]{2,1,0:T(8,128)(2,1)} %get-tuple-element.50.feat_ref, f32[256,2048]{1,0:T(8,128)} %get-tuple-element.63.y_ref, bf16[3,256,2048]{2,1,0:T(8,128)(2,1)} %get-tuple-element.64.grads_ref, bf16[32,2048]{1,0:T(8,128)(2,1)} %copy-done.2, ...), custom_call_target="tpu_custom_call" | custom-call | tf_op jit(solution)/shard_map/outputs/pallas_call | solution.py:496
  91.6 0.0 collective-permute-done.5
  91.6 0.1 add_convert_fusion.1
  91.6 2.5 %collective-permute-start.10 = (bf16[48,1024]{1,0:T(8,128)(2,1)S(1)}, bf16[48,1024]{1,0:T(8,128)(2,1)S(1)}, u32[]{:S(2)}, u32[]{:S(2)}) collective-permute-start(bf16[48,1024]{1,0:T(8,128)(2,1)S(1)} %add_convert_fusion.1), channel_id=1, source_target_pairs={{0,64},{4,68},{8,72},{12,76},{16,80},{20,84},{24,88},{28,92},{32,9... | collective-permute-start | bytes 294920 | tf_op jit(solution)/shard_map/ppermute | solution.py:350
  94.2 0.9 collective-permute-start.11
  95.0 0.6 collective-permute-start.9
  95.6 4.7 %outputs.3 = (bf16[256,2048]{1,0:T(8,128)(2,1)}, bf16[256,2048]{1,0:T(8,128)(2,1)}) custom-call(bf16[3,256,2048]{2,1,0:T(8,128)(2,1)} %get-tuple-element.50.feat_ref, f32[256,2048]{1,0:T(8,128)} %get-tuple-element.63.y_ref, bf16[3,256,2048]{2,1,0:T(8,128)(2,1)} %get-tuple-element.64.grads_ref, ...), custom_call_target="tpu_custom_call", output_to_operand_aliasing={{0}: (6, {}), {1}: (7, {})} | custom-call | tf_op jit(solution)/shard_map/outputs/pallas_call | solution.py:496
  100.4 0.1 add_convert_fusion.mine_ref
  100.4 0.1 collective-permute-start.12
  100.5 1.3 %collective-permute-done.12.other_ref = bf16[48,1024]{1,0:T(8,128)(2,1)S(1)} collective-permute-done((bf16[48,1024]{1,0:T(8,128)(2,1)S(1)}, bf16[48,1024]{1,0:T(8,128)(2,1)S(1)}, u32[]{:S(2)}, u32[]{:S(2)}) %collective-permute-start.12) | collective-permute-done | bytes 98336 | tf_op jit(solution)/shard_map/ppermute | solution.py:350
  101.8 0.6 copy-done.4
  102.4 1.7 %spread.1 = (f32[3,7,2048]{2,1,0:T(8,128)}, f32[16,2048]{1,0:T(8,128)}, f32[1,2048]{1,0:T(1,128)}) custom-call(s32[1]{0:T(128)} %bitcast.2.core_ref, bf16[48,1024]{1,0:T(8,128)(2,1)} %copy-done.3, bf16[48,1024]{1,0:T(8,128)(2,1)} %copy-done.4), custom_call_target="tpu_custom_call" | custom-call | tf_op jit(solution)/shard_map/spread/pallas_call | solution.py:523
  (19 shorter events, 0.0 us)
Async XLA Ops:
  0.6 7.3 %copy-start.8 = (s32[256]{0:T(256)S(1)}, s32[256]{0:T(256)}, u32[]{:S(2)}) copy-start(s32[256]{0:T(256)} %param.8) | copy-start | bytes 3076
  2.3 13.3 %collective-permute-start.1 = (f32[8,128]{1,0:T(8,128)}, f32[8,128]{1,0:T(8,128)S(1)}, u32[]{:S(2)}, u32[]{:S(2)}) collective-permute-start(f32[8,128]{1,0:T(8,128)} %get-tuple-element.49.sum0_ref), channel_id=1, source_target_pairs={{0,1},{1,2},{2,3},{3,0},{4,5},{5,6},{6,7},{7,4},{8,9},{9,10},{10,1... | collective-permute-start | bytes 12296 | tf_op jit(solution)/shard_map/ppermute | solution.py:394
  3.9 11.6 %collective-permute-start.2 = (f32[8,128]{1,0:T(8,128)}, f32[8,128]{1,0:T(8,128)S(1)}, u32[]{:S(2)}, u32[]{:S(2)}) collective-permute-start(f32[8,128]{1,0:T(8,128)} %get-tuple-element.49.sum0_ref), channel_id=1, source_target_pairs={{0,2},{1,3},{2,0},{3,1},{4,6},{5,7},{6,4},{7,5},{8,10},{9,11},{10,... | collective-permute-start | bytes 12296 | tf_op jit(solution)/shard_map/ppermute | solution.py:394
  7.2 8.4 %collective-permute-start.3 = (f32[8,128]{1,0:T(8,128)}, f32[8,128]{1,0:T(8,128)S(1)}, u32[]{:S(2)}, u32[]{:S(2)}) collective-permute-start(f32[8,128]{1,0:T(8,128)} %get-tuple-element.49.sum0_ref), channel_id=1, source_target_pairs={{0,3},{1,0},{2,1},{3,2},{4,7},{5,4},{6,5},{7,6},{8,11},{9,8},{10,9... | collective-permute-start | bytes 12296 | tf_op jit(solution)/shard_map/ppermute | solution.py:394
  8.0 5.2 %collective-permute-start = (s32[6]{0:T(128)S(1)}, s32[6]{0:T(128)S(1)}, u32[]{:S(2)}, u32[]{:S(2)}) collective-permute-start(s32[6]{0:T(128)S(1)} %slice.3), channel_id=1, source_target_pairs={{0,4},{4,8},{8,12},{12,16},{16,20},{20,24},{24,28},{28,32},{32,36}... | collective-permute-start | bytes 80 | tf_op jit(solution)/shard_map/ppermute | solution.py:356
  15.5 0.6 copy-start.5
  15.6 0.6 copy-start.6
  15.6 0.6 copy-start.7
  26.2 19.6 %all-to-all-start = ((f32[32,16,128]{2,1,0:T(8,128)}), f32[32,16,128]{2,1,0:T(8,128)S(1)}, u32[]{:S(2)}, u32[]{:S(2)}) async-start(f32[32,16,128]{2,1,0:T(8,128)} %get-tuple-element.52.ends_ref), calls=%async_computation | async-start | bytes 524288 | tf_op jit(solution)/shard_map/all_to_all | solution.py:367
  45.9 0.7 copy-start.1
  48.3 15.0 %all-to-all-start.1 = ((f32[32,16,128]{2,1,0:T(8,128)}), f32[32,16,128]{2,1,0:T(8,128)S(1)}, u32[]{:S(2)}, u32[]{:S(2)}) async-start(f32[32,16,128]{2,1,0:T(8,128)} %carry.1), calls=%async_computation.1 | async-start | bytes 524288 | tf_op jit(solution)/shard_map/all_to_all | solution.py:367
  63.3 0.7 copy-start
  75.8 2.5 %collective-permute-start.4 = (bf16[48,1024]{1,0:T(8,128)(2,1)S(1)}, bf16[48,1024]{1,0:T(8,128)(2,1)S(1)}, u32[]{:S(2)}, u32[]{:S(2)}) collective-permute-start(bf16[48,1024]{1,0:T(8,128)(2,1)S(1)} %dynamic-slice_convert_fusion), channel_id=1, source_target_pairs={{0,4},{4,0},{8,12},{12,8},{16,20},{20,16},{24,28},{28,24},{32,36},... | collective-permute-start | bytes 294920 | tf_op jit(solution)/shard_map/ppermute | solution.py:350
  76.3 9.9 %collective-permute-start.8 = (bf16[32,2048]{1,0:T(8,128)(2,1)}, bf16[32,2048]{1,0:T(8,128)(2,1)S(1)}, u32[]{:S(2)}, u32[]{:S(2)}) collective-permute-start(bf16[32,2048]{1,0:T(8,128)(2,1)} %get-tuple-element.65), channel_id=1, source_target_pairs={{4,0},{8,4},{12,8},{16,12},{20,16},{24,20},{28,24},{32,28},{36,32}... | collective-permute-start | bytes 393224 | tf_op jit(solution)/shard_map/ppermute | solution.py:356
  79.3 12.3 %collective-permute-start.5 = (bf16[48,1024]{1,0:T(8,128)(2,1)S(1)}, bf16[48,1024]{1,0:T(8,128)(2,1)S(1)}, u32[]{:S(2)}, u32[]{:S(2)}) collective-permute-start(bf16[48,1024]{1,0:T(8,128)(2,1)S(1)} %add_convert_fusion.2), channel_id=1, source_target_pairs={{0,8},{4,12},{8,16},{12,20},{16,24},{20,28},{24,0},{28,4},{32,40},... | collective-permute-start | bytes 294920 | tf_op jit(solution)/shard_map/ppermute | solution.py:350
  80.7 10.9 %collective-permute-start.6 = (bf16[48,1024]{1,0:T(8,128)(2,1)S(1)}, bf16[48,1024]{1,0:T(8,128)(2,1)S(1)}, u32[]{:S(2)}, u32[]{:S(2)}) collective-permute-start(bf16[48,1024]{1,0:T(8,128)(2,1)S(1)} %add_convert_fusion.2), channel_id=1, source_target_pairs={{0,16},{4,20},{8,24},{12,28},{16,0},{20,4},{24,8},{28,12},{32,48},... | collective-permute-start | bytes 294920 | tf_op jit(solution)/shard_map/ppermute | solution.py:350
  81.7 9.9 %collective-permute-start.7 = (bf16[48,1024]{1,0:T(8,128)(2,1)S(1)}, bf16[48,1024]{1,0:T(8,128)(2,1)S(1)}, u32[]{:S(2)}, u32[]{:S(2)}) collective-permute-start(bf16[48,1024]{1,0:T(8,128)(2,1)S(1)} %add_convert_fusion.2), channel_id=1, source_target_pairs={{0,24},{4,28},{8,0},{12,4},{16,8},{20,12},{24,16},{28,20},{32,56},... | collective-permute-start | bytes 294920 | tf_op jit(solution)/shard_map/ppermute | solution.py:350
  86.2 0.7 copy-start.2
  91.6 8.7 %collective-permute-start.10 = (bf16[48,1024]{1,0:T(8,128)(2,1)S(1)}, bf16[48,1024]{1,0:T(8,128)(2,1)S(1)}, u32[]{:S(2)}, u32[]{:S(2)}) collective-permute-start(bf16[48,1024]{1,0:T(8,128)(2,1)S(1)} %add_convert_fusion.1), channel_id=1, source_target_pairs={{0,64},{4,68},{8,72},{12,76},{16,80},{20,84},{24,88},{28,92},{32,9... | collective-permute-start | bytes 294920 | tf_op jit(solution)/shard_map/ppermute | solution.py:350
  94.2 6.2 %collective-permute-start.11 = (bf16[48,1024]{1,0:T(8,128)(2,1)S(1)}, bf16[48,1024]{1,0:T(8,128)(2,1)S(1)}, u32[]{:S(2)}, u32[]{:S(2)}) collective-permute-start(bf16[48,1024]{1,0:T(8,128)(2,1)S(1)} %add_convert_fusion.1), channel_id=1, source_target_pairs={{0,96},{4,100},{8,104},{12,108},{16,112},{20,116},{24,120},{28,124... | collective-permute-start | bytes 294920 | tf_op jit(solution)/shard_map/ppermute | solution.py:350
  95.0 5.3 %collective-permute-start.9 = (bf16[48,1024]{1,0:T(8,128)(2,1)S(1)}, bf16[48,1024]{1,0:T(8,128)(2,1)S(1)}, u32[]{:S(2)}, u32[]{:S(2)}) collective-permute-start(bf16[48,1024]{1,0:T(8,128)(2,1)S(1)} %add_convert_fusion.1), channel_id=1, source_target_pairs={{0,32},{4,36},{8,40},{12,44},{16,48},{20,52},{24,56},{28,60},{32,6... | collective-permute-start | bytes 294920 | tf_op jit(solution)/shard_map/ppermute | solution.py:350
  100.4 1.4 %copy-start.3 = (bf16[48,1024]{1,0:T(8,128)(2,1)}, bf16[48,1024]{1,0:T(8,128)(2,1)S(1)}, u32[]{:S(2)}) copy-start(bf16[48,1024]{1,0:T(8,128)(2,1)S(1)} %add_convert_fusion.mine_ref) | copy-start | bytes 294916
  100.4 1.4 %collective-permute-start.12 = (bf16[48,1024]{1,0:T(8,128)(2,1)S(1)}, bf16[48,1024]{1,0:T(8,128)(2,1)S(1)}, u32[]{:S(2)}, u32[]{:S(2)}) collective-permute-start(bf16[48,1024]{1,0:T(8,128)(2,1)S(1)} %add_convert_fusion.mine_ref), channel_id=1, source_target_pairs={{0,4},{4,0},{8,12},{12,8},{16,20},{20,16},{24,28},{28,24},{32,36},... | collective-permute-start | bytes 294920 | tf_op jit(solution)/shard_map/ppermute | solution.py:350
  101.8 0.6 copy-start.4

commit v3 on v2

--- a/solution.py
+++ b/solution.py
@@ -24,7 +24,17 @@
 
 
 def part_of(h):
-    return slice(h * LANES, (h + 1) * LANES)
+    if isinstance(h, int):
+        return slice(h * LANES, (h + 1) * LANES)
+    return pl.ds(pl.multiple_of(h * LANES, LANES), LANES)
+
+
+def each_part(body):
+    def step(h, carry):
+        body(h)
+        return carry
+
+    lax.fori_loop(0, HALVES, step, 0)
 
 
 def tree(terms):
@@ -104,7 +114,8 @@
         x_ref[h] = mixed[:, part_of(h)].reshape(steps, SEGS, LANES)
         g_ref[h] = glong[:, part_of(h)].reshape(steps, SEGS, LANES)
     seg = lax.broadcasted_iota(jnp.int32, (SEGS, LANES), 0)
-    for h in range(HALVES):
+
+    def scan(h):
         for part in range(2):
             base = part * 8
             rates = [rows(rate_ref, base + n, h) for n in range(8)]
@@ -124,8 +135,9 @@
                     dec = dec + jnp.where(seg < SEGS - hop, factor, 0.0) * pltpu.roll(
                         dec, SEGS - hop, 0
                     )
-                ends_ref[2 * h + part, n : n + 1, :] = inc[SEGS - 1 :]
-                ends_ref[2 * h + part, 8 + n : 9 + n, :] = dec[0:1]
+                ends_ref[0, base + n : base + n + 1, part_of(h)] = inc[SEGS - 1 :]
+                line = POLES + base + n
+                ends_ref[0, line : line + 1, part_of(h)] = dec[0:1]
                 inner_ref[0, base + n, :, part_of(h)] = jnp.where(
                     seg >= 1, pltpu.roll(inc, 1, 0), 0.0
                 )
@@ -133,26 +145,91 @@
                     seg < SEGS - 1, pltpu.roll(dec, SEGS - 1, 0), 0.0
                 )
 
-
-def carry_kernel(length, got_ref, rate_ref, out_ref):
-    devices = got_ref.shape[0]
-    decay = jnp.exp(rate_ref[...] * (-float(length)))
-    state = jnp.zeros((8, LANES), f32)
-    adjoint = jnp.zeros((8, LANES), f32)
-    for j in range(devices):
-        out_ref[j, 0:8, :] = state
-        state = decay * state + got_ref[j, 0:8, :]
-        k = devices - 1 - j
-        out_ref[k, 8:16, :] = adjoint
-        adjoint = decay * adjoint + got_ref[k, 8:16, :]
-
-
-def forward_kernel(
-    feat_ref, cotp_ref, inner_ref, rate_ref, residue_ref, skip_ref,
-    conv_ref, param_ref, x_ref, g_ref,
+    each_part(scan)
+
+
+def decays(rate_ref, core, devices):
+    half = rate_ref.shape[1] // 2
+    spot = pl.ds(pl.multiple_of(core * half, half), half)
+    return jnp.exp(rate_ref[:, spot] * (-float(devices)))
+
+
+def chip_kernel(
+    length, place_ref, own_ref, other_ref, rate_ref, chip_ref, pair_ref, *sent_refs
 ):
-    steps = x_ref.shape[0]
-    for h in range(HALVES):
+    core = place_ref[0] % 2
+    y = place_ref[0] // 8
+    decay = decays(rate_ref, core, length)
+    own, other = own_ref[core], other_ref[core]
+    low, high = jnp.where(core == 0, own, other), jnp.where(core == 0, other, own)
+    state = decay * low[:POLES] + high[:POLES]
+    adjoint = low[POLES:] + decay * high[POLES:]
+    chip_ref[0:POLES] = state
+    chip_ref[POLES:] = adjoint
+    pair_ref[0:POLES] = low[:POLES]
+    pair_ref[POLES:] = high[POLES:]
+    for k, sent_ref in enumerate(sent_refs):
+        sent_ref[...] = jnp.where(y + k + 1 < 4, state, adjoint)
+
+
+def column_kernel(length, place_ref, chip_ref, got1_ref, got2_ref, got3_ref, rate_ref, *outs):
+    core = place_ref[0] % 2
+    x = place_ref[0] // 2 % 4
+    y = place_ref[0] // 8
+    row = decays(rate_ref, core, 8 * length)
+    power = [jnp.ones_like(row), row, row * row]
+    before = jnp.zeros_like(row)
+    behind = jnp.zeros_like(row)
+    for k, got_ref in enumerate((got1_ref, got2_ref, got3_ref)):
+        got = got_ref[...]
+        lower = y >= k + 1
+        before = before + jnp.where(lower, power[k] * got, 0.0)
+        behind = behind + jnp.where(lower, 0.0, power[2 - k] * got)
+    state = chip_ref[0:POLES] + row * before
+    adjoint = chip_ref[POLES:] + row * behind
+    outs[0][0:POLES] = before
+    outs[0][POLES:] = behind
+    for k, sent_ref in enumerate(outs[1:]):
+        upward = x + k + 1 < 4
+        sent_ref[0:POLES] = jnp.where(upward, state, before)
+        sent_ref[POLES:] = jnp.where(upward, behind, adjoint)
+
+
+def row_kernel(
+    length, place_ref, pair_ref, column_ref, got1_ref, got2_ref, got3_ref, rate_ref,
+    mine_ref, sent_ref,
+):
+    core = place_ref[0] % 2
+    decay = decays(rate_ref, core, length)
+    chip = decay * decay
+    power = [jnp.ones_like(chip), chip, chip * chip]
+    state = power[2] * chip * column_ref[0:POLES]
+    adjoint = power[2] * chip * column_ref[POLES:]
+    for k, got_ref in enumerate((got1_ref, got2_ref, got3_ref)):
+        state = state + power[k] * got_ref[0:POLES]
+        adjoint = adjoint + power[2 - k] * got_ref[POLES:]
+    first = core == 0
+    next_state = decay * state + pair_ref[0:POLES]
+    next_adjoint = decay * adjoint + pair_ref[POLES:]
+    mine_ref[0:POLES] = jnp.where(first, state, next_state)
+    sent_ref[0:POLES] = jnp.where(first, next_state, state)
+    mine_ref[POLES:] = jnp.where(first, next_adjoint, adjoint)
+    sent_ref[POLES:] = jnp.where(first, adjoint, next_adjoint)
+
+
+def main_kernel(
+    place_ref, feat_ref, cotp_ref, inner_ref, mine_ref, other_ref, rate_ref, residue_ref,
+    skip_ref, hot_t_ref, normed_ref,
+    y_ref, grads_ref, first_ref, params_ref, m_ref, x_ref, g_ref, enter_ref, sums_ref,
+):
+    length = y_ref.shape[0]
+    steps = length // SEGS
+    blocks = pl.num_programs(0)
+    here = pl.program_id(0) // (blocks // 2) == place_ref[0] % 2
+    enter_ref[...] = jnp.where(here, mine_ref[...], other_ref[...])
+    seg = lax.broadcasted_iota(jnp.int32, (SEGS, LANES), 0).astype(f32)
+
+    def scan(h):
         at = part_of(h)
         mixed = feat_ref[1, :, at].astype(f32) * feat_ref[2, :, at].astype(f32)
         glong = cotp_ref[:, at].astype(f32) * feat_ref[0, :, at].astype(f32)
@@ -163,81 +240,39 @@
         pieces = []
         for part in range(2):
             base = part * 8
-            decay = [jnp.exp(-rows(rate_ref, base + n, h)) for n in range(8)]
+            rates = [rows(rate_ref, base + n, h) for n in range(8)]
+            decay = [jnp.exp(-p) for p in rates]
             residue = [rows(residue_ref, base + n, h) for n in range(8)]
-            state = [inner_ref[0, base + n, :, at] for n in range(8)]
-            acc = [jnp.zeros((SEGS, LANES), f32)] * 8
-            for i in range(steps):
-                now, other = x_ref[i], g_ref[i]
-                state = [d * s + now for d, s in zip(decay, state)]
-                summed = tree([r * s for r, s in zip(residue, state)])
-                spot = slice(SEGS * i, SEGS * i + SEGS)
-                conv_ref[spot, at] = summed + (conv_ref[spot, at] if part else skip * now)
-                acc = [a + other * s for a, s in zip(acc, state)]
-                if not part:
-                    total = total + other * now
-            pieces += [jnp.sum(a, 0, keepdims=True) for a in acc]
-        pieces.append(jnp.sum(total, 0, keepdims=True))
-        pieces.append(jnp.zeros((24 - len(pieces), LANES), f32))
-        param_ref[:, at] = jnp.concatenate(pieces, 0)
-
-
-def backward_kernel(
-    feat_ref, cotp_ref, inner_ref, rate_ref, residue_ref, skip_ref, grad_ref, g_ref
-):
-    steps = g_ref.shape[0]
-    for h in range(HALVES):
-        at = part_of(h)
-        glong = cotp_ref[:, at].astype(f32) * feat_ref[0, :, at].astype(f32)
-        g_ref[...] = glong.reshape(steps, SEGS, LANES)
-        skip = jnp.broadcast_to(skip_ref[:, at], (SEGS, LANES))
-        for part in range(2):
-            base = part * 8
-            decay = [jnp.exp(-rows(rate_ref, base + n, h)) for n in range(8)]
-            residue = [rows(residue_ref, base + n, h) for n in range(8)]
-            state = [inner_ref[1, base + n, :, at] for n in range(8)]
-            for i in reversed(range(steps)):
-                now = g_ref[i]
-                state = [d * s + now for d, s in zip(decay, state)]
-                summed = tree([r * s for r, s in zip(residue, state)])
-                spot = slice(SEGS * i, SEGS * i + SEGS)
-                grad_ref[spot, at] = summed + (grad_ref[spot, at] if part else skip * now)
-
-
-def finish_kernel(
-    feat_ref, cotp_ref, conv_ref, mixgrad_ref, local_ref, ends_ref, enter_ref, rate_ref,
-    residue_ref, hot_t_ref, normed_ref,
-    y_ref, grads_ref, first_ref, params_ref, m_ref,
-):
-    length = y_ref.shape[0]
-    steps = length // SEGS
-    seg = lax.broadcasted_iota(jnp.int32, (SEGS, LANES), 0).astype(f32)
-    for h in range(HALVES):
-        at = part_of(h)
-        rates = [rows(rate_ref, n, h) for n in range(POLES)]
-        decay = [jnp.exp(-p) for p in rates]
-        for way in range(2):
-            gap = (SEGS - 1.0 - seg) if way else seg
-            wave = []
-            for n in range(POLES):
-                line = 8 * way + n % 8
-                entering = enter_ref[2 * h + n // 8, line : line + 1, :]
-                start = entering * residue_ref[n : n + 1, at]
-                wave.append(jnp.exp(rates[n] * (gap * (-float(steps)))) * start)
-            src, dst = (mixgrad_ref, m_ref) if way else (conv_ref, y_ref)
-            for k in range(steps):
-                i = steps - 1 - k if way else k
-                wave = [d * u for d, u in zip(decay, wave)]
-                spot = slice(SEGS * i, SEGS * i + SEGS)
-                dst[spot, at] = tree([src[spot, at]] + wave)
-        for part in range(2):
-            span = slice(8 * part, 8 * part + 8)
-            cross = (
-                enter_ref[2 * h + part, 0:8, :]
-                * ends_ref[2 * h + part, 8:16, :]
-                * jnp.exp(-rate_ref[span, at])
-            )
-            params_ref[span, at] = local_ref[span, at] + cross
+            for way in range(2):
+                gap = ((SEGS - 1.0 - seg) if way else seg) * (-float(steps))
+                src, dst = (g_ref, m_ref) if way else (x_ref, y_ref)
+                state = [
+                    inner_ref[way, base + n, :, at]
+                    + jnp.exp(rates[n] * gap)
+                    * enter_ref[POLES * way + base + n : POLES * way + base + n + 1, at]
+                    for n in range(8)
+                ]
+                acc = [jnp.zeros((SEGS, LANES), f32)] * 8
+                for k in range(steps):
+                    i = steps - 1 - k if way else k
+                    now = src[i]
+                    state = [d * s + now for d, s in zip(decay, state)]
+                    summed = tree([r * s for r, s in zip(residue, state)])
+                    spot = slice(SEGS * i, SEGS * i + SEGS)
+                    dst[spot, at] = summed + (dst[spot, at] if part else skip * now)
+                    if not way:
+                        other = g_ref[i]
+                        acc = [a + other * s for a, s in zip(acc, state)]
+                        if not part:
+                            total = total + other * now
+                if not way:
+                    pieces += [jnp.sum(a, 0, keepdims=True) for a in acc]
+        sums_ref[0:POLES, at] = jnp.concatenate(pieces, 0)
+        sums_ref[40:48, at] = jnp.concatenate(
+            [jnp.sum(total, 0, keepdims=True), jnp.zeros((7, LANES), f32)], 0
+        )
+
+    each_part(scan)
     long_conv = y_ref[...]
     grad_mixed = m_ref[...]
     grads = [
@@ -246,14 +281,13 @@
         (grad_mixed * feat_ref[1].astype(f32)).astype(bf16),
     ]
     normed = normed_ref[...]
-    params_ref[40:48, :] = local_ref[16:24, :]
     heads = []
     for f in range(3):
         grads_ref[f] = grads[f]
-        wide = grads[f].astype(f32)
+        wide = grads[f][: 8 * TAPS - 8].astype(f32)
         heads += [wide[8 * i : 8 * i + 1] for i in range(TAPS - 1)] + [jnp.zeros((2, WIDTH), f32)]
         by_token = jnp.dot(hot_t_ref[...], grads[f], preferred_element_type=f32)
-        params_ref[16 + 8 * f : 24 + 8 * f, :] = jnp.concatenate(
+        sums_ref[16 + 8 * f : 24 + 8 * f, :] = jnp.concatenate(
             [
                 jnp.sum(by_token[8 * i : 8 * i + 8] * normed, 0, keepdims=True)
                 for i in range(TAPS + 1)
@@ -262,18 +296,20 @@
         )
     heads.append(jnp.zeros((8, WIDTH), f32))
     first_ref[...] = jnp.concatenate(heads, 0).astype(bf16)
+    params_ref[0] = sums_ref[...].astype(bf16)
 
 
 def output_kernel(
-    feat_ref, y_ref, grads_ref, after_ref, weight_ref, order_t_ref, *rest
+    feat_ref, y_ref, grads_ref, halo_ref, weight_ref, order_t_ref, *rest
 ):
-    hyena_ref, out_ref, wide_ref, sum_ref = rest[-4:]
+    hyena_ref, out_ref, wide_ref, sum_ref, after_ref = rest[-5:]
     hyena = (feat_ref[0].astype(f32) * y_ref[...]).astype(bf16)
     hyena_ref[...] = jnp.dot(order_t_ref[...], hyena, preferred_element_type=f32).astype(bf16)
-    after = after_ref[...].astype(f32)
+    after_ref[...] = halo_ref[...].astype(f32)
     steps = grads_ref.shape[1] // SEGS
     seg = lax.broadcasted_iota(jnp.int32, (SEGS, LANES), 0)
-    for h in range(HALVES):
+
+    def taps(h):
         at = part_of(h)
         for f in range(3):
             wide_ref[f, 0:steps] = (
@@ -292,12 +328,14 @@
                     ahead[f].append(wide_ref[f, j])
                 else:
                     j -= steps
-                    last = jnp.broadcast_to(after[8 * f + j : 8 * f + j + 1, at], (SEGS, LANES))
+                    last = rows(after_ref, 8 * f + j, h)
                     turned = pltpu.roll(wide_ref[f, j], SEGS - 1, 0)
                     ahead[f].append(jnp.where(seg < SEGS - 1, turned, last))
                 terms += [w * a for w, a in zip(weight[f], ahead[f])]
                 ahead[f] = ahead[f][1:]
             sum_ref[SEGS * i : SEGS * i + SEGS, at] = tree(terms)
+
+    each_part(taps)
     out_ref[...] = jnp.dot(
         order_t_ref[...], sum_ref[...].astype(bf16), preferred_element_type=f32
     ).astype(bf16)
@@ -324,16 +362,12 @@
     return pl.BlockSpec(shape + (WIDTH,), lambda b: (0,) * len(shape) + (b,))
 
 
-def firsts():
-    return pl.BlockSpec((2 * HALVES, 16, LANES), lambda b: (b, 0, 0))
-
-
 def struct(shape, dtype):
     return jax.ShapeDtypeStruct(shape, dtype)
 
 
-def roomy():
-    return pltpu.CompilerParams(vmem_limit_bytes=60 * 1024 * 1024)
+def roomy(mib=60):
+    return pltpu.CompilerParams(vmem_limit_bytes=mib * 1024 * 1024)
 
 
 def place(y, x, core):
@@ -361,10 +395,6 @@
     for other in others:
         total = total + other.astype(f32)
     return total.astype(bf16)
-
-
-def exchange(block):
-    return lax.all_to_all(block, "seq", 0, 0, tiled=True)
 
 
 def per_device(
@@ -376,7 +406,6 @@
     steps = length // SEGS
     count = channels // WIDTH
     grid = (count,)
-    owners = 2 * channels // LANES
     position = lax.axis_index("seq")
     core = position % 2
 
@@ -412,77 +441,81 @@
         + [whole(8, LANES)] * 4
         + [lanes(1), lanes(3, TAPS), lanes(POLES), lanes(length)],
         out_specs=[
-            lanes(3, length), lanes(length), lanes(8), lanes(2, POLES, SEGS), firsts(),
+            lanes(3, length), lanes(length), lanes(8), lanes(2, POLES, SEGS),
+            pl.BlockSpec((1, 2 * POLES, WIDTH), lambda b: (b // (count // 2), 0, b % (count // 2))),
         ],
         out_shape=[
             struct((3, length, channels), bf16), struct((length, channels), bf16),
             struct((8, channels), f32), struct((2, POLES, SEGS, channels), f32),
-            struct((owners, 16, LANES), f32),
+            struct((2, 2 * POLES, channels // 2), f32),
         ],
         scratch_shapes=[pltpu.VMEM((HALVES, steps, SEGS, LANES), f32)] * 2,
         compiler_params=roomy(),
         name="states",
     )(hot, order, embed, *sums, norm_gain[None], conv_weight, pole_rates, cotangent)
 
-    own_rates = lax.dynamic_slice(pole_rates, (core * 8, (position // 2) * LANES), (8, LANES))
-    gathered = exchange(ends)
-    local = [lanes(3, length), lanes(length), lanes(2, POLES, SEGS), lanes(POLES), lanes(POLES),
-             lanes(1)]
-    conv_local, param_local = pl.pallas_call(
-        forward_kernel,
-        grid=grid,
-        in_specs=local,
-        out_specs=[lanes(length), lanes(24)],
-        out_shape=[struct((length, channels), f32), struct((24, channels), f32)],
-        scratch_shapes=[pltpu.VMEM((steps, SEGS, LANES), f32)] * 2,
-        compiler_params=roomy(),
-        name="forward",
-    )(feats, cotp, inner, pole_rates, residues, skip_gain[None])
-    gathered, conv_local = lax.optimization_barrier((gathered, conv_local))
-    carried = pl.pallas_call(
-        lambda *refs: carry_kernel(length, *refs),
-        out_shape=struct((owners, 16, LANES), f32),
-        compiler_params=roomy(),
-        name="carry",
-    )(gathered, own_rates)
-    carried, cotp_late = lax.optimization_barrier((carried, cotp))
-    entering = exchange(carried)
-    mix_local = pl.pallas_call(
-        backward_kernel,
-        grid=grid,
-        in_specs=local,
-        out_specs=lanes(length),
-        out_shape=struct((length, channels), f32),
-        scratch_shapes=[pltpu.VMEM((steps, SEGS, LANES), f32)],
-        compiler_params=roomy(),
-        name="backward",
-    )(feats, cotp_late, inner, pole_rates, residues, skip_gain[None])
+    place = position[None].astype(jnp.int32)
+    smem = pl.BlockSpec(memory_space=pltpu.SMEM)
+    vmem = pl.BlockSpec(memory_space=pltpu.VMEM)
+    half = channels // 2
+    one, two = struct((POLES, half), f32), struct((2 * POLES, half), f32)
+
+    def small(body, name, out_shape, *args):
+        return pl.pallas_call(
+            lambda *refs: body(length, *refs),
+            in_specs=[smem] + [vmem] * len(args),
+            out_specs=[vmem] * len(out_shape),
+            out_shape=out_shape,
+            compiler_params=pltpu.CompilerParams(vmem_limit_bytes=16 * 1024 * 1024),
+            name=name,
+        )(place, *args)
+
+    paired = turn(ends, 0, 0, 1)
+    chip, pair, *sent = small(
+        chip_kernel, "chip", [two, two, one, one, one], ends, paired, pole_rates
+    )
+    got = [turn(block, k + 1, 0, 0) for k, block in enumerate(sent)]
+    column, *sent = small(
+        column_kernel, "column", [two, two, two, two], chip, *got, pole_rates
+    )
+    got = [turn(block, 0, k + 1, 0) for k, block in enumerate(sent)]
+    mine, sent = small(
+        row_kernel, "row", [two, two], pair, column, *got, pole_rates
+    )
+    other = turn(sent, 0, 0, 1)
 
     long_conv, grads, first, params = pl.pallas_call(
-        finish_kernel,
+        main_kernel,
         grid=grid,
         in_specs=[
-            lanes(3, length), lanes(length), lanes(length), lanes(length), lanes(24), firsts(),
-            firsts(), lanes(POLES), lanes(POLES), whole(64, length), lanes(8),
-        ],
-        out_specs=[lanes(length), lanes(3, length), lanes(32), lanes(PARAM_ROWS)],
+            smem, lanes(3, length), lanes(length), lanes(2, POLES, SEGS),
+            pl.BlockSpec((2 * POLES, WIDTH), lambda b: (0, b % (count // 2))),
+            pl.BlockSpec((2 * POLES, WIDTH), lambda b: (0, b % (count // 2))),
+            lanes(POLES), lanes(POLES), lanes(1), whole(64, length), lanes(8),
+        ],
+        out_specs=[
+            lanes(length), lanes(3, length), lanes(32),
+            pl.BlockSpec(
+                (1, PARAM_ROWS, WIDTH), lambda b: (b // (count // 2), 0, b % (count // 2))
+            ),
+        ],
         out_shape=[
             struct((length, channels), f32), struct((3, length, channels), bf16),
-            struct((32, channels), bf16), struct((PARAM_ROWS, channels), f32),
-        ],
-        scratch_shapes=[pltpu.VMEM((length, WIDTH), f32)],
-        compiler_params=roomy(),
-        name="finish",
+            struct((32, channels), bf16), struct((2, PARAM_ROWS, half), bf16),
+        ],
+        scratch_shapes=[pltpu.VMEM((length, WIDTH), f32)]
+        + [pltpu.VMEM((steps, SEGS, LANES), f32)] * 2
+        + [pltpu.VMEM((2 * POLES, WIDTH), f32), pltpu.VMEM((PARAM_ROWS, WIDTH), f32)],
+        compiler_params=roomy(60),
+        name="main",
     )(
-        feats, cotp, conv_local, mix_local, param_local, ends, entering, pole_rates, residues,
-        hot_t, normed,
+        place, feats, cotp, inner, mine, other, pole_rates, residues, skip_gain[None], hot_t,
+        normed,
     )
 
     after = shifted(first, -1)
-    half = channels // 2
-    kept = lax.dynamic_slice(params, (0, core * half), (PARAM_ROWS, half))
-    given = lax.dynamic_slice(params, (0, (1 - core) * half), (PARAM_ROWS, half))
-    chip = added(kept, turn(given.astype(bf16), 0, 0, 1))
+    joined = turn(params, 0, 0, 1)
+    chip = added(*[lax.dynamic_index_in_dim(p, core, 0, False) for p in (params, joined)])
     near = [turn(chip, 0, k, 0) for k in (1, 2, 3)]
     half_grid = count // 2
 
@@ -504,6 +537,7 @@
             out_shape=[struct((length, channels), bf16)] * 2,
             scratch_shapes=[
                 pltpu.VMEM((3, steps, SEGS, LANES), f32), pltpu.VMEM((length, WIDTH), f32),
+                pltpu.VMEM((32, WIDTH), f32),
             ],
             input_output_aliases={6: 0, 7: 1} if previous else {},
             compiler_params=roomy(),
@@ -519,15 +553,14 @@
     *far, hyena, grad_input = lax.optimization_barrier((*far, hyena, grad_input))
     mine = added(row, *far)
     other = turn(mine, 0, 0, 1)
-    vmem = pl.BlockSpec(memory_space=pltpu.VMEM)
     conv_total, residue_total, skip_total = pl.pallas_call(
         spread_kernel,
-        in_specs=[pl.BlockSpec(memory_space=pltpu.SMEM), vmem, vmem],
+        in_specs=[smem, vmem, vmem],
         out_shape=[
             struct((3, TAPS, channels), f32), struct((POLES, channels), f32),
             struct((1, channels), f32),
         ],
-        compiler_params=roomy(),
+        compiler_params=roomy(16),
         name="spread",
     )(core[None].astype(jnp.int32), mine, other)
     return hyena, grad_input, conv_total, residue_total, skip_total[0]

time: 106 us -> 96.8 us (0.913); the launches traced: 104 us -> 96.2 us
  Pallas kernels: 54.6 us -> 42.2 us
  waiting for transfers between devices: 6.47 us -> 17.2 us
  starting transfers between devices: 34.9 us -> 30.7 us
  local copies, waits for them, and re-layouts: 6.16 us -> 4.15 us
    all_to_all x2 -> x0, starting transfers between devices: 15.7 us -> none  [exchange(): return lax.all_to_all(block, 'seq', 0, 0, tiled=True)]
    pallas_call x5, Pallas kernels: 31.8 us -> 18 us  [the longest x1 17.1 us: per_device(): pl.pallas_call(main_kernel, grid=grid, in_specs=[smem, lanes(3, length),...]
    ppermute x8 -> x16, starting transfers between devices: 6.97 us -> 19.7 us  [turn(): return lax.ppermute(block, 'seq', route)]
    ppermute x8 -> x16, waiting for transfers between devices: 1.31 us -> 11.8 us  [turn(): return lax.ppermute(block, 'seq', route)]
    dynamic_slice x1 -> x0, local copies, waits for them, and re-layouts: 1.29 us -> none  [per_device(): lax.dynamic_slice(pole_rates, (core * 8, position // 2 * LANES), (8, LANES))]
    ppermute x3, starting transfers between devices: 5.67 us -> 4.46 us  [per_device(): lax.ppermute(squares, 'ch', [(i, (i + k) % 4) for i in range(4)])]
  transfers between devices with their start and end apart: 15 -> 21, of which waited for: 3 -> 10; matrix products, arithmetic and copies ran while one was open for 3% -> 2% of each run, Pallas kernels for 28% -> 12%
where the time goes in v3:
time: 96.8 us; the launch traced here: 96.2 us
  Pallas kernels  42.2 us (44%)
  starting transfers between devices  30.7 us (32%)
  waiting for transfers between devices  17.2 us (18%)
  local copies, waits for them, and re-layouts  4.15 us (4%)
  other arithmetic  1.11 us (1%)
    ppermute x16, starting transfers between devices, turn(): return lax.ppermute(block, 'seq', route)  19.7 us
    pallas_call x1, Pallas kernels, per_device(): pl.pallas_call(main_kernel, grid=grid, in_specs=[smem, lanes(3, length),...  17.1 us
    ppermute x16, waiting for transfers between devices, turn(): return lax.ppermute(block, 'seq', route)  11.8 us
    pallas_call x1, Pallas kernels, per_device(): pl.pallas_call(states_kernel, grid=grid, in_specs=[whole(length, 128), wh...  10.6 us
    pallas_call x2, Pallas kernels, outputs(): pl.pallas_call(output_kernel, grid=(half_grid,), in_specs=[spot(1, length...  10.2 us
    ppermute x2, starting transfers between devices, shifted(): return lax.ppermute(block, 'seq', route)  6.55 us
    ppermute x2, waiting for transfers between devices, shifted(): return lax.ppermute(block, 'seq', route)  5.37 us
    ppermute x3, starting transfers between devices, per_device(): lax.ppermute(squares, 'ch', [(i, (i + k) % 4) for i in range(4)])  4.46 us
  transfers between devices with their start and end apart: 21, of which 10 were waited for; matrix products, arithmetic and copies ran while one was open for 2% of the time, Pallas kernels for 12%

profile of v3, /device:TPU:7, one launch (start us, length us, event | category | flops | bytes accessed | tf_op | source)
XLA Modules:
  0.0 96.2 jit_solution(4290806190986748118)
XLA Ops:
  0.7 1.6 %embed.1 = (f32[8,2048]{1,0:T(8,128)}, f32[8,128]{1,0:T(8,128)}) custom-call(bf16[512,2048]{1,0:T(8,128)(2,1)} %table_ref.1), custom_call_target="tpu_custom_call" | custom-call | tf_op jit(solution)/shard_map/embed/pallas_call | solution.py:412
  2.3 3.8 %collective-permute-start.3 = (f32[8,128]{1,0:T(8,128)}, f32[8,128]{1,0:T(8,128)S(1)}, u32[]{:S(2)}, u32[]{:S(2)}) collective-permute-start(f32[8,128]{1,0:T(8,128)} %get-tuple-element.54.sum0_ref), channel_id=1, source_target_pairs={{0,3},{1,0},{2,1},{3,2},{4,7},{5,4},{6,5},{7,6},{8,11},{9,8},{10,9... | collective-permute-start | bytes 12296 | tf_op jit(solution)/shard_map/ppermute | solution.py:423
  6.1 0.7 collective-permute-start.1
  6.8 0.1 slice.3
  6.8 4.5 %collective-permute-start = (s32[6]{0:T(128)S(1)}, s32[6]{0:T(128)S(1)}, u32[]{:S(2)}, u32[]{:S(2)}) collective-permute-start(s32[6]{0:T(128)S(1)} %slice.3), channel_id=1, source_target_pairs={{0,4},{4,8},{8,12},{12,16},{16,20},{20,24},{24,28},{28,32},{32,36}... | collective-permute-start | bytes 80 | tf_op jit(solution)/shard_map/ppermute | solution.py:390
  11.3 0.7 collective-permute-done
  12.1 0.1 pad_add_fusion
  12.1 0.6 broadcast_in_dim.20.tokens_ref
  12.7 1.7 %hot.1 = (bf16[256,128]{1,0:T(8,128)(2,1)}, bf16[64,256]{1,0:T(8,128)(2,1)}, bf16[256,256]{1,0:T(8,128)(2,1)}, bf16[256,256]{1,0:T(8,128)(2,1)}) custom-call(s32[1,384]{1,0:T(1,128)} %broadcast_in_dim.20.tokens_ref), custom_call_target="tpu_custom_call" | custom-call | tf_op jit(solution)/shard_map/hot/pallas_call | solution.py:427
  14.4 0.5 copy-done.5
  15.0 10.6 %states.1 = (bf16[3,256,2048]{2,1,0:T(8,128)(2,1)}, bf16[256,2048]{1,0:T(8,128)(2,1)}, f32[8,2048]{1,0:T(8,128)}, f32[2,16,8,2048]{3,2,1,0:T(8,128)}, f32[2,32,1024]{2,1,0:T(8,128)}) custom-call(bf16[256,128]{1,0:T(8,128)(2,1)} %get-tuple-element.51.hot_ref, bf16[256,256]{1,0:T(8,128)(2,1)} %get-tuple-element.52.order_ref, ...), custom_call_target="tpu_custom_call" | custom-call | tf_op jit(solution)/shard_map/states/pallas_call | solution.py:437
  25.6 1.2 %collective-permute-start.4 = (f32[2,32,1024]{2,1,0:T(8,128)}, f32[2,32,1024]{2,1,0:T(8,128)S(1)}, u32[]{:S(2)}, u32[]{:S(2)}) collective-permute-start(f32[2,32,1024]{2,1,0:T(8,128)} %get-tuple-element.58.refs_1_), channel_id=1, source_target_pairs={{0,4},{4,0},{8,12},{12,8},{16,20},{20,16},{24,28},{28,24},{32,36},... | collective-permute-start | bytes 786440 | tf_op jit(solution)/shard_map/ppermute | solution.py:384
  26.9 1.4 %collective-permute-done.4.refs_2_ = f32[2,32,1024]{2,1,0:T(8,128)S(1)} collective-permute-done((f32[2,32,1024]{2,1,0:T(8,128)}, f32[2,32,1024]{2,1,0:T(8,128)S(1)}, u32[]{:S(2)}, u32[]{:S(2)}) %collective-permute-start.4) | collective-permute-done | bytes 262176 | tf_op jit(solution)/shard_map/ppermute | solution.py:384
  28.2 0.9 copy-done.1
  29.2 1.4 %collective-permute-start.5 = (f32[16,1024]{1,0:T(8,128)S(1)}, f32[16,1024]{1,0:T(8,128)S(1)}, u32[]{:S(2)}, u32[]{:S(2)}) collective-permute-start(f32[16,1024]{1,0:T(8,128)S(1)} %get-tuple-element.61), channel_id=1, source_target_pairs={{0,32},{4,36},{8,40},{12,44},{16,48},{20,52},{24,56},{28,60},{32,6... | collective-permute-start | bytes 196616 | tf_op jit(solution)/shard_map/ppermute | solution.py:384
  30.6 2.6 %collective-permute-start.6 = (f32[16,1024]{1,0:T(8,128)S(1)}, f32[16,1024]{1,0:T(8,128)S(1)}, u32[]{:S(2)}, u32[]{:S(2)}) collective-permute-start(f32[16,1024]{1,0:T(8,128)S(1)} %get-tuple-element.62), channel_id=1, source_target_pairs={{0,64},{4,68},{8,72},{12,76},{16,80},{20,84},{24,88},{28,92},{32,9... | collective-permute-start | bytes 196616 | tf_op jit(solution)/shard_map/ppermute | solution.py:384
  33.2 1.1 %collective-permute-start.7 = (f32[16,1024]{1,0:T(8,128)S(1)}, f32[16,1024]{1,0:T(8,128)S(1)}, u32[]{:S(2)}, u32[]{:S(2)}) collective-permute-start(f32[16,1024]{1,0:T(8,128)S(1)} %get-tuple-element.63), channel_id=1, source_target_pairs={{0,96},{4,100},{8,104},{12,108},{16,112},{20,116},{24,120},{28,124... | collective-permute-start | bytes 196616 | tf_op jit(solution)/shard_map/ppermute | solution.py:384
  34.3 1.9 %collective-permute-done.6.refs_3_ = f32[16,1024]{1,0:T(8,128)S(1)} collective-permute-done((f32[16,1024]{1,0:T(8,128)S(1)}, f32[16,1024]{1,0:T(8,128)S(1)}, u32[]{:S(2)}, u32[]{:S(2)}) %collective-permute-start.6) | collective-permute-done | bytes 65568 | tf_op jit(solution)/shard_map/ppermute | solution.py:384
  36.2 0.5 collective-permute-done.7.refs_4_
  36.6 0.1 column.1
  36.7 2.4 %collective-permute-start.8 = (f32[32,1024]{1,0:T(8,128)S(1)}, f32[32,1024]{1,0:T(8,128)S(1)}, u32[]{:S(2)}, u32[]{:S(2)}) collective-permute-start(f32[32,1024]{1,0:T(8,128)S(1)} %get-tuple-element.65), channel_id=1, source_target_pairs={{0,8},{4,12},{8,16},{12,20},{16,24},{20,28},{24,0},{28,4},{32,40},... | collective-permute-start | bytes 393224 | tf_op jit(solution)/shard_map/ppermute | solution.py:384
  39.1 0.6 collective-permute-start.10
  39.8 2.9 %collective-permute-done.8.refs_3_ = f32[32,1024]{1,0:T(8,128)S(1)} collective-permute-done((f32[32,1024]{1,0:T(8,128)S(1)}, f32[32,1024]{1,0:T(8,128)S(1)}, u32[]{:S(2)}, u32[]{:S(2)}) %collective-permute-start.8) | collective-permute-done | bytes 131104 | tf_op jit(solution)/shard_map/ppermute | solution.py:384
  42.6 1.9 %collective-permute-done.9.refs_4_ = f32[32,1024]{1,0:T(8,128)S(1)} collective-permute-done((f32[32,1024]{1,0:T(8,128)S(1)}, f32[32,1024]{1,0:T(8,128)S(1)}, u32[]{:S(2)}, u32[]{:S(2)}) %collective-permute-start.9) | collective-permute-done | bytes 131104 | tf_op jit(solution)/shard_map/ppermute | solution.py:384
  44.5 1.0 %collective-permute-done.10.refs_5_ = f32[32,1024]{1,0:T(8,128)S(1)} collective-permute-done((f32[32,1024]{1,0:T(8,128)S(1)}, f32[32,1024]{1,0:T(8,128)S(1)}, u32[]{:S(2)}, u32[]{:S(2)}) %collective-permute-start.10) | collective-permute-done | bytes 131104 | tf_op jit(solution)/shard_map/ppermute | solution.py:384
  45.6 0.1 row.1
  45.6 0.6 copy-done.2
  46.3 3.5 %collective-permute-start.11 = (f32[32,1024]{1,0:T(8,128)S(1)}, f32[32,1024]{1,0:T(8,128)S(1)}, u32[]{:S(2)}, u32[]{:S(2)}) collective-permute-start(f32[32,1024]{1,0:T(8,128)S(1)} %get-tuple-element.69), channel_id=1, source_target_pairs={{0,4},{4,0},{8,12},{12,8},{16,20},{20,16},{24,28},{28,24},{32,36},... | collective-permute-start | bytes 393224 | tf_op jit(solution)/shard_map/ppermute | solution.py:384
  49.8 1.0 %collective-permute-done.11.other_ref = f32[32,1024]{1,0:T(8,128)S(1)} collective-permute-done((f32[32,1024]{1,0:T(8,128)S(1)}, f32[32,1024]{1,0:T(8,128)S(1)}, u32[]{:S(2)}, u32[]{:S(2)}) %collective-permute-start.11) | collective-permute-done | bytes 131104 | tf_op jit(solution)/shard_map/ppermute | solution.py:384
  50.8 0.7 copy-done.4
  51.4 17.1 %main.1 = (f32[256,2048]{1,0:T(8,128)}, bf16[3,256,2048]{2,1,0:T(8,128)(2,1)}, bf16[32,2048]{1,0:T(8,128)(2,1)}, bf16[2,48,1024]{2,1,0:T(8,128)(2,1)}) custom-call(s32[1]{0:T(128)} %bitcast.refs_0_.place_ref, bf16[3,256,2048]{2,1,0:T(8,128)(2,1)} %get-tuple-element.55.feat_ref, bf16[256,2048]{1,0:T(8,128)(2,1)} %get-tuple-element.56.cotp_ref, ...), custom_call_target="tpu_custom_call" | custom-call | tf_op jit(solution)/shard_map/main/pallas_call | solution.py:487
  68.5 0.4 collective-permute-start.12
  69.0 2.0 %collective-permute-start.16 = (bf16[32,2048]{1,0:T(8,128)(2,1)}, bf16[32,2048]{1,0:T(8,128)(2,1)S(1)}, u32[]{:S(2)}, u32[]{:S(2)}) collective-permute-start(bf16[32,2048]{1,0:T(8,128)(2,1)} %get-tuple-element.75), channel_id=1, source_target_pairs={{4,0},{8,4},{12,8},{16,12},{20,16},{24,20},{28,24},{32,28},{36,32}... | collective-permute-start | bytes 393224 | tf_op jit(solution)/shard_map/ppermute | solution.py:390
  71.0 0.9 fusion
  71.9 0.1 collective-permute-start.15
  72.0 1.8 %collective-permute-start.14 = (bf16[48,1024]{1,0:T(8,128)(2,1)S(1)}, bf16[48,1024]{1,0:T(8,128)(2,1)S(1)}, u32[]{:S(2)}, u32[]{:S(2)}) collective-permute-start(bf16[48,1024]{1,0:T(8,128)(2,1)S(1)} %fusion), channel_id=1, source_target_pairs={{0,16},{4,20},{8,24},{12,28},{16,0},{20,4},{24,8},{28,12},{32,48},... | collective-permute-start | bytes 294920 | tf_op jit(solution)/shard_map/ppermute | solution.py:384
  73.8 0.9 collective-permute-start.13
  74.7 4.7 %collective-permute-done.16.halo_ref = bf16[32,2048]{1,0:T(8,128)(2,1)S(1)} collective-permute-done((bf16[32,2048]{1,0:T(8,128)(2,1)}, bf16[32,2048]{1,0:T(8,128)(2,1)S(1)}, u32[]{:S(2)}, u32[]{:S(2)}) %collective-permute-start.16) | collective-permute-done | bytes 131104 | tf_op jit(solution)/shard_map/ppermute | solution.py:390
  79.4 0.7 copy-done.3
  80.0 5.1 %outputs.2 = (bf16[256,2048]{1,0:T(8,128)(2,1)}, bf16[256,2048]{1,0:T(8,128)(2,1)}) custom-call(bf16[3,256,2048]{2,1,0:T(8,128)(2,1)} %get-tuple-element.55.feat_ref, f32[256,2048]{1,0:T(8,128)} %get-tuple-element.73.y_ref, bf16[3,256,2048]{2,1,0:T(8,128)(2,1)} %get-tuple-element.74.grads_ref, bf16[32,2048]{1,0:T(8,128)(2,1)} %copy-done.3, ...), custom_call_target="tpu_custom_call" | custom-call | tf_op jit(solution)/shard_map/outputs/pallas_call | solution.py:529
  85.2 0.1 add_convert_fusion.1
  85.2 0.1 collective-permute-start.19
  85.3 3.6 %collective-permute-start.18 = (bf16[48,1024]{1,0:T(8,128)(2,1)S(1)}, bf16[48,1024]{1,0:T(8,128)(2,1)S(1)}, u32[]{:S(2)}, u32[]{:S(2)}) collective-permute-start(bf16[48,1024]{1,0:T(8,128)(2,1)S(1)} %add_convert_fusion.1), channel_id=1, source_target_pairs={{0,64},{4,68},{8,72},{12,76},{16,80},{20,84},{24,88},{28,92},{32,9... | collective-permute-start | bytes 294920 | tf_op jit(solution)/shard_map/ppermute | solution.py:384
  88.9 5.1 %outputs.3 = (bf16[256,2048]{1,0:T(8,128)(2,1)}, bf16[256,2048]{1,0:T(8,128)(2,1)}) custom-call(bf16[3,256,2048]{2,1,0:T(8,128)(2,1)} %get-tuple-element.55.feat_ref, f32[256,2048]{1,0:T(8,128)} %get-tuple-element.73.y_ref, bf16[3,256,2048]{2,1,0:T(8,128)(2,1)} %get-tuple-element.74.grads_ref, ...), custom_call_target="tpu_custom_call", output_to_operand_aliasing={{0}: (6, {}), {1}: (7, {})} | custom-call | tf_op jit(solution)/shard_map/outputs/pallas_call | solution.py:529
  94.0 0.1 add_convert_fusion.mine_ref
  94.1 0.1 collective-permute-start.20
  94.2 1.3 %collective-permute-done.20.other_ref = bf16[48,1024]{1,0:T(8,128)(2,1)S(1)} collective-permute-done((bf16[48,1024]{1,0:T(8,128)(2,1)S(1)}, bf16[48,1024]{1,0:T(8,128)(2,1)S(1)}, u32[]{:S(2)}, u32[]{:S(2)}) %collective-permute-start.20) | collective-permute-done | bytes 98336 | tf_op jit(solution)/shard_map/ppermute | solution.py:384
  95.5 0.7 spread.1
  (29 shorter events, 0.2 us)
Async XLA Ops:
  0.6 6.1 %copy-start.8 = (s32[256]{0:T(256)S(1)}, s32[256]{0:T(256)}, u32[]{:S(2)}) copy-start(s32[256]{0:T(256)} %param.8) | copy-start | bytes 3076
  0.6 27.6 %copy-start = (f32[16,2048]{1,0:T(8,128)S(1)}, f32[16,2048]{1,0:T(8,128)}, u32[]{:S(2)}) copy-start(f32[16,2048]{1,0:T(8,128)} %rate_ref.3) | copy-start | bytes 393220
  2.3 12.1 %collective-permute-start.3 = (f32[8,128]{1,0:T(8,128)}, f32[8,128]{1,0:T(8,128)S(1)}, u32[]{:S(2)}, u32[]{:S(2)}) collective-permute-start(f32[8,128]{1,0:T(8,128)} %get-tuple-element.54.sum0_ref), channel_id=1, source_target_pairs={{0,3},{1,0},{2,1},{3,2},{4,7},{5,4},{6,5},{7,6},{8,11},{9,8},{10,9... | collective-permute-start | bytes 12296 | tf_op jit(solution)/shard_map/ppermute | solution.py:423
  6.1 8.3 %collective-permute-start.2 = (f32[8,128]{1,0:T(8,128)}, f32[8,128]{1,0:T(8,128)S(1)}, u32[]{:S(2)}, u32[]{:S(2)}) collective-permute-start(f32[8,128]{1,0:T(8,128)} %get-tuple-element.54.sum0_ref), channel_id=1, source_target_pairs={{0,2},{1,3},{2,0},{3,1},{4,6},{5,7},{6,4},{7,5},{8,10},{9,11},{10,... | collective-permute-start | bytes 12296 | tf_op jit(solution)/shard_map/ppermute | solution.py:423
  6.1 8.3 %collective-permute-start.1 = (f32[8,128]{1,0:T(8,128)}, f32[8,128]{1,0:T(8,128)S(1)}, u32[]{:S(2)}, u32[]{:S(2)}) collective-permute-start(f32[8,128]{1,0:T(8,128)} %get-tuple-element.54.sum0_ref), channel_id=1, source_target_pairs={{0,1},{1,2},{2,3},{3,0},{4,5},{5,6},{6,7},{7,4},{8,9},{9,10},{10,1... | collective-permute-start | bytes 12296 | tf_op jit(solution)/shard_map/ppermute | solution.py:423
  6.8 5.2 %collective-permute-start = (s32[6]{0:T(128)S(1)}, s32[6]{0:T(128)S(1)}, u32[]{:S(2)}, u32[]{:S(2)}) collective-permute-start(s32[6]{0:T(128)S(1)} %slice.3), channel_id=1, source_target_pairs={{0,4},{4,8},{8,12},{12,16},{16,20},{20,24},{24,28},{28,32},{32,36}... | collective-permute-start | bytes 80 | tf_op jit(solution)/shard_map/ppermute | solution.py:390
  14.4 0.6 copy-start.5
  14.4 0.6 copy-start.6
  14.4 0.6 copy-start.7
  25.6 2.6 %collective-permute-start.4 = (f32[2,32,1024]{2,1,0:T(8,128)}, f32[2,32,1024]{2,1,0:T(8,128)S(1)}, u32[]{:S(2)}, u32[]{:S(2)}) collective-permute-start(f32[2,32,1024]{2,1,0:T(8,128)} %get-tuple-element.58.refs_1_), channel_id=1, source_target_pairs={{0,4},{4,0},{8,12},{12,8},{16,20},{20,16},{24,28},{28,24},{32,36},... | collective-permute-start | bytes 786440 | tf_op jit(solution)/shard_map/ppermute | solution.py:384
  28.2 1.0 copy-start.1
  29.2 5.1 %collective-permute-start.5 = (f32[16,1024]{1,0:T(8,128)S(1)}, f32[16,1024]{1,0:T(8,128)S(1)}, u32[]{:S(2)}, u32[]{:S(2)}) collective-permute-start(f32[16,1024]{1,0:T(8,128)S(1)} %get-tuple-element.61), channel_id=1, source_target_pairs={{0,32},{4,36},{8,40},{12,44},{16,48},{20,52},{24,56},{28,60},{32,6... | collective-permute-start | bytes 196616 | tf_op jit(solution)/shard_map/ppermute | solution.py:384
  30.6 5.6 %collective-permute-start.6 = (f32[16,1024]{1,0:T(8,128)S(1)}, f32[16,1024]{1,0:T(8,128)S(1)}, u32[]{:S(2)}, u32[]{:S(2)}) collective-permute-start(f32[16,1024]{1,0:T(8,128)S(1)} %get-tuple-element.62), channel_id=1, source_target_pairs={{0,64},{4,68},{8,72},{12,76},{16,80},{20,84},{24,88},{28,92},{32,9... | collective-permute-start | bytes 196616 | tf_op jit(solution)/shard_map/ppermute | solution.py:384
  33.2 3.4 %collective-permute-start.7 = (f32[16,1024]{1,0:T(8,128)S(1)}, f32[16,1024]{1,0:T(8,128)S(1)}, u32[]{:S(2)}, u32[]{:S(2)}) collective-permute-start(f32[16,1024]{1,0:T(8,128)S(1)} %get-tuple-element.63), channel_id=1, source_target_pairs={{0,96},{4,100},{8,104},{12,108},{16,112},{20,116},{24,120},{28,124... | collective-permute-start | bytes 196616 | tf_op jit(solution)/shard_map/ppermute | solution.py:384
  36.7 5.9 %collective-permute-start.8 = (f32[32,1024]{1,0:T(8,128)S(1)}, f32[32,1024]{1,0:T(8,128)S(1)}, u32[]{:S(2)}, u32[]{:S(2)}) collective-permute-start(f32[32,1024]{1,0:T(8,128)S(1)} %get-tuple-element.65), channel_id=1, source_target_pairs={{0,8},{4,12},{8,16},{12,20},{16,24},{20,28},{24,0},{28,4},{32,40},... | collective-permute-start | bytes 393224 | tf_op jit(solution)/shard_map/ppermute | solution.py:384
  39.1 5.4 %collective-permute-start.9 = (f32[32,1024]{1,0:T(8,128)S(1)}, f32[32,1024]{1,0:T(8,128)S(1)}, u32[]{:S(2)}, u32[]{:S(2)}) collective-permute-start(f32[32,1024]{1,0:T(8,128)S(1)} %get-tuple-element.66), channel_id=1, source_target_pairs={{0,16},{4,20},{8,24},{12,28},{16,0},{20,4},{24,8},{28,12},{32,48},... | collective-permute-start | bytes 393224 | tf_op jit(solution)/shard_map/ppermute | solution.py:384
  39.1 6.4 %collective-permute-start.10 = (f32[32,1024]{1,0:T(8,128)S(1)}, f32[32,1024]{1,0:T(8,128)S(1)}, u32[]{:S(2)}, u32[]{:S(2)}) collective-permute-start(f32[32,1024]{1,0:T(8,128)S(1)} %get-tuple-element.67), channel_id=1, source_target_pairs={{0,24},{4,28},{8,0},{12,4},{16,8},{20,12},{24,16},{28,20},{32,56},... | collective-permute-start | bytes 393224 | tf_op jit(solution)/shard_map/ppermute | solution.py:384
  45.6 0.7 copy-start.2
  46.3 4.5 %collective-permute-start.11 = (f32[32,1024]{1,0:T(8,128)S(1)}, f32[32,1024]{1,0:T(8,128)S(1)}, u32[]{:S(2)}, u32[]{:S(2)}) collective-permute-start(f32[32,1024]{1,0:T(8,128)S(1)} %get-tuple-element.69), channel_id=1, source_target_pairs={{0,4},{4,0},{8,12},{12,8},{16,20},{20,16},{24,28},{28,24},{32,36},... | collective-permute-start | bytes 393224 | tf_op jit(solution)/shard_map/ppermute | solution.py:384
  50.8 0.7 copy-start.4
  68.5 2.5 %collective-permute-start.12 = (bf16[2,48,1024]{2,1,0:T(8,128)(2,1)}, bf16[2,48,1024]{2,1,0:T(8,128)(2,1)S(1)}, u32[]{:S(2)}, u32[]{:S(2)}) collective-permute-start(bf16[2,48,1024]{2,1,0:T(8,128)(2,1)} %get-tuple-element.72), channel_id=1, source_target_pairs={{0,4},{4,0},{8,12},{12,8},{16,20},{20,16},{24,28},{28,24},{32,36},... | collective-permute-start | bytes 589832 | tf_op jit(solution)/shard_map/ppermute | solution.py:384
  69.0 10.4 %collective-permute-start.16 = (bf16[32,2048]{1,0:T(8,128)(2,1)}, bf16[32,2048]{1,0:T(8,128)(2,1)S(1)}, u32[]{:S(2)}, u32[]{:S(2)}) collective-permute-start(bf16[32,2048]{1,0:T(8,128)(2,1)} %get-tuple-element.75), channel_id=1, source_target_pairs={{4,0},{8,4},{12,8},{16,12},{20,16},{24,20},{28,24},{32,28},{36,32}... | collective-permute-start | bytes 393224 | tf_op jit(solution)/shard_map/ppermute | solution.py:390
  71.9 13.2 %collective-permute-start.15 = (bf16[48,1024]{1,0:T(8,128)(2,1)S(1)}, bf16[48,1024]{1,0:T(8,128)(2,1)S(1)}, u32[]{:S(2)}, u32[]{:S(2)}) collective-permute-start(bf16[48,1024]{1,0:T(8,128)(2,1)S(1)} %fusion), channel_id=1, source_target_pairs={{0,24},{4,28},{8,0},{12,4},{16,8},{20,12},{24,16},{28,20},{32,56},... | collective-permute-start | bytes 294920 | tf_op jit(solution)/shard_map/ppermute | solution.py:384
  72.0 13.1 %collective-permute-start.14 = (bf16[48,1024]{1,0:T(8,128)(2,1)S(1)}, bf16[48,1024]{1,0:T(8,128)(2,1)S(1)}, u32[]{:S(2)}, u32[]{:S(2)}) collective-permute-start(bf16[48,1024]{1,0:T(8,128)(2,1)S(1)} %fusion), channel_id=1, source_target_pairs={{0,16},{4,20},{8,24},{12,28},{16,0},{20,4},{24,8},{28,12},{32,48},... | collective-permute-start | bytes 294920 | tf_op jit(solution)/shard_map/ppermute | solution.py:384
  73.8 11.3 %collective-permute-start.13 = (bf16[48,1024]{1,0:T(8,128)(2,1)S(1)}, bf16[48,1024]{1,0:T(8,128)(2,1)S(1)}, u32[]{:S(2)}, u32[]{:S(2)}) collective-permute-start(bf16[48,1024]{1,0:T(8,128)(2,1)S(1)} %fusion), channel_id=1, source_target_pairs={{0,8},{4,12},{8,16},{12,20},{16,24},{20,28},{24,0},{28,4},{32,40},... | collective-permute-start | bytes 294920 | tf_op jit(solution)/shard_map/ppermute | solution.py:384
  79.4 0.7 copy-start.3
  85.2 8.8 %collective-permute-start.19 = (bf16[48,1024]{1,0:T(8,128)(2,1)S(1)}, bf16[48,1024]{1,0:T(8,128)(2,1)S(1)}, u32[]{:S(2)}, u32[]{:S(2)}) collective-permute-start(bf16[48,1024]{1,0:T(8,128)(2,1)S(1)} %add_convert_fusion.1), channel_id=1, source_target_pairs={{0,96},{4,100},{8,104},{12,108},{16,112},{20,116},{24,120},{28,124... | collective-permute-start | bytes 294920 | tf_op jit(solution)/shard_map/ppermute | solution.py:384
  85.3 8.7 %collective-permute-start.18 = (bf16[48,1024]{1,0:T(8,128)(2,1)S(1)}, bf16[48,1024]{1,0:T(8,128)(2,1)S(1)}, u32[]{:S(2)}, u32[]{:S(2)}) collective-permute-start(bf16[48,1024]{1,0:T(8,128)(2,1)S(1)} %add_convert_fusion.1), channel_id=1, source_target_pairs={{0,64},{4,68},{8,72},{12,76},{16,80},{20,84},{24,88},{28,92},{32,9... | collective-permute-start | bytes 294920 | tf_op jit(solution)/shard_map/ppermute | solution.py:384
  88.9 5.1 %collective-permute-start.17 = (bf16[48,1024]{1,0:T(8,128)(2,1)S(1)}, bf16[48,1024]{1,0:T(8,128)(2,1)S(1)}, u32[]{:S(2)}, u32[]{:S(2)}) collective-permute-start(bf16[48,1024]{1,0:T(8,128)(2,1)S(1)} %add_convert_fusion.1), channel_id=1, source_target_pairs={{0,32},{4,36},{8,40},{12,44},{16,48},{20,52},{24,56},{28,60},{32,6... | collective-permute-start | bytes 294920 | tf_op jit(solution)/shard_map/ppermute | solution.py:384
  94.1 1.4 %collective-permute-start.20 = (bf16[48,1024]{1,0:T(8,128)(2,1)S(1)}, bf16[48,1024]{1,0:T(8,128)(2,1)S(1)}, u32[]{:S(2)}, u32[]{:S(2)}) collective-permute-start(bf16[48,1024]{1,0:T(8,128)(2,1)S(1)} %add_convert_fusion.mine_ref), channel_id=1, source_target_pairs={{0,4},{4,0},{8,12},{12,8},{16,20},{20,16},{24,28},{28,24},{32,36},... | collective-permute-start | bytes 294920 | tf_op jit(solution)/shard_map/ppermute | solution.py:384

commit v4 on v3

--- a/solution.py
+++ b/solution.py
@@ -1,5 +1,6 @@
 import jax
 import jax.numpy as jnp
+import numpy as np
 from jax import lax
 from jax.experimental import pallas as pl
 from jax.experimental.pallas import tpu as pltpu
@@ -15,6 +16,7 @@
 HALVES = 4
 WIDTH = HALVES * LANES
 PARAM_ROWS = 48
+RUN = 8
 f32 = jnp.float32
 bf16 = jnp.bfloat16
 
@@ -53,28 +55,25 @@
     squares_ref[...] = jnp.broadcast_to(summed, squares_ref.shape)
 
 
-def hot_kernel(tokens_ref, hot_ref, hot_t_ref, order_ref, order_t_ref):
-    length = order_ref.shape[0]
+def hot_kernel(previous_ref, tokens_ref, hot_ref, hot_t_ref):
+    length = tokens_ref.shape[1]
     steps = length // SEGS
-    margin = TAPS - 1
     letter = lax.broadcasted_iota(jnp.int32, (8, length), 0)
     value = jnp.full((8, length), -1, jnp.int32)
     for n, v in enumerate(LETTERS):
         value = jnp.where(letter == n, v, value)
-    tokens = tokens_ref[...]
+    tokens = jnp.concatenate([previous_ref[...], tokens_ref[...]], 1)
     pieces = []
     for i in range(TAPS):
-        seen = jnp.broadcast_to(tokens[:, margin - i : margin - i + length], (8, length))
+        seen = jnp.broadcast_to(tokens[:, length - i : 2 * length - i], (8, length))
         pieces.append(jnp.where(seen == value, 1.0, 0.0))
     pieces.append(jnp.zeros((8, length), f32))
     natural = jnp.concatenate(pieces, 0).astype(bf16)
     row = lax.broadcasted_iota(jnp.int32, (length, length), 0)
     col = lax.broadcasted_iota(jnp.int32, (length, length), 1)
     order = jnp.where((row % SEGS) * steps + row // SEGS == col, 1.0, 0.0).astype(bf16)
-    order_t = jnp.where((col % SEGS) * steps + col // SEGS == row, 1.0, 0.0).astype(bf16)
-    order_ref[...] = order
-    order_t_ref[...] = order_t
-    hot_t_ref[...] = jnp.dot(natural, order_t, preferred_element_type=f32).astype(bf16)
+    hot_t_ref[...] = lax.dot_general(
+        natural, order, (((1,), (1,)), ((), ())), preferred_element_type=f32).astype(bf16)
     double = jnp.concatenate([natural, natural], 0)
     hot_ref[...] = lax.dot_general(
         order, double, (((1,), (1,)), ((), ())), preferred_element_type=f32
@@ -84,7 +83,7 @@
 def states_kernel(
     hot_ref, order_ref, embed_ref, sum0_ref, sum1_ref, sum2_ref, sum3_ref, gain_ref,
     weight_ref, rate_ref, cot_ref,
-    feat_ref, cotp_ref, normed_ref, inner_ref, ends_ref, x_ref, g_ref,
+    feat_ref, cotp_ref, normed_ref, inner_ref, runs_ref, ends_ref, x_ref, g_ref,
 ):
     steps = x_ref.shape[1]
     squares = (sum0_ref[...] + sum1_ref[...]) + (sum2_ref[...] + sum3_ref[...])
@@ -120,13 +119,23 @@
             base = part * 8
             rates = [rows(rate_ref, base + n, h) for n in range(8)]
             decay = [jnp.exp(-p) for p in rates]
+            leap = [jnp.exp(p * (-float(RUN))) for p in rates]
             fwd = [jnp.zeros((SEGS, LANES), f32)] * 8
             bwd = fwd
-            for i in range(steps):
-                now = x_ref[h, i]
-                fwd = [d * s + now for d, s in zip(decay, fwd)]
-                now = g_ref[h, steps - 1 - i]
-                bwd = [d * s + now for d, s in zip(decay, bwd)]
+            runs = steps // RUN
+            for c in range(runs):
+                ahead = [x_ref[h, RUN * c]] * 8
+                back = [g_ref[h, steps - 1 - RUN * c]] * 8
+                for i in range(RUN * c + 1, RUN * c + RUN):
+                    now = x_ref[h, i]
+                    ahead = [d * s + now for d, s in zip(decay, ahead)]
+                    now = g_ref[h, steps - 1 - i]
+                    back = [d * s + now for d, s in zip(decay, back)]
+                for n in range(8):
+                    runs_ref[0, c, base + n, :, part_of(h)] = ahead[n]
+                    runs_ref[1, runs - 1 - c, base + n, :, part_of(h)] = back[n]
+                fwd = [e + d * s for e, d, s in zip(ahead, leap, fwd)]
+                bwd = [e + d * s for e, d, s in zip(back, leap, bwd)]
             for n in range(8):
                 inc, dec = fwd[n], bwd[n]
                 for hop in (1, 2, 4):
@@ -218,12 +227,14 @@
 
 
 def main_kernel(
-    place_ref, feat_ref, cotp_ref, inner_ref, mine_ref, other_ref, rate_ref, residue_ref,
-    skip_ref, hot_t_ref, normed_ref,
-    y_ref, grads_ref, first_ref, params_ref, m_ref, x_ref, g_ref, enter_ref, sums_ref,
+    place_ref, feat_ref, cotp_ref, inner_ref, runs_ref, mine_ref, other_ref, rate_ref,
+    residue_ref, skip_ref, hot_t_ref, normed_ref,
+    gated_ref, grads_ref, first_ref, params_ref,
+    y_ref, m_ref, x_ref, g_ref, enter_ref, sums_ref, wide_ref, cross_ref,
 ):
     length = y_ref.shape[0]
     steps = length // SEGS
+    runs = steps // RUN
     blocks = pl.num_programs(0)
     here = pl.program_id(0) // (blocks // 2) == place_ref[0] % 2
     enter_ref[...] = jnp.where(here, mine_ref[...], other_ref[...])
@@ -235,45 +246,69 @@
         glong = cotp_ref[:, at].astype(f32) * feat_ref[0, :, at].astype(f32)
         x_ref[...] = mixed.reshape(steps, SEGS, LANES)
         g_ref[...] = glong.reshape(steps, SEGS, LANES)
-        skip = jnp.broadcast_to(skip_ref[:, at], (SEGS, LANES))
-        total = jnp.zeros((SEGS, LANES), f32)
-        pieces = []
-        for part in range(2):
-            base = part * 8
-            rates = [rows(rate_ref, base + n, h) for n in range(8)]
-            decay = [jnp.exp(-p) for p in rates]
-            residue = [rows(residue_ref, base + n, h) for n in range(8)]
+        packed = jnp.exp(-rate_ref[:, at])
+        weight = residue_ref[:, at]
+        taps = []
+        for k in range(RUN):
+            tap = jnp.sum(weight, 0, keepdims=True)
+            taps.append(jnp.broadcast_to(tap if k else tap + skip_ref[:, at], (SEGS, LANES)))
+            weight = weight * packed
+        for n in range(POLES):
+            rate = rows(rate_ref, n, h)
+            wide_ref[0, n] = jnp.exp(-rate)
+            wide_ref[1, n] = jnp.exp(rate * (-float(RUN)))
+            wide_ref[2, n] = rows(residue_ref, n, h)
             for way in range(2):
                 gap = ((SEGS - 1.0 - seg) if way else seg) * (-float(steps))
-                src, dst = (g_ref, m_ref) if way else (x_ref, y_ref)
-                state = [
-                    inner_ref[way, base + n, :, at]
-                    + jnp.exp(rates[n] * gap)
-                    * enter_ref[POLES * way + base + n : POLES * way + base + n + 1, at]
-                    for n in range(8)
-                ]
-                acc = [jnp.zeros((SEGS, LANES), f32)] * 8
-                for k in range(steps):
-                    i = steps - 1 - k if way else k
-                    now = src[i]
-                    state = [d * s + now for d, s in zip(decay, state)]
-                    summed = tree([r * s for r, s in zip(residue, state)])
-                    spot = slice(SEGS * i, SEGS * i + SEGS)
-                    dst[spot, at] = summed + (dst[spot, at] if part else skip * now)
-                    if not way:
-                        other = g_ref[i]
-                        acc = [a + other * s for a, s in zip(acc, state)]
-                        if not part:
-                            total = total + other * now
-                if not way:
-                    pieces += [jnp.sum(a, 0, keepdims=True) for a in acc]
-        sums_ref[0:POLES, at] = jnp.concatenate(pieces, 0)
-        sums_ref[40:48, at] = jnp.concatenate(
-            [jnp.sum(total, 0, keepdims=True), jnp.zeros((7, LANES), f32)], 0
+                wide_ref[3 + way, n] = inner_ref[way, n, :, at] + jnp.exp(rate * gap) * rows(
+                    enter_ref, POLES * way + n, h
+                )
+        decay = [wide_ref[0, n] for n in range(POLES)]
+        for c in range(runs):
+            wave = []
+            for n in range(POLES):
+                state = wide_ref[3, n]
+                wave.append(wide_ref[2, n] * state)
+                cross = state * runs_ref[1, c, n, :, at]
+                cross_ref[n] = cross_ref[n] + cross if c else cross
+                wide_ref[3, n] = runs_ref[0, c, n, :, at] + wide_ref[1, n] * state
+            for k in range(RUN):
+                i = RUN * c + k
+                wave = [d * u for d, u in zip(decay, wave)]
+                near = [taps[j] * x_ref[i - j] for j in range(k + 1)]
+                y_ref[SEGS * i : SEGS * i + SEGS, at] = tree(wave + near)
+        for c in reversed(range(runs)):
+            wave = []
+            for n in range(POLES):
+                state = wide_ref[4, n]
+                wave.append(wide_ref[2, n] * state)
+                wide_ref[4, n] = runs_ref[1, c, n, :, at] + wide_ref[1, n] * state
+            for k in range(RUN):
+                i = RUN * c + RUN - 1 - k
+                wave = [d * u for d, u in zip(decay, wave)]
+                near = [taps[j] * g_ref[i + j] for j in range(k + 1)]
+                m_ref[SEGS * i : SEGS * i + SEGS, at] = tree(wave + near)
+        lags = [[] for _ in range(RUN)]
+        for c in range(runs):
+            xs = [x_ref[RUN * c + k] for k in range(RUN)]
+            gs = [g_ref[RUN * c + k] for k in range(RUN)]
+            for k in range(RUN):
+                lags[k].append(tree([gs[j] * xs[j - k] for j in range(k, RUN)]))
+            if c:
+                lags = [[tree(lag)] for lag in lags]
+        lags = [jnp.sum(lag[0], 0, keepdims=True) for lag in lags]
+        inside = jnp.zeros((POLES, LANES), f32)
+        for lag in reversed(lags):
+            inside = inside * packed + lag
+        across = jnp.concatenate(
+            [jnp.sum(cross_ref[n], 0, keepdims=True) for n in range(POLES)], 0
         )
+        sums_ref[0:POLES, at] = inside + packed * across
+        sums_ref[40:48, at] = jnp.concatenate([lags[0], jnp.zeros((7, LANES), f32)], 0)
 
     each_part(scan)
     long_conv = y_ref[...]
+    gated_ref[...] = (feat_ref[0].astype(f32) * long_conv).astype(bf16)
     grad_mixed = m_ref[...]
     grads = [
         (cotp_ref[...].astype(f32) * long_conv).astype(bf16),
@@ -300,11 +335,12 @@
 
 
 def output_kernel(
-    feat_ref, y_ref, grads_ref, halo_ref, weight_ref, order_t_ref, *rest
+    gated_ref, grads_ref, halo_ref, weight_ref, order_t_ref, *rest
 ):
     hyena_ref, out_ref, wide_ref, sum_ref, after_ref = rest[-5:]
-    hyena = (feat_ref[0].astype(f32) * y_ref[...]).astype(bf16)
-    hyena_ref[...] = jnp.dot(order_t_ref[...], hyena, preferred_element_type=f32).astype(bf16)
+    hyena_ref[...] = jnp.dot(
+        order_t_ref[...], gated_ref[...], preferred_element_type=f32
+    ).astype(bf16)
     after_ref[...] = halo_ref[...].astype(f32)
     steps = grads_ref.shape[1] // SEGS
     seg = lax.broadcasted_iota(jnp.int32, (SEGS, LANES), 0)
@@ -402,7 +438,6 @@
 ):
     length = token_ids.shape[0]
     channels = embedding.shape[1]
-    margin = TAPS - 1
     steps = length // SEGS
     count = channels // WIDTH
     grid = (count,)
@@ -418,23 +453,22 @@
         compiler_params=roomy(),
         name="embed",
     )(embedding)
-    leading = shifted(token_ids[length - margin :], 1)
+    tokens = token_ids[None]
+    previous = shifted(tokens, 1)
+    line = np.arange(length)
+    table = ((line % SEGS) * steps + line // SEGS)[:, None] == line[None, :]
+    order, order_t = jnp.asarray(table, bf16), jnp.asarray(table.T, bf16)
     sums = [squares] + [
         lax.ppermute(squares, "ch", [(i, (i + k) % 4) for i in range(4)]) for k in (1, 2, 3)
     ]
-    tail = jnp.zeros((LANES - margin,), jnp.int32)
-    tokens = jnp.concatenate([leading, token_ids, tail])[None]
-    hot, hot_t, order, order_t = pl.pallas_call(
+    hot, hot_t = pl.pallas_call(
         hot_kernel,
-        out_shape=[
-            struct((length, 128), bf16), struct((64, length), bf16),
-            struct((length, length), bf16), struct((length, length), bf16),
-        ],
+        out_shape=[struct((length, 128), bf16), struct((64, length), bf16)],
         compiler_params=roomy(),
         name="hot",
-    )(tokens)
-
-    feats, cotp, normed, inner, ends = pl.pallas_call(
+    )(previous, tokens)
+
+    feats, cotp, normed, inner, runs, ends = pl.pallas_call(
         states_kernel,
         grid=grid,
         in_specs=[whole(length, 128), whole(length, length), lanes(8)]
@@ -442,11 +476,13 @@
         + [lanes(1), lanes(3, TAPS), lanes(POLES), lanes(length)],
         out_specs=[
             lanes(3, length), lanes(length), lanes(8), lanes(2, POLES, SEGS),
+            lanes(2, steps // RUN, POLES, SEGS),
             pl.BlockSpec((1, 2 * POLES, WIDTH), lambda b: (b // (count // 2), 0, b % (count // 2))),
         ],
         out_shape=[
             struct((3, length, channels), bf16), struct((length, channels), bf16),
             struct((8, channels), f32), struct((2, POLES, SEGS, channels), f32),
+            struct((2, steps // RUN, POLES, SEGS, channels), f32),
             struct((2, 2 * POLES, channels // 2), f32),
         ],
         scratch_shapes=[pltpu.VMEM((HALVES, steps, SEGS, LANES), f32)] * 2,
@@ -484,11 +520,12 @@
     )
     other = turn(sent, 0, 0, 1)
 
-    long_conv, grads, first, params = pl.pallas_call(
+    gated, grads, first, params = pl.pallas_call(
         main_kernel,
         grid=grid,
         in_specs=[
             smem, lanes(3, length), lanes(length), lanes(2, POLES, SEGS),
+            lanes(2, steps // RUN, POLES, SEGS),
             pl.BlockSpec((2 * POLES, WIDTH), lambda b: (0, b % (count // 2))),
             pl.BlockSpec((2 * POLES, WIDTH), lambda b: (0, b % (count // 2))),
             lanes(POLES), lanes(POLES), lanes(1), whole(64, length), lanes(8),
@@ -500,16 +537,17 @@
             ),
         ],
         out_shape=[
-            struct((length, channels), f32), struct((3, length, channels), bf16),
+            struct((length, channels), bf16), struct((3, length, channels), bf16),
             struct((32, channels), bf16), struct((2, PARAM_ROWS, half), bf16),
         ],
-        scratch_shapes=[pltpu.VMEM((length, WIDTH), f32)]
+        scratch_shapes=[pltpu.VMEM((length, WIDTH), f32)] * 2
         + [pltpu.VMEM((steps, SEGS, LANES), f32)] * 2
-        + [pltpu.VMEM((2 * POLES, WIDTH), f32), pltpu.VMEM((PARAM_ROWS, WIDTH), f32)],
+        + [pltpu.VMEM((2 * POLES, WIDTH), f32), pltpu.VMEM((PARAM_ROWS, WIDTH), f32)]
+        + [pltpu.VMEM((5, POLES, SEGS, LANES), f32), pltpu.VMEM((POLES, SEGS, LANES), f32)],
         compiler_params=roomy(60),
         name="main",
     )(
-        place, feats, cotp, inner, mine, other, pole_rates, residues, skip_gain[None], hot_t,
+        place, feats, cotp, inner, runs, mine, other, pole_rates, residues, skip_gain[None], hot_t,
         normed,
     )
 
@@ -530,7 +568,7 @@
             output_kernel,
             grid=(half_grid,),
             in_specs=[
-                spot(1, length), spot(length), spot(3, length), spot(32), spot(3, TAPS),
+                spot(length), spot(3, length), spot(32), spot(3, TAPS),
                 whole(length, length), *anywhere,
             ],
             out_specs=[spot(length), spot(length)],
@@ -539,10 +577,10 @@
                 pltpu.VMEM((3, steps, SEGS, LANES), f32), pltpu.VMEM((length, WIDTH), f32),
                 pltpu.VMEM((32, WIDTH), f32),
             ],
-            input_output_aliases={6: 0, 7: 1} if previous else {},
+            input_output_aliases={5: 0, 6: 1} if previous else {},
             compiler_params=roomy(),
             name="outputs",
-        )(feats, long_conv, grads, after, conv_weight, order_t, *previous)
+        )(gated, grads, after, conv_weight, order_t, *previous)
 
     hyena, grad_input = outputs(0)
     *near, hyena, grad_input = lax.optimization_barrier((*near, hyena, grad_input))

time: 96.8 us -> 96 us (level)
  Pallas kernels: 42.2 us -> 41.1 us
    ppermute x16, starting transfers between devices: 19.7 us -> 17.6 us  [turn(): return lax.ppermute(block, 'seq', route)]
    pallas_call x1, Pallas kernels: 17.1 us -> 15.8 us  [per_device(): pl.pallas_call(main_kernel, grid=grid, in_specs=[smem, lanes(3, length),...]
    ppermute x3, starting transfers between devices: 4.46 us -> 5.67 us  [per_device(): lax.ppermute(squares, 'ch', [(i, (i + k) % 4) for i in range(4)])]
  transfers between devices with their start and end apart: 21 -> 21, of which waited for: 10 -> 9; matrix products, arithmetic and copies ran while one was open for 2% -> 1% of each run, Pallas kernels for 12% -> 12%
where the time goes in v4:
time: 96 us; the launch traced here: 94.5 us
  Pallas kernels  41.1 us (43%)
  starting transfers between devices  29.8 us (31%)
  waiting for transfers between devices  17.7 us (18%)
  local copies, waits for them, and re-layouts  4.06 us (4%)
  other arithmetic  1.04 us (1%)
    ppermute x16, starting transfers between devices, turn(): return lax.ppermute(block, 'seq', route)  17.6 us
    pallas_call x1, Pallas kernels, per_device(): pl.pallas_call(main_kernel, grid=grid, in_specs=[smem, lanes(3, length),...  15.8 us
    ppermute x16, waiting for transfers between devices, turn(): return lax.ppermute(block, 'seq', route)  11.8 us
    pallas_call x1, Pallas kernels, per_device(): pl.pallas_call(states_kernel, grid=grid, in_specs=[whole(length, 128), wh...  11.1 us
    pallas_call x2, Pallas kernels, outputs(): pl.pallas_call(output_kernel, grid=(half_grid,), in_specs=[spot(length),...  9.99 us
    ppermute x2, starting transfers between devices, shifted(): return lax.ppermute(block, 'seq', route)  6.55 us
    ppermute x2, waiting for transfers between devices, shifted(): return lax.ppermute(block, 'seq', route)  5.88 us
    ppermute x3, starting transfers between devices, per_device(): lax.ppermute(squares, 'ch', [(i, (i + k) % 4) for i in range(4)])  5.67 us
  transfers between devices with their start and end apart: 21, of which 9 were waited for; matrix products, arithmetic and copies ran while one was open for 1% of the time, Pallas kernels for 12%

profile of v4, /device:TPU:7, one launch (start us, length us, event | category | flops | bytes accessed | tf_op | source)
XLA Modules:
  0.0 94.5 jit_solution(13102579212632532486)
XLA Ops:
  0.6 1.6 %embed.1 = (f32[8,2048]{1,0:T(8,128)}, f32[8,128]{1,0:T(8,128)}) custom-call(bf16[512,2048]{1,0:T(8,128)(2,1)} %table_ref.1), custom_call_target="tpu_custom_call" | custom-call | tf_op jit(solution)/shard_map/embed/pallas_call | solution.py:447
  2.3 1.6 %collective-permute-start.1 = (f32[8,128]{1,0:T(8,128)}, f32[8,128]{1,0:T(8,128)S(1)}, u32[]{:S(2)}, u32[]{:S(2)}) collective-permute-start(f32[8,128]{1,0:T(8,128)} %get-tuple-element.52.sum0_ref), channel_id=1, source_target_pairs={{0,1},{1,2},{2,3},{3,0},{4,5},{5,6},{6,7},{7,4},{8,9},{9,10},{10,1... | collective-permute-start | bytes 12296 | tf_op jit(solution)/shard_map/ppermute | solution.py:462
  3.9 3.3 %collective-permute-start.2 = (f32[8,128]{1,0:T(8,128)}, f32[8,128]{1,0:T(8,128)S(1)}, u32[]{:S(2)}, u32[]{:S(2)}) collective-permute-start(f32[8,128]{1,0:T(8,128)} %get-tuple-element.52.sum0_ref), channel_id=1, source_target_pairs={{0,2},{1,3},{2,0},{3,1},{4,6},{5,7},{6,4},{7,5},{8,10},{9,11},{10,... | collective-permute-start | bytes 12296 | tf_op jit(solution)/shard_map/ppermute | solution.py:462
  7.2 0.7 collective-permute-start.3
  8.0 4.5 %collective-permute-start = (s32[1,256]{1,0:T(1,128)}, s32[1,256]{1,0:T(1,128)S(1)}, u32[]{:S(2)}, u32[]{:S(2)}) collective-permute-start(s32[1,256]{1,0:T(1,128)} %bitcast.10), channel_id=1, source_target_pairs={{0,4},{4,8},{8,12},{12,16},{16,20},{20,24},{24,28},{28,32},{32,36}... | collective-permute-start | bytes 3080 | tf_op jit(solution)/shard_map/ppermute | solution.py:426
  12.5 0.9 collective-permute-done.previous_ref
  13.4 0.6 copy-done.8
  14.0 1.6 %hot.1 = (bf16[256,128]{1,0:T(8,128)(2,1)}, bf16[64,256]{1,0:T(8,128)(2,1)}) custom-call(s32[1,256]{1,0:T(1,128)} %copy-done.8, s32[1,256]{1,0:T(1,128)} %bitcast.11), custom_call_target="tpu_custom_call" | custom-call | tf_op jit(solution)/shard_map/hot/pallas_call | solution.py:464
  15.6 0.6 copy-done.5
  16.2 11.1 %states.1 = (bf16[3,256,2048]{2,1,0:T(8,128)(2,1)}, bf16[256,2048]{1,0:T(8,128)(2,1)}, f32[8,2048]{1,0:T(8,128)}, f32[2,16,8,2048]{3,2,1,0:T(8,128)}, f32[2,4,16...) custom-call(bf16[256,128]{1,0:T(8,128)(2,1)} %get-tuple-element.50.hot_ref, bf16[256,256]{1,0:T(8,128)(2,1)} %constant.29.clone.order_ref, ...), custom_call_target="tpu_custom_call" | custom-call | tf_op jit(solution)/shard_map/states/pallas_call | solution.py:471
  27.3 1.2 %collective-permute-start.4 = (f32[2,32,1024]{2,1,0:T(8,128)}, f32[2,32,1024]{2,1,0:T(8,128)S(1)}, u32[]{:S(2)}, u32[]{:S(2)}) collective-permute-start(f32[2,32,1024]{2,1,0:T(8,128)} %get-tuple-element.57.refs_1_), channel_id=1, source_target_pairs={{0,4},{4,0},{8,12},{12,8},{16,20},{20,16},{24,28},{28,24},{32,36},... | collective-permute-start | bytes 786440 | tf_op jit(solution)/shard_map/ppermute | solution.py:420
  28.5 1.4 %collective-permute-done.4.refs_2_ = f32[2,32,1024]{2,1,0:T(8,128)S(1)} collective-permute-done((f32[2,32,1024]{2,1,0:T(8,128)}, f32[2,32,1024]{2,1,0:T(8,128)S(1)}, u32[]{:S(2)}, u32[]{:S(2)}) %collective-permute-start.4) | collective-permute-done | bytes 262176 | tf_op jit(solution)/shard_map/ppermute | solution.py:420
  29.9 0.9 %copy-done.1 = f32[2,32,1024]{2,1,0:T(8,128)S(1)} copy-done((f32[2,32,1024]{2,1,0:T(8,128)S(1)}, f32[2,32,1024]{2,1,0:T(8,128)}, u32[]{:S(2)}) %copy-start.1) | copy-done | bytes 262168
  30.9 1.4 %collective-permute-start.5 = (f32[16,1024]{1,0:T(8,128)S(1)}, f32[16,1024]{1,0:T(8,128)S(1)}, u32[]{:S(2)}, u32[]{:S(2)}) collective-permute-start(f32[16,1024]{1,0:T(8,128)S(1)} %get-tuple-element.60), channel_id=1, source_target_pairs={{0,32},{4,36},{8,40},{12,44},{16,48},{20,52},{24,56},{28,60},{32,6... | collective-permute-start | bytes 196616 | tf_op jit(solution)/shard_map/ppermute | solution.py:420
  32.3 2.6 %collective-permute-start.6 = (f32[16,1024]{1,0:T(8,128)S(1)}, f32[16,1024]{1,0:T(8,128)S(1)}, u32[]{:S(2)}, u32[]{:S(2)}) collective-permute-start(f32[16,1024]{1,0:T(8,128)S(1)} %get-tuple-element.61), channel_id=1, source_target_pairs={{0,64},{4,68},{8,72},{12,76},{16,80},{20,84},{24,88},{28,92},{32,9... | collective-permute-start | bytes 196616 | tf_op jit(solution)/shard_map/ppermute | solution.py:420
  34.9 1.1 %collective-permute-start.7 = (f32[16,1024]{1,0:T(8,128)S(1)}, f32[16,1024]{1,0:T(8,128)S(1)}, u32[]{:S(2)}, u32[]{:S(2)}) collective-permute-start(f32[16,1024]{1,0:T(8,128)S(1)} %get-tuple-element.62), channel_id=1, source_target_pairs={{0,96},{4,100},{8,104},{12,108},{16,112},{20,116},{24,120},{28,124... | collective-permute-start | bytes 196616 | tf_op jit(solution)/shard_map/ppermute | solution.py:420
  36.0 1.9 %collective-permute-done.6.refs_3_ = f32[16,1024]{1,0:T(8,128)S(1)} collective-permute-done((f32[16,1024]{1,0:T(8,128)S(1)}, f32[16,1024]{1,0:T(8,128)S(1)}, u32[]{:S(2)}, u32[]{:S(2)}) %collective-permute-start.6) | collective-permute-done | bytes 65568 | tf_op jit(solution)/shard_map/ppermute | solution.py:420
  37.8 0.5 collective-permute-done.7.refs_4_
  38.3 0.1 column.1
  38.4 0.6 collective-permute-start.10
  39.0 2.1 %collective-permute-start.8 = (f32[32,1024]{1,0:T(8,128)S(1)}, f32[32,1024]{1,0:T(8,128)S(1)}, u32[]{:S(2)}, u32[]{:S(2)}) collective-permute-start(f32[32,1024]{1,0:T(8,128)S(1)} %get-tuple-element.64), channel_id=1, source_target_pairs={{0,8},{4,12},{8,16},{12,20},{16,24},{20,28},{24,0},{28,4},{32,40},... | collective-permute-start | bytes 393224 | tf_op jit(solution)/shard_map/ppermute | solution.py:420
  41.1 0.8 collective-permute-start.9
  42.0 1.5 %collective-permute-done.10.refs_5_ = f32[32,1024]{1,0:T(8,128)S(1)} collective-permute-done((f32[32,1024]{1,0:T(8,128)S(1)}, f32[32,1024]{1,0:T(8,128)S(1)}, u32[]{:S(2)}, u32[]{:S(2)}) %collective-permute-start.10) | collective-permute-done | bytes 131104 | tf_op jit(solution)/shard_map/ppermute | solution.py:420
  43.5 4.3 %collective-permute-done.9.refs_4_ = f32[32,1024]{1,0:T(8,128)S(1)} collective-permute-done((f32[32,1024]{1,0:T(8,128)S(1)}, f32[32,1024]{1,0:T(8,128)S(1)}, u32[]{:S(2)}, u32[]{:S(2)}) %collective-permute-start.9) | collective-permute-done | bytes 131104 | tf_op jit(solution)/shard_map/ppermute | solution.py:420
  47.8 0.1 row.1
  47.9 0.6 copy-done.2
  48.5 2.2 %collective-permute-start.11 = (f32[32,1024]{1,0:T(8,128)S(1)}, f32[32,1024]{1,0:T(8,128)S(1)}, u32[]{:S(2)}, u32[]{:S(2)}) collective-permute-start(f32[32,1024]{1,0:T(8,128)S(1)} %get-tuple-element.68), channel_id=1, source_target_pairs={{0,4},{4,0},{8,12},{12,8},{16,20},{20,16},{24,28},{28,24},{32,36},... | collective-permute-start | bytes 393224 | tf_op jit(solution)/shard_map/ppermute | solution.py:420
  50.7 1.0 %collective-permute-done.11.other_ref = f32[32,1024]{1,0:T(8,128)S(1)} collective-permute-done((f32[32,1024]{1,0:T(8,128)S(1)}, f32[32,1024]{1,0:T(8,128)S(1)}, u32[]{:S(2)}, u32[]{:S(2)}) %collective-permute-start.11) | collective-permute-done | bytes 131104 | tf_op jit(solution)/shard_map/ppermute | solution.py:420
  51.7 0.7 copy-done.4
  52.3 15.8 %main.1 = (bf16[256,2048]{1,0:T(8,128)(2,1)}, bf16[3,256,2048]{2,1,0:T(8,128)(2,1)}, bf16[32,2048]{1,0:T(8,128)(2,1)}, bf16[2,48,1024]{2,1,0:T(8,128)(2,1)}) custom-call(s32[1]{0:T(128)} %bitcast.refs_0_.place_ref, bf16[3,256,2048]{2,1,0:T(8,128)(2,1)} %get-tuple-element.53.feat_ref, bf16[256,2048]{1,0:T(8,128)(2,1)} %get-tuple-element.54.cotp_ref, ...), custom_call_target="tpu_custom_call" | custom-call | tf_op jit(solution)/shard_map/main/pallas_call | solution.py:523
  68.1 0.4 collective-permute-start.12
  68.6 2.0 %collective-permute-start.16 = (bf16[32,2048]{1,0:T(8,128)(2,1)}, bf16[32,2048]{1,0:T(8,128)(2,1)S(1)}, u32[]{:S(2)}, u32[]{:S(2)}) collective-permute-start(bf16[32,2048]{1,0:T(8,128)(2,1)} %get-tuple-element.74), channel_id=1, source_target_pairs={{4,0},{8,4},{12,8},{16,12},{20,16},{24,20},{28,24},{32,28},{36,32}... | collective-permute-start | bytes 393224 | tf_op jit(solution)/shard_map/ppermute | solution.py:426
  70.6 0.9 fusion
  71.6 1.6 %collective-permute-start.13 = (bf16[48,1024]{1,0:T(8,128)(2,1)S(1)}, bf16[48,1024]{1,0:T(8,128)(2,1)S(1)}, u32[]{:S(2)}, u32[]{:S(2)}) collective-permute-start(bf16[48,1024]{1,0:T(8,128)(2,1)S(1)} %fusion), channel_id=1, source_target_pairs={{0,8},{4,12},{8,16},{12,20},{16,24},{20,28},{24,0},{28,4},{32,40},... | collective-permute-start | bytes 294920 | tf_op jit(solution)/shard_map/ppermute | solution.py:420
  73.2 0.4 collective-permute-start.14
  73.6 0.3 collective-permute-start.15
  73.9 5.0 %collective-permute-done.16.halo_ref = bf16[32,2048]{1,0:T(8,128)(2,1)S(1)} collective-permute-done((bf16[32,2048]{1,0:T(8,128)(2,1)}, bf16[32,2048]{1,0:T(8,128)(2,1)S(1)}, u32[]{:S(2)}, u32[]{:S(2)}) %collective-permute-start.16) | collective-permute-done | bytes 131104 | tf_op jit(solution)/shard_map/ppermute | solution.py:426
  78.8 0.7 copy-done.3
  79.5 5.0 %outputs.2 = (bf16[256,2048]{1,0:T(8,128)(2,1)}, bf16[256,2048]{1,0:T(8,128)(2,1)}) custom-call(bf16[256,2048]{1,0:T(8,128)(2,1)} %get-tuple-element.72.gated_ref, bf16[3,256,2048]{2,1,0:T(8,128)(2,1)} %get-tuple-element.73.grads_ref, bf16[32,2048]{1,0:T(8,128)(2,1)} %copy-done.3, f32[3,7,2048]{2,1,0:T(8,128)} %weight_ref.5, ...), custom_call_target="tpu_custom_call" | custom-call | tf_op jit(solution)/shard_map/outputs/pallas_call | solution.py:567
  84.5 0.1 add_convert_fusion.1
  84.6 0.1 collective-permute-start.17
  84.7 0.1 collective-permute-start.18
  84.8 2.6 %collective-permute-start.19 = (bf16[48,1024]{1,0:T(8,128)(2,1)S(1)}, bf16[48,1024]{1,0:T(8,128)(2,1)S(1)}, u32[]{:S(2)}, u32[]{:S(2)}) collective-permute-start(bf16[48,1024]{1,0:T(8,128)(2,1)S(1)} %add_convert_fusion.1), channel_id=1, source_target_pairs={{0,96},{4,100},{8,104},{12,108},{16,112},{20,116},{24,120},{28,124... | collective-permute-start | bytes 294920 | tf_op jit(solution)/shard_map/ppermute | solution.py:420
  87.3 5.0 %outputs.3 = (bf16[256,2048]{1,0:T(8,128)(2,1)}, bf16[256,2048]{1,0:T(8,128)(2,1)}) custom-call(bf16[256,2048]{1,0:T(8,128)(2,1)} %get-tuple-element.72.gated_ref, bf16[3,256,2048]{2,1,0:T(8,128)(2,1)} %get-tuple-element.73.grads_ref, bf16[32,2048]{1,0:T(8,128)(2,1)} %copy-done.3, ...), custom_call_target="tpu_custom_call", output_to_operand_aliasing={{0}: (5, {}), {1}: (6, {})} | custom-call | tf_op jit(solution)/shard_map/outputs/pallas_call | solution.py:567
  92.4 0.1 add_convert_fusion.mine_ref
  92.4 0.1 collective-permute-start.20
  92.5 1.3 %collective-permute-done.20.other_ref = bf16[48,1024]{1,0:T(8,128)(2,1)S(1)} collective-permute-done((bf16[48,1024]{1,0:T(8,128)(2,1)S(1)}, bf16[48,1024]{1,0:T(8,128)(2,1)S(1)}, u32[]{:S(2)}, u32[]{:S(2)}) %collective-permute-start.20) | collective-permute-done | bytes 98336 | tf_op jit(solution)/shard_map/ppermute | solution.py:420
  93.8 0.7 spread.1
  (25 shorter events, 0.1 us)
Async XLA Ops:
  0.6 29.3 %copy-start = (f32[16,2048]{1,0:T(8,128)S(1)}, f32[16,2048]{1,0:T(8,128)}, u32[]{:S(2)}) copy-start(f32[16,2048]{1,0:T(8,128)} %rate_ref.3) | copy-start | bytes 393220
  2.3 13.3 %collective-permute-start.1 = (f32[8,128]{1,0:T(8,128)}, f32[8,128]{1,0:T(8,128)S(1)}, u32[]{:S(2)}, u32[]{:S(2)}) collective-permute-start(f32[8,128]{1,0:T(8,128)} %get-tuple-element.52.sum0_ref), channel_id=1, source_target_pairs={{0,1},{1,2},{2,3},{3,0},{4,5},{5,6},{6,7},{7,4},{8,9},{9,10},{10,1... | collective-permute-start | bytes 12296 | tf_op jit(solution)/shard_map/ppermute | solution.py:462
  3.9 11.7 %collective-permute-start.2 = (f32[8,128]{1,0:T(8,128)}, f32[8,128]{1,0:T(8,128)S(1)}, u32[]{:S(2)}, u32[]{:S(2)}) collective-permute-start(f32[8,128]{1,0:T(8,128)} %get-tuple-element.52.sum0_ref), channel_id=1, source_target_pairs={{0,2},{1,3},{2,0},{3,1},{4,6},{5,7},{6,4},{7,5},{8,10},{9,11},{10,... | collective-permute-start | bytes 12296 | tf_op jit(solution)/shard_map/ppermute | solution.py:462
  7.2 8.4 %collective-permute-start.3 = (f32[8,128]{1,0:T(8,128)}, f32[8,128]{1,0:T(8,128)S(1)}, u32[]{:S(2)}, u32[]{:S(2)}) collective-permute-start(f32[8,128]{1,0:T(8,128)} %get-tuple-element.52.sum0_ref), channel_id=1, source_target_pairs={{0,3},{1,0},{2,1},{3,2},{4,7},{5,4},{6,5},{7,6},{8,11},{9,8},{10,9... | collective-permute-start | bytes 12296 | tf_op jit(solution)/shard_map/ppermute | solution.py:462
  8.0 5.4 %collective-permute-start = (s32[1,256]{1,0:T(1,128)}, s32[1,256]{1,0:T(1,128)S(1)}, u32[]{:S(2)}, u32[]{:S(2)}) collective-permute-start(s32[1,256]{1,0:T(1,128)} %bitcast.10), channel_id=1, source_target_pairs={{0,4},{4,8},{8,12},{12,16},{16,20},{20,24},{24,28},{28,32},{32,36}... | collective-permute-start | bytes 3080 | tf_op jit(solution)/shard_map/ppermute | solution.py:426
  13.4 0.6 copy-start.8
  15.6 0.6 copy-start.5
  15.6 0.6 copy-start.6
  15.6 0.6 copy-start.7
  27.3 2.6 %collective-permute-start.4 = (f32[2,32,1024]{2,1,0:T(8,128)}, f32[2,32,1024]{2,1,0:T(8,128)S(1)}, u32[]{:S(2)}, u32[]{:S(2)}) collective-permute-start(f32[2,32,1024]{2,1,0:T(8,128)} %get-tuple-element.57.refs_1_), channel_id=1, source_target_pairs={{0,4},{4,0},{8,12},{12,8},{16,20},{20,16},{24,28},{28,24},{32,36},... | collective-permute-start | bytes 786440 | tf_op jit(solution)/shard_map/ppermute | solution.py:420
  29.9 1.0 %copy-start.1 = (f32[2,32,1024]{2,1,0:T(8,128)S(1)}, f32[2,32,1024]{2,1,0:T(8,128)}, u32[]{:S(2)}) copy-start(f32[2,32,1024]{2,1,0:T(8,128)} %get-tuple-element.57.refs_1_) | copy-start | bytes 786436
  30.9 5.1 %collective-permute-start.5 = (f32[16,1024]{1,0:T(8,128)S(1)}, f32[16,1024]{1,0:T(8,128)S(1)}, u32[]{:S(2)}, u32[]{:S(2)}) collective-permute-start(f32[16,1024]{1,0:T(8,128)S(1)} %get-tuple-element.60), channel_id=1, source_target_pairs={{0,32},{4,36},{8,40},{12,44},{16,48},{20,52},{24,56},{28,60},{32,6... | collective-permute-start | bytes 196616 | tf_op jit(solution)/shard_map/ppermute | solution.py:420
  32.3 5.6 %collective-permute-start.6 = (f32[16,1024]{1,0:T(8,128)S(1)}, f32[16,1024]{1,0:T(8,128)S(1)}, u32[]{:S(2)}, u32[]{:S(2)}) collective-permute-start(f32[16,1024]{1,0:T(8,128)S(1)} %get-tuple-element.61), channel_id=1, source_target_pairs={{0,64},{4,68},{8,72},{12,76},{16,80},{20,84},{24,88},{28,92},{32,9... | collective-permute-start | bytes 196616 | tf_op jit(solution)/shard_map/ppermute | solution.py:420
  34.9 3.4 %collective-permute-start.7 = (f32[16,1024]{1,0:T(8,128)S(1)}, f32[16,1024]{1,0:T(8,128)S(1)}, u32[]{:S(2)}, u32[]{:S(2)}) collective-permute-start(f32[16,1024]{1,0:T(8,128)S(1)} %get-tuple-element.62), channel_id=1, source_target_pairs={{0,96},{4,100},{8,104},{12,108},{16,112},{20,116},{24,120},{28,124... | collective-permute-start | bytes 196616 | tf_op jit(solution)/shard_map/ppermute | solution.py:420
  38.4 5.1 %collective-permute-start.10 = (f32[32,1024]{1,0:T(8,128)S(1)}, f32[32,1024]{1,0:T(8,128)S(1)}, u32[]{:S(2)}, u32[]{:S(2)}) collective-permute-start(f32[32,1024]{1,0:T(8,128)S(1)} %get-tuple-element.66), channel_id=1, source_target_pairs={{0,24},{4,28},{8,0},{12,4},{16,8},{20,12},{24,16},{28,20},{32,56},... | collective-permute-start | bytes 393224 | tf_op jit(solution)/shard_map/ppermute | solution.py:420
  39.0 4.5 %collective-permute-start.8 = (f32[32,1024]{1,0:T(8,128)S(1)}, f32[32,1024]{1,0:T(8,128)S(1)}, u32[]{:S(2)}, u32[]{:S(2)}) collective-permute-start(f32[32,1024]{1,0:T(8,128)S(1)} %get-tuple-element.64), channel_id=1, source_target_pairs={{0,8},{4,12},{8,16},{12,20},{16,24},{20,28},{24,0},{28,4},{32,40},... | collective-permute-start | bytes 393224 | tf_op jit(solution)/shard_map/ppermute | solution.py:420
  41.1 6.6 %collective-permute-start.9 = (f32[32,1024]{1,0:T(8,128)S(1)}, f32[32,1024]{1,0:T(8,128)S(1)}, u32[]{:S(2)}, u32[]{:S(2)}) collective-permute-start(f32[32,1024]{1,0:T(8,128)S(1)} %get-tuple-element.65), channel_id=1, source_target_pairs={{0,16},{4,20},{8,24},{12,28},{16,0},{20,4},{24,8},{28,12},{32,48},... | collective-permute-start | bytes 393224 | tf_op jit(solution)/shard_map/ppermute | solution.py:420
  47.9 0.7 copy-start.2
  48.5 3.2 %collective-permute-start.11 = (f32[32,1024]{1,0:T(8,128)S(1)}, f32[32,1024]{1,0:T(8,128)S(1)}, u32[]{:S(2)}, u32[]{:S(2)}) collective-permute-start(f32[32,1024]{1,0:T(8,128)S(1)} %get-tuple-element.68), channel_id=1, source_target_pairs={{0,4},{4,0},{8,12},{12,8},{16,20},{20,16},{24,28},{28,24},{32,36},... | collective-permute-start | bytes 393224 | tf_op jit(solution)/shard_map/ppermute | solution.py:420
  51.7 0.7 copy-start.4
  68.1 2.5 %collective-permute-start.12 = (bf16[2,48,1024]{2,1,0:T(8,128)(2,1)}, bf16[2,48,1024]{2,1,0:T(8,128)(2,1)S(1)}, u32[]{:S(2)}, u32[]{:S(2)}) collective-permute-start(bf16[2,48,1024]{2,1,0:T(8,128)(2,1)} %get-tuple-element.71), channel_id=1, source_target_pairs={{0,4},{4,0},{8,12},{12,8},{16,20},{20,16},{24,28},{28,24},{32,36},... | collective-permute-start | bytes 589832 | tf_op jit(solution)/shard_map/ppermute | solution.py:420
  68.6 10.3 %collective-permute-start.16 = (bf16[32,2048]{1,0:T(8,128)(2,1)}, bf16[32,2048]{1,0:T(8,128)(2,1)S(1)}, u32[]{:S(2)}, u32[]{:S(2)}) collective-permute-start(bf16[32,2048]{1,0:T(8,128)(2,1)} %get-tuple-element.74), channel_id=1, source_target_pairs={{4,0},{8,4},{12,8},{16,12},{20,16},{24,20},{28,24},{32,28},{36,32}... | collective-permute-start | bytes 393224 | tf_op jit(solution)/shard_map/ppermute | solution.py:426
  71.6 12.9 %collective-permute-start.13 = (bf16[48,1024]{1,0:T(8,128)(2,1)S(1)}, bf16[48,1024]{1,0:T(8,128)(2,1)S(1)}, u32[]{:S(2)}, u32[]{:S(2)}) collective-permute-start(bf16[48,1024]{1,0:T(8,128)(2,1)S(1)} %fusion), channel_id=1, source_target_pairs={{0,8},{4,12},{8,16},{12,20},{16,24},{20,28},{24,0},{28,4},{32,40},... | collective-permute-start | bytes 294920 | tf_op jit(solution)/shard_map/ppermute | solution.py:420
  73.2 11.3 %collective-permute-start.14 = (bf16[48,1024]{1,0:T(8,128)(2,1)S(1)}, bf16[48,1024]{1,0:T(8,128)(2,1)S(1)}, u32[]{:S(2)}, u32[]{:S(2)}) collective-permute-start(bf16[48,1024]{1,0:T(8,128)(2,1)S(1)} %fusion), channel_id=1, source_target_pairs={{0,16},{4,20},{8,24},{12,28},{16,0},{20,4},{24,8},{28,12},{32,48},... | collective-permute-start | bytes 294920 | tf_op jit(solution)/shard_map/ppermute | solution.py:420
  73.6 10.9 %collective-permute-start.15 = (bf16[48,1024]{1,0:T(8,128)(2,1)S(1)}, bf16[48,1024]{1,0:T(8,128)(2,1)S(1)}, u32[]{:S(2)}, u32[]{:S(2)}) collective-permute-start(bf16[48,1024]{1,0:T(8,128)(2,1)S(1)} %fusion), channel_id=1, source_target_pairs={{0,24},{4,28},{8,0},{12,4},{16,8},{20,12},{24,16},{28,20},{32,56},... | collective-permute-start | bytes 294920 | tf_op jit(solution)/shard_map/ppermute | solution.py:420
  78.8 0.7 copy-start.3
  84.6 7.7 %collective-permute-start.17 = (bf16[48,1024]{1,0:T(8,128)(2,1)S(1)}, bf16[48,1024]{1,0:T(8,128)(2,1)S(1)}, u32[]{:S(2)}, u32[]{:S(2)}) collective-permute-start(bf16[48,1024]{1,0:T(8,128)(2,1)S(1)} %add_convert_fusion.1), channel_id=1, source_target_pairs={{0,32},{4,36},{8,40},{12,44},{16,48},{20,52},{24,56},{28,60},{32,6... | collective-permute-start | bytes 294920 | tf_op jit(solution)/shard_map/ppermute | solution.py:420
  84.7 7.7 %collective-permute-start.18 = (bf16[48,1024]{1,0:T(8,128)(2,1)S(1)}, bf16[48,1024]{1,0:T(8,128)(2,1)S(1)}, u32[]{:S(2)}, u32[]{:S(2)}) collective-permute-start(bf16[48,1024]{1,0:T(8,128)(2,1)S(1)} %add_convert_fusion.1), channel_id=1, source_target_pairs={{0,64},{4,68},{8,72},{12,76},{16,80},{20,84},{24,88},{28,92},{32,9... | collective-permute-start | bytes 294920 | tf_op jit(solution)/shard_map/ppermute | solution.py:420
  84.8 7.6 %collective-permute-start.19 = (bf16[48,1024]{1,0:T(8,128)(2,1)S(1)}, bf16[48,1024]{1,0:T(8,128)(2,1)S(1)}, u32[]{:S(2)}, u32[]{:S(2)}) collective-permute-start(bf16[48,1024]{1,0:T(8,128)(2,1)S(1)} %add_convert_fusion.1), channel_id=1, source_target_pairs={{0,96},{4,100},{8,104},{12,108},{16,112},{20,116},{24,120},{28,124... | collective-permute-start | bytes 294920 | tf_op jit(solution)/shard_map/ppermute | solution.py:420
  92.4 1.4 %collective-permute-start.20 = (bf16[48,1024]{1,0:T(8,128)(2,1)S(1)}, bf16[48,1024]{1,0:T(8,128)(2,1)S(1)}, u32[]{:S(2)}, u32[]{:S(2)}) collective-permute-start(bf16[48,1024]{1,0:T(8,128)(2,1)S(1)} %add_convert_fusion.mine_ref), channel_id=1, source_target_pairs={{0,4},{4,0},{8,12},{12,8},{16,20},{20,16},{24,28},{28,24},{32,36},... | collective-permute-start | bytes 294920 | tf_op jit(solution)/shard_map/ppermute | solution.py:420

commit v5 on v4

--- a/solution.py
+++ b/solution.py
@@ -17,6 +17,7 @@
 WIDTH = HALVES * LANES
 PARAM_ROWS = 48
 RUN = 8
+SCAN_WIDTH = 2 * LANES
 f32 = jnp.float32
 bf16 = jnp.bfloat16
 
@@ -31,12 +32,12 @@
     return pl.ds(pl.multiple_of(h * LANES, LANES), LANES)
 
 
-def each_part(body):
+def each_part(body, parts=HALVES):
     def step(h, carry):
         body(h)
         return carry
 
-    lax.fori_loop(0, HALVES, step, 0)
+    lax.fori_loop(0, parts, step, 0)
 
 
 def tree(terms):
@@ -306,7 +307,7 @@
         sums_ref[0:POLES, at] = inside + packed * across
         sums_ref[40:48, at] = jnp.concatenate([lags[0], jnp.zeros((7, LANES), f32)], 0)
 
-    each_part(scan)
+    each_part(scan, SCAN_WIDTH // LANES)
     long_conv = y_ref[...]
     gated_ref[...] = (feat_ref[0].astype(f32) * long_conv).astype(bf16)
     grad_mixed = m_ref[...]
@@ -320,7 +321,7 @@
     for f in range(3):
         grads_ref[f] = grads[f]
         wide = grads[f][: 8 * TAPS - 8].astype(f32)
-        heads += [wide[8 * i : 8 * i + 1] for i in range(TAPS - 1)] + [jnp.zeros((2, WIDTH), f32)]
+        heads += [wide[8 * i : 8 * i + 1] for i in range(TAPS - 1)] + [jnp.zeros((2, SCAN_WIDTH), f32)]
         by_token = jnp.dot(hot_t_ref[...], grads[f], preferred_element_type=f32)
         sums_ref[16 + 8 * f : 24 + 8 * f, :] = jnp.concatenate(
             [
@@ -329,7 +330,7 @@
             ],
             0,
         )
-    heads.append(jnp.zeros((8, WIDTH), f32))
+    heads.append(jnp.zeros((8, SCAN_WIDTH), f32))
     first_ref[...] = jnp.concatenate(heads, 0).astype(bf16)
     params_ref[0] = sums_ref[...].astype(bf16)
 
@@ -520,29 +521,34 @@
     )
     other = turn(sent, 0, 0, 1)
 
+    span = channels // SCAN_WIDTH // 2
+
+    def slim(*shape):
+        return pl.BlockSpec(shape + (SCAN_WIDTH,), lambda b: (0,) * len(shape) + (b,))
+
     gated, grads, first, params = pl.pallas_call(
         main_kernel,
-        grid=grid,
+        grid=(2 * span,),
         in_specs=[
-            smem, lanes(3, length), lanes(length), lanes(2, POLES, SEGS),
-            lanes(2, steps // RUN, POLES, SEGS),
-            pl.BlockSpec((2 * POLES, WIDTH), lambda b: (0, b % (count // 2))),
-            pl.BlockSpec((2 * POLES, WIDTH), lambda b: (0, b % (count // 2))),
-            lanes(POLES), lanes(POLES), lanes(1), whole(64, length), lanes(8),
+            smem, slim(3, length), slim(length), slim(2, POLES, SEGS),
+            slim(2, steps // RUN, POLES, SEGS),
+            pl.BlockSpec((2 * POLES, SCAN_WIDTH), lambda b: (0, b % span)),
+            pl.BlockSpec((2 * POLES, SCAN_WIDTH), lambda b: (0, b % span)),
+            slim(POLES), slim(POLES), slim(1), whole(64, length), slim(8),
         ],
         out_specs=[
-            lanes(length), lanes(3, length), lanes(32),
+            slim(length), slim(3, length), slim(32),
             pl.BlockSpec(
-                (1, PARAM_ROWS, WIDTH), lambda b: (b // (count // 2), 0, b % (count // 2))
+                (1, PARAM_ROWS, SCAN_WIDTH), lambda b: (b // span, 0, b % span)
             ),
         ],
         out_shape=[
             struct((length, channels), bf16), struct((3, length, channels), bf16),
             struct((32, channels), bf16), struct((2, PARAM_ROWS, half), bf16),
         ],
-        scratch_shapes=[pltpu.VMEM((length, WIDTH), f32)] * 2
+        scratch_shapes=[pltpu.VMEM((length, SCAN_WIDTH), f32)] * 2
         + [pltpu.VMEM((steps, SEGS, LANES), f32)] * 2
-        + [pltpu.VMEM((2 * POLES, WIDTH), f32), pltpu.VMEM((PARAM_ROWS, WIDTH), f32)]
+        + [pltpu.VMEM((2 * POLES, SCAN_WIDTH), f32), pltpu.VMEM((PARAM_ROWS, SCAN_WIDTH), f32)]
         + [pltpu.VMEM((5, POLES, SEGS, LANES), f32), pltpu.VMEM((POLES, SEGS, LANES), f32)],
         compiler_params=roomy(60),
         name="main",

time: 96 us -> 95.5 us (level)
  no operation moved by 1% of the time
where the time goes in v5:
time: 95.5 us; the launch traced here: 93.9 us
  Pallas kernels  40.4 us (42%)
  starting transfers between devices  29.8 us (31%)
  waiting for transfers between devices  17.7 us (19%)
  local copies, waits for them, and re-layouts  4.06 us (4%)
  other arithmetic  1.04 us (1%)
    ppermute x16, starting transfers between devices, turn(): return lax.ppermute(block, 'seq', route)  17.6 us
    pallas_call x1, Pallas kernels, per_device(): pl.pallas_call(main_kernel, grid=(2 * span,), in_specs=[smem, slim(3, len...  15.2 us
    ppermute x16, waiting for transfers between devices, turn(): return lax.ppermute(block, 'seq', route)  11.8 us
    pallas_call x1, Pallas kernels, per_device(): pl.pallas_call(states_kernel, grid=grid, in_specs=[whole(length, 128), wh...  11.1 us
    pallas_call x2, Pallas kernels, outputs(): pl.pallas_call(output_kernel, grid=(half_grid,), in_specs=[spot(length),...  9.99 us
    ppermute x2, starting transfers between devices, shifted(): return lax.ppermute(block, 'seq', route)  6.55 us
    ppermute x2, waiting for transfers between devices, shifted(): return lax.ppermute(block, 'seq', route)  5.88 us
    ppermute x3, starting transfers between devices, per_device(): lax.ppermute(squares, 'ch', [(i, (i + k) % 4) for i in range(4)])  5.67 us
  transfers between devices with their start and end apart: 21, of which 9 were waited for; matrix products, arithmetic and copies ran while one was open for 1% of the time, Pallas kernels for 12%

profile of v5, /device:TPU:7, one launch (start us, length us, event | category | flops | bytes accessed | tf_op | source)
XLA Modules:
  0.0 93.9 jit_solution(14142090657745614626)
XLA Ops:
  0.6 1.6 %embed.1 = (f32[8,2048]{1,0:T(8,128)}, f32[8,128]{1,0:T(8,128)}) custom-call(bf16[512,2048]{1,0:T(8,128)(2,1)} %table_ref.1), custom_call_target="tpu_custom_call" | custom-call | tf_op jit(solution)/shard_map/embed/pallas_call | solution.py:448
  2.3 1.6 %collective-permute-start.1 = (f32[8,128]{1,0:T(8,128)}, f32[8,128]{1,0:T(8,128)S(1)}, u32[]{:S(2)}, u32[]{:S(2)}) collective-permute-start(f32[8,128]{1,0:T(8,128)} %get-tuple-element.52.sum0_ref), channel_id=1, source_target_pairs={{0,1},{1,2},{2,3},{3,0},{4,5},{5,6},{6,7},{7,4},{8,9},{9,10},{10,1... | collective-permute-start | bytes 12296 | tf_op jit(solution)/shard_map/ppermute | solution.py:463
  3.9 3.3 %collective-permute-start.2 = (f32[8,128]{1,0:T(8,128)}, f32[8,128]{1,0:T(8,128)S(1)}, u32[]{:S(2)}, u32[]{:S(2)}) collective-permute-start(f32[8,128]{1,0:T(8,128)} %get-tuple-element.52.sum0_ref), channel_id=1, source_target_pairs={{0,2},{1,3},{2,0},{3,1},{4,6},{5,7},{6,4},{7,5},{8,10},{9,11},{10,... | collective-permute-start | bytes 12296 | tf_op jit(solution)/shard_map/ppermute | solution.py:463
  7.2 0.7 collective-permute-start.3
  8.0 4.5 %collective-permute-start = (s32[1,256]{1,0:T(1,128)}, s32[1,256]{1,0:T(1,128)S(1)}, u32[]{:S(2)}, u32[]{:S(2)}) collective-permute-start(s32[1,256]{1,0:T(1,128)} %bitcast.10), channel_id=1, source_target_pairs={{0,4},{4,8},{8,12},{12,16},{16,20},{20,24},{24,28},{28,32},{32,36}... | collective-permute-start | bytes 3080 | tf_op jit(solution)/shard_map/ppermute | solution.py:427
  12.5 0.9 collective-permute-done.previous_ref
  13.4 0.6 copy-done.8
  14.0 1.6 %hot.1 = (bf16[256,128]{1,0:T(8,128)(2,1)}, bf16[64,256]{1,0:T(8,128)(2,1)}) custom-call(s32[1,256]{1,0:T(1,128)} %copy-done.8, s32[1,256]{1,0:T(1,128)} %bitcast.11), custom_call_target="tpu_custom_call" | custom-call | tf_op jit(solution)/shard_map/hot/pallas_call | solution.py:465
  15.6 0.6 copy-done.5
  16.2 11.1 %states.1 = (bf16[3,256,2048]{2,1,0:T(8,128)(2,1)}, bf16[256,2048]{1,0:T(8,128)(2,1)}, f32[8,2048]{1,0:T(8,128)}, f32[2,16,8,2048]{3,2,1,0:T(8,128)}, f32[2,4,16...) custom-call(bf16[256,128]{1,0:T(8,128)(2,1)} %get-tuple-element.50.hot_ref, bf16[256,256]{1,0:T(8,128)(2,1)} %constant.29.clone.order_ref, ...), custom_call_target="tpu_custom_call" | custom-call | tf_op jit(solution)/shard_map/states/pallas_call | solution.py:472
  27.3 1.2 %collective-permute-start.4 = (f32[2,32,1024]{2,1,0:T(8,128)}, f32[2,32,1024]{2,1,0:T(8,128)S(1)}, u32[]{:S(2)}, u32[]{:S(2)}) collective-permute-start(f32[2,32,1024]{2,1,0:T(8,128)} %get-tuple-element.57.refs_1_), channel_id=1, source_target_pairs={{0,4},{4,0},{8,12},{12,8},{16,20},{20,16},{24,28},{28,24},{32,36},... | collective-permute-start | bytes 786440 | tf_op jit(solution)/shard_map/ppermute | solution.py:421
  28.5 1.4 %collective-permute-done.4.refs_2_ = f32[2,32,1024]{2,1,0:T(8,128)S(1)} collective-permute-done((f32[2,32,1024]{2,1,0:T(8,128)}, f32[2,32,1024]{2,1,0:T(8,128)S(1)}, u32[]{:S(2)}, u32[]{:S(2)}) %collective-permute-start.4) | collective-permute-done | bytes 262176 | tf_op jit(solution)/shard_map/ppermute | solution.py:421
  29.9 0.9 %copy-done.1 = f32[2,32,1024]{2,1,0:T(8,128)S(1)} copy-done((f32[2,32,1024]{2,1,0:T(8,128)S(1)}, f32[2,32,1024]{2,1,0:T(8,128)}, u32[]{:S(2)}) %copy-start.1) | copy-done | bytes 262168
  30.9 1.4 %collective-permute-start.5 = (f32[16,1024]{1,0:T(8,128)S(1)}, f32[16,1024]{1,0:T(8,128)S(1)}, u32[]{:S(2)}, u32[]{:S(2)}) collective-permute-start(f32[16,1024]{1,0:T(8,128)S(1)} %get-tuple-element.60), channel_id=1, source_target_pairs={{0,32},{4,36},{8,40},{12,44},{16,48},{20,52},{24,56},{28,60},{32,6... | collective-permute-start | bytes 196616 | tf_op jit(solution)/shard_map/ppermute | solution.py:421
  32.3 2.6 %collective-permute-start.6 = (f32[16,1024]{1,0:T(8,128)S(1)}, f32[16,1024]{1,0:T(8,128)S(1)}, u32[]{:S(2)}, u32[]{:S(2)}) collective-permute-start(f32[16,1024]{1,0:T(8,128)S(1)} %get-tuple-element.61), channel_id=1, source_target_pairs={{0,64},{4,68},{8,72},{12,76},{16,80},{20,84},{24,88},{28,92},{32,9... | collective-permute-start | bytes 196616 | tf_op jit(solution)/shard_map/ppermute | solution.py:421
  34.9 1.1 %collective-permute-start.7 = (f32[16,1024]{1,0:T(8,128)S(1)}, f32[16,1024]{1,0:T(8,128)S(1)}, u32[]{:S(2)}, u32[]{:S(2)}) collective-permute-start(f32[16,1024]{1,0:T(8,128)S(1)} %get-tuple-element.62), channel_id=1, source_target_pairs={{0,96},{4,100},{8,104},{12,108},{16,112},{20,116},{24,120},{28,124... | collective-permute-start | bytes 196616 | tf_op jit(solution)/shard_map/ppermute | solution.py:421
  36.0 1.9 %collective-permute-done.6.refs_3_ = f32[16,1024]{1,0:T(8,128)S(1)} collective-permute-done((f32[16,1024]{1,0:T(8,128)S(1)}, f32[16,1024]{1,0:T(8,128)S(1)}, u32[]{:S(2)}, u32[]{:S(2)}) %collective-permute-start.6) | collective-permute-done | bytes 65568 | tf_op jit(solution)/shard_map/ppermute | solution.py:421
  37.8 0.5 collective-permute-done.7.refs_4_
  38.3 0.1 column.1
  38.4 0.6 collective-permute-start.10
  39.0 2.1 %collective-permute-start.8 = (f32[32,1024]{1,0:T(8,128)S(1)}, f32[32,1024]{1,0:T(8,128)S(1)}, u32[]{:S(2)}, u32[]{:S(2)}) collective-permute-start(f32[32,1024]{1,0:T(8,128)S(1)} %get-tuple-element.64), channel_id=1, source_target_pairs={{0,8},{4,12},{8,16},{12,20},{16,24},{20,28},{24,0},{28,4},{32,40},... | collective-permute-start | bytes 393224 | tf_op jit(solution)/shard_map/ppermute | solution.py:421
  41.1 0.8 collective-permute-start.9
  42.0 1.5 %collective-permute-done.10.refs_5_ = f32[32,1024]{1,0:T(8,128)S(1)} collective-permute-done((f32[32,1024]{1,0:T(8,128)S(1)}, f32[32,1024]{1,0:T(8,128)S(1)}, u32[]{:S(2)}, u32[]{:S(2)}) %collective-permute-start.10) | collective-permute-done | bytes 131104 | tf_op jit(solution)/shard_map/ppermute | solution.py:421
  43.5 4.3 %collective-permute-done.9.refs_4_ = f32[32,1024]{1,0:T(8,128)S(1)} collective-permute-done((f32[32,1024]{1,0:T(8,128)S(1)}, f32[32,1024]{1,0:T(8,128)S(1)}, u32[]{:S(2)}, u32[]{:S(2)}) %collective-permute-start.9) | collective-permute-done | bytes 131104 | tf_op jit(solution)/shard_map/ppermute | solution.py:421
  47.8 0.1 row.1
  47.9 0.6 copy-done.2
  48.5 2.2 %collective-permute-start.11 = (f32[32,1024]{1,0:T(8,128)S(1)}, f32[32,1024]{1,0:T(8,128)S(1)}, u32[]{:S(2)}, u32[]{:S(2)}) collective-permute-start(f32[32,1024]{1,0:T(8,128)S(1)} %get-tuple-element.68), channel_id=1, source_target_pairs={{0,4},{4,0},{8,12},{12,8},{16,20},{20,16},{24,28},{28,24},{32,36},... | collective-permute-start | bytes 393224 | tf_op jit(solution)/shard_map/ppermute | solution.py:421
  50.7 1.0 %collective-permute-done.11.other_ref = f32[32,1024]{1,0:T(8,128)S(1)} collective-permute-done((f32[32,1024]{1,0:T(8,128)S(1)}, f32[32,1024]{1,0:T(8,128)S(1)}, u32[]{:S(2)}, u32[]{:S(2)}) %collective-permute-start.11) | collective-permute-done | bytes 131104 | tf_op jit(solution)/shard_map/ppermute | solution.py:421
  51.7 0.7 copy-done.4
  52.3 15.2 %main.1 = (bf16[256,2048]{1,0:T(8,128)(2,1)}, bf16[3,256,2048]{2,1,0:T(8,128)(2,1)}, bf16[32,2048]{1,0:T(8,128)(2,1)}, bf16[2,48,1024]{2,1,0:T(8,128)(2,1)}) custom-call(s32[1]{0:T(128)} %bitcast.refs_0_.place_ref, bf16[3,256,2048]{2,1,0:T(8,128)(2,1)} %get-tuple-element.53.feat_ref, bf16[256,2048]{1,0:T(8,128)(2,1)} %get-tuple-element.54.cotp_ref, ...), custom_call_target="tpu_custom_call" | custom-call | tf_op jit(solution)/shard_map/main/pallas_call | solution.py:529
  67.5 0.4 collective-permute-start.12
  68.0 2.0 %collective-permute-start.16 = (bf16[32,2048]{1,0:T(8,128)(2,1)}, bf16[32,2048]{1,0:T(8,128)(2,1)S(1)}, u32[]{:S(2)}, u32[]{:S(2)}) collective-permute-start(bf16[32,2048]{1,0:T(8,128)(2,1)} %get-tuple-element.74), channel_id=1, source_target_pairs={{4,0},{8,4},{12,8},{16,12},{20,16},{24,20},{28,24},{32,28},{36,32}... | collective-permute-start | bytes 393224 | tf_op jit(solution)/shard_map/ppermute | solution.py:427
  70.0 0.9 fusion
  71.0 1.6 %collective-permute-start.13 = (bf16[48,1024]{1,0:T(8,128)(2,1)S(1)}, bf16[48,1024]{1,0:T(8,128)(2,1)S(1)}, u32[]{:S(2)}, u32[]{:S(2)}) collective-permute-start(bf16[48,1024]{1,0:T(8,128)(2,1)S(1)} %fusion), channel_id=1, source_target_pairs={{0,8},{4,12},{8,16},{12,20},{16,24},{20,28},{24,0},{28,4},{32,40},... | collective-permute-start | bytes 294920 | tf_op jit(solution)/shard_map/ppermute | solution.py:421
  72.6 0.4 collective-permute-start.14
  73.0 0.3 collective-permute-start.15
  73.3 5.0 %collective-permute-done.16.halo_ref = bf16[32,2048]{1,0:T(8,128)(2,1)S(1)} collective-permute-done((bf16[32,2048]{1,0:T(8,128)(2,1)}, bf16[32,2048]{1,0:T(8,128)(2,1)S(1)}, u32[]{:S(2)}, u32[]{:S(2)}) %collective-permute-start.16) | collective-permute-done | bytes 131104 | tf_op jit(solution)/shard_map/ppermute | solution.py:427
  78.2 0.7 copy-done.3
  78.9 5.0 %outputs.2 = (bf16[256,2048]{1,0:T(8,128)(2,1)}, bf16[256,2048]{1,0:T(8,128)(2,1)}) custom-call(bf16[256,2048]{1,0:T(8,128)(2,1)} %get-tuple-element.72.gated_ref, bf16[3,256,2048]{2,1,0:T(8,128)(2,1)} %get-tuple-element.73.grads_ref, bf16[32,2048]{1,0:T(8,128)(2,1)} %copy-done.3, f32[3,7,2048]{2,1,0:T(8,128)} %weight_ref.5, ...), custom_call_target="tpu_custom_call" | custom-call | tf_op jit(solution)/shard_map/outputs/pallas_call | solution.py:573
  83.9 0.1 add_convert_fusion.1
  84.0 0.1 collective-permute-start.17
  84.1 0.1 collective-permute-start.18
  84.1 2.6 %collective-permute-start.19 = (bf16[48,1024]{1,0:T(8,128)(2,1)S(1)}, bf16[48,1024]{1,0:T(8,128)(2,1)S(1)}, u32[]{:S(2)}, u32[]{:S(2)}) collective-permute-start(bf16[48,1024]{1,0:T(8,128)(2,1)S(1)} %add_convert_fusion.1), channel_id=1, source_target_pairs={{0,96},{4,100},{8,104},{12,108},{16,112},{20,116},{24,120},{28,124... | collective-permute-start | bytes 294920 | tf_op jit(solution)/shard_map/ppermute | solution.py:421
  86.7 5.0 %outputs.3 = (bf16[256,2048]{1,0:T(8,128)(2,1)}, bf16[256,2048]{1,0:T(8,128)(2,1)}) custom-call(bf16[256,2048]{1,0:T(8,128)(2,1)} %get-tuple-element.72.gated_ref, bf16[3,256,2048]{2,1,0:T(8,128)(2,1)} %get-tuple-element.73.grads_ref, bf16[32,2048]{1,0:T(8,128)(2,1)} %copy-done.3, ...), custom_call_target="tpu_custom_call", output_to_operand_aliasing={{0}: (5, {}), {1}: (6, {})} | custom-call | tf_op jit(solution)/shard_map/outputs/pallas_call | solution.py:573
  91.7 0.1 add_convert_fusion.mine_ref
  91.8 0.1 collective-permute-start.20
  91.9 1.3 %collective-permute-done.20.other_ref = bf16[48,1024]{1,0:T(8,128)(2,1)S(1)} collective-permute-done((bf16[48,1024]{1,0:T(8,128)(2,1)S(1)}, bf16[48,1024]{1,0:T(8,128)(2,1)S(1)}, u32[]{:S(2)}, u32[]{:S(2)}) %collective-permute-start.20) | collective-permute-done | bytes 98336 | tf_op jit(solution)/shard_map/ppermute | solution.py:421
  93.2 0.7 spread.1
  (25 shorter events, 0.1 us)
Async XLA Ops:
  0.6 29.3 %copy-start = (f32[16,2048]{1,0:T(8,128)S(1)}, f32[16,2048]{1,0:T(8,128)}, u32[]{:S(2)}) copy-start(f32[16,2048]{1,0:T(8,128)} %rate_ref.3) | copy-start | bytes 393220
  2.3 13.3 %collective-permute-start.1 = (f32[8,128]{1,0:T(8,128)}, f32[8,128]{1,0:T(8,128)S(1)}, u32[]{:S(2)}, u32[]{:S(2)}) collective-permute-start(f32[8,128]{1,0:T(8,128)} %get-tuple-element.52.sum0_ref), channel_id=1, source_target_pairs={{0,1},{1,2},{2,3},{3,0},{4,5},{5,6},{6,7},{7,4},{8,9},{9,10},{10,1... | collective-permute-start | bytes 12296 | tf_op jit(solution)/shard_map/ppermute | solution.py:463
  3.9 11.7 %collective-permute-start.2 = (f32[8,128]{1,0:T(8,128)}, f32[8,128]{1,0:T(8,128)S(1)}, u32[]{:S(2)}, u32[]{:S(2)}) collective-permute-start(f32[8,128]{1,0:T(8,128)} %get-tuple-element.52.sum0_ref), channel_id=1, source_target_pairs={{0,2},{1,3},{2,0},{3,1},{4,6},{5,7},{6,4},{7,5},{8,10},{9,11},{10,... | collective-permute-start | bytes 12296 | tf_op jit(solution)/shard_map/ppermute | solution.py:463
  7.2 8.4 %collective-permute-start.3 = (f32[8,128]{1,0:T(8,128)}, f32[8,128]{1,0:T(8,128)S(1)}, u32[]{:S(2)}, u32[]{:S(2)}) collective-permute-start(f32[8,128]{1,0:T(8,128)} %get-tuple-element.52.sum0_ref), channel_id=1, source_target_pairs={{0,3},{1,0},{2,1},{3,2},{4,7},{5,4},{6,5},{7,6},{8,11},{9,8},{10,9... | collective-permute-start | bytes 12296 | tf_op jit(solution)/shard_map/ppermute | solution.py:463
  8.0 5.4 %collective-permute-start = (s32[1,256]{1,0:T(1,128)}, s32[1,256]{1,0:T(1,128)S(1)}, u32[]{:S(2)}, u32[]{:S(2)}) collective-permute-start(s32[1,256]{1,0:T(1,128)} %bitcast.10), channel_id=1, source_target_pairs={{0,4},{4,8},{8,12},{12,16},{16,20},{20,24},{24,28},{28,32},{32,36}... | collective-permute-start | bytes 3080 | tf_op jit(solution)/shard_map/ppermute | solution.py:427
  13.4 0.6 copy-start.8
  15.6 0.6 copy-start.5
  15.6 0.6 copy-start.6
  15.6 0.6 copy-start.7
  27.3 2.6 %collective-permute-start.4 = (f32[2,32,1024]{2,1,0:T(8,128)}, f32[2,32,1024]{2,1,0:T(8,128)S(1)}, u32[]{:S(2)}, u32[]{:S(2)}) collective-permute-start(f32[2,32,1024]{2,1,0:T(8,128)} %get-tuple-element.57.refs_1_), channel_id=1, source_target_pairs={{0,4},{4,0},{8,12},{12,8},{16,20},{20,16},{24,28},{28,24},{32,36},... | collective-permute-start | bytes 786440 | tf_op jit(solution)/shard_map/ppermute | solution.py:421
  29.9 1.0 %copy-start.1 = (f32[2,32,1024]{2,1,0:T(8,128)S(1)}, f32[2,32,1024]{2,1,0:T(8,128)}, u32[]{:S(2)}) copy-start(f32[2,32,1024]{2,1,0:T(8,128)} %get-tuple-element.57.refs_1_) | copy-start | bytes 786436
  30.9 5.1 %collective-permute-start.5 = (f32[16,1024]{1,0:T(8,128)S(1)}, f32[16,1024]{1,0:T(8,128)S(1)}, u32[]{:S(2)}, u32[]{:S(2)}) collective-permute-start(f32[16,1024]{1,0:T(8,128)S(1)} %get-tuple-element.60), channel_id=1, source_target_pairs={{0,32},{4,36},{8,40},{12,44},{16,48},{20,52},{24,56},{28,60},{32,6... | collective-permute-start | bytes 196616 | tf_op jit(solution)/shard_map/ppermute | solution.py:421
  32.3 5.6 %collective-permute-start.6 = (f32[16,1024]{1,0:T(8,128)S(1)}, f32[16,1024]{1,0:T(8,128)S(1)}, u32[]{:S(2)}, u32[]{:S(2)}) collective-permute-start(f32[16,1024]{1,0:T(8,128)S(1)} %get-tuple-element.61), channel_id=1, source_target_pairs={{0,64},{4,68},{8,72},{12,76},{16,80},{20,84},{24,88},{28,92},{32,9... | collective-permute-start | bytes 196616 | tf_op jit(solution)/shard_map/ppermute | solution.py:421
  34.9 3.4 %collective-permute-start.7 = (f32[16,1024]{1,0:T(8,128)S(1)}, f32[16,1024]{1,0:T(8,128)S(1)}, u32[]{:S(2)}, u32[]{:S(2)}) collective-permute-start(f32[16,1024]{1,0:T(8,128)S(1)} %get-tuple-element.62), channel_id=1, source_target_pairs={{0,96},{4,100},{8,104},{12,108},{16,112},{20,116},{24,120},{28,124... | collective-permute-start | bytes 196616 | tf_op jit(solution)/shard_map/ppermute | solution.py:421
  38.4 5.1 %collective-permute-start.10 = (f32[32,1024]{1,0:T(8,128)S(1)}, f32[32,1024]{1,0:T(8,128)S(1)}, u32[]{:S(2)}, u32[]{:S(2)}) collective-permute-start(f32[32,1024]{1,0:T(8,128)S(1)} %get-tuple-element.66), channel_id=1, source_target_pairs={{0,24},{4,28},{8,0},{12,4},{16,8},{20,12},{24,16},{28,20},{32,56},... | collective-permute-start | bytes 393224 | tf_op jit(solution)/shard_map/ppermute | solution.py:421
  39.0 4.5 %collective-permute-start.8 = (f32[32,1024]{1,0:T(8,128)S(1)}, f32[32,1024]{1,0:T(8,128)S(1)}, u32[]{:S(2)}, u32[]{:S(2)}) collective-permute-start(f32[32,1024]{1,0:T(8,128)S(1)} %get-tuple-element.64), channel_id=1, source_target_pairs={{0,8},{4,12},{8,16},{12,20},{16,24},{20,28},{24,0},{28,4},{32,40},... | collective-permute-start | bytes 393224 | tf_op jit(solution)/shard_map/ppermute | solution.py:421
  41.1 6.6 %collective-permute-start.9 = (f32[32,1024]{1,0:T(8,128)S(1)}, f32[32,1024]{1,0:T(8,128)S(1)}, u32[]{:S(2)}, u32[]{:S(2)}) collective-permute-start(f32[32,1024]{1,0:T(8,128)S(1)} %get-tuple-element.65), channel_id=1, source_target_pairs={{0,16},{4,20},{8,24},{12,28},{16,0},{20,4},{24,8},{28,12},{32,48},... | collective-permute-start | bytes 393224 | tf_op jit(solution)/shard_map/ppermute | solution.py:421
  47.9 0.7 copy-start.2
  48.5 3.2 %collective-permute-start.11 = (f32[32,1024]{1,0:T(8,128)S(1)}, f32[32,1024]{1,0:T(8,128)S(1)}, u32[]{:S(2)}, u32[]{:S(2)}) collective-permute-start(f32[32,1024]{1,0:T(8,128)S(1)} %get-tuple-element.68), channel_id=1, source_target_pairs={{0,4},{4,0},{8,12},{12,8},{16,20},{20,16},{24,28},{28,24},{32,36},... | collective-permute-start | bytes 393224 | tf_op jit(solution)/shard_map/ppermute | solution.py:421
  51.7 0.7 copy-start.4
  67.5 2.5 %collective-permute-start.12 = (bf16[2,48,1024]{2,1,0:T(8,128)(2,1)}, bf16[2,48,1024]{2,1,0:T(8,128)(2,1)S(1)}, u32[]{:S(2)}, u32[]{:S(2)}) collective-permute-start(bf16[2,48,1024]{2,1,0:T(8,128)(2,1)} %get-tuple-element.71), channel_id=1, source_target_pairs={{0,4},{4,0},{8,12},{12,8},{16,20},{20,16},{24,28},{28,24},{32,36},... | collective-permute-start | bytes 589832 | tf_op jit(solution)/shard_map/ppermute | solution.py:421
  68.0 10.3 %collective-permute-start.16 = (bf16[32,2048]{1,0:T(8,128)(2,1)}, bf16[32,2048]{1,0:T(8,128)(2,1)S(1)}, u32[]{:S(2)}, u32[]{:S(2)}) collective-permute-start(bf16[32,2048]{1,0:T(8,128)(2,1)} %get-tuple-element.74), channel_id=1, source_target_pairs={{4,0},{8,4},{12,8},{16,12},{20,16},{24,20},{28,24},{32,28},{36,32}... | collective-permute-start | bytes 393224 | tf_op jit(solution)/shard_map/ppermute | solution.py:427
  71.0 12.9 %collective-permute-start.13 = (bf16[48,1024]{1,0:T(8,128)(2,1)S(1)}, bf16[48,1024]{1,0:T(8,128)(2,1)S(1)}, u32[]{:S(2)}, u32[]{:S(2)}) collective-permute-start(bf16[48,1024]{1,0:T(8,128)(2,1)S(1)} %fusion), channel_id=1, source_target_pairs={{0,8},{4,12},{8,16},{12,20},{16,24},{20,28},{24,0},{28,4},{32,40},... | collective-permute-start | bytes 294920 | tf_op jit(solution)/shard_map/ppermute | solution.py:421
  72.6 11.3 %collective-permute-start.14 = (bf16[48,1024]{1,0:T(8,128)(2,1)S(1)}, bf16[48,1024]{1,0:T(8,128)(2,1)S(1)}, u32[]{:S(2)}, u32[]{:S(2)}) collective-permute-start(bf16[48,1024]{1,0:T(8,128)(2,1)S(1)} %fusion), channel_id=1, source_target_pairs={{0,16},{4,20},{8,24},{12,28},{16,0},{20,4},{24,8},{28,12},{32,48},... | collective-permute-start | bytes 294920 | tf_op jit(solution)/shard_map/ppermute | solution.py:421
  73.0 10.9 %collective-permute-start.15 = (bf16[48,1024]{1,0:T(8,128)(2,1)S(1)}, bf16[48,1024]{1,0:T(8,128)(2,1)S(1)}, u32[]{:S(2)}, u32[]{:S(2)}) collective-permute-start(bf16[48,1024]{1,0:T(8,128)(2,1)S(1)} %fusion), channel_id=1, source_target_pairs={{0,24},{4,28},{8,0},{12,4},{16,8},{20,12},{24,16},{28,20},{32,56},... | collective-permute-start | bytes 294920 | tf_op jit(solution)/shard_map/ppermute | solution.py:421
  78.2 0.7 copy-start.3
  84.0 7.7 %collective-permute-start.17 = (bf16[48,1024]{1,0:T(8,128)(2,1)S(1)}, bf16[48,1024]{1,0:T(8,128)(2,1)S(1)}, u32[]{:S(2)}, u32[]{:S(2)}) collective-permute-start(bf16[48,1024]{1,0:T(8,128)(2,1)S(1)} %add_convert_fusion.1), channel_id=1, source_target_pairs={{0,32},{4,36},{8,40},{12,44},{16,48},{20,52},{24,56},{28,60},{32,6... | collective-permute-start | bytes 294920 | tf_op jit(solution)/shard_map/ppermute | solution.py:421
  84.1 7.7 %collective-permute-start.18 = (bf16[48,1024]{1,0:T(8,128)(2,1)S(1)}, bf16[48,1024]{1,0:T(8,128)(2,1)S(1)}, u32[]{:S(2)}, u32[]{:S(2)}) collective-permute-start(bf16[48,1024]{1,0:T(8,128)(2,1)S(1)} %add_convert_fusion.1), channel_id=1, source_target_pairs={{0,64},{4,68},{8,72},{12,76},{16,80},{20,84},{24,88},{28,92},{32,9... | collective-permute-start | bytes 294920 | tf_op jit(solution)/shard_map/ppermute | solution.py:421
  84.1 7.6 %collective-permute-start.19 = (bf16[48,1024]{1,0:T(8,128)(2,1)S(1)}, bf16[48,1024]{1,0:T(8,128)(2,1)S(1)}, u32[]{:S(2)}, u32[]{:S(2)}) collective-permute-start(bf16[48,1024]{1,0:T(8,128)(2,1)S(1)} %add_convert_fusion.1), channel_id=1, source_target_pairs={{0,96},{4,100},{8,104},{12,108},{16,112},{20,116},{24,120},{28,124... | collective-permute-start | bytes 294920 | tf_op jit(solution)/shard_map/ppermute | solution.py:421
  91.8 1.4 %collective-permute-start.20 = (bf16[48,1024]{1,0:T(8,128)(2,1)S(1)}, bf16[48,1024]{1,0:T(8,128)(2,1)S(1)}, u32[]{:S(2)}, u32[]{:S(2)}) collective-permute-start(bf16[48,1024]{1,0:T(8,128)(2,1)S(1)} %add_convert_fusion.mine_ref), channel_id=1, source_target_pairs={{0,4},{4,0},{8,12},{12,8},{16,20},{20,16},{24,28},{28,24},{32,36},... | collective-permute-start | bytes 294920 | tf_op jit(solution)/shard_map/ppermute | solution.py:421
